TPU v7x, 128 devices: a whole 4x4x4 slice. The times are simulated.
128 devices in a mesh: seq: 32 (over x, y, core), head: 4 (over z).
Axes of the slice: x: 4, y: 4, z: 4, core: 2. Of those that a mesh axis runs over, the one named last changes fastest.
Arguments:
- queries: bfloat16 [32768, 4096], P('seq', 'head'), may hold values from -90 to 90
- keys: bfloat16 [32768, 4096], P('seq', 'head'), may hold values from -50 to 50
- values: bfloat16 [32768, 4096], P('seq', 'head'), may hold values from -6 to 6
- cluster_ids: int32 [32768, 32], P('seq', 'head'), may hold values from 0 to 255, as said below
- out_weight: bfloat16 [4096, 4096], P('head', 'seq'), may hold values from -2.390625 to 2.390625
Outputs:
- mixed: bfloat16 [32768, 4096], P('seq', 'head')
Inputs may be any that keep to these rules, and one draw needn't show every extreme that they name: `cluster_ids`: in every head each of the 256 clusters holds at least one token.
All inputs are finite; a program needn't handle non-finite values.
Results may differ from a plain program's by a relative error of at most 0.01.
Values may be sent and summed in bfloat16 or wider, within the bound.
No kernel may reach another device: no remote copies, remote signals or barrier semaphores. Data moves between devices by JAX's collectives and lax.ppermute only.
A program may use at most 128 MiB of HBM per device.

v0:
```python
import jax
import jax.numpy as jnp
from jax import lax
from jax.sharding import Mesh
from jax.sharding import PartitionSpec as P

HDIM = 128
CLUSTERS = 256
SEQ = ("seq_0", "seq_1", "seq_2")


def split_up(value, dim, size):
    shape = value.shape
    tiles = value.reshape(*shape[:dim], size, shape[dim] // size, *shape[dim + 1 :])
    return jnp.moveaxis(tiles, dim, 0)


def summed_on_arrival(value, axis, dim):
    tiles = split_up(value, dim, lax.axis_size(axis))
    arrived = lax.all_to_all(tiles, axis, split_axis=0, concat_axis=0, tiled=True)
    return arrived.sum(axis=0)


def sum_in_two_steps(value, axes, dim):
    far, near = axes
    own = summed_on_arrival(split_up(value, dim, lax.axis_size(far)), near, dim + 1)
    return jnp.sum(lax.all_to_all(own, far, 0, 0, tiled=True), axis=0)


def rows_for(lines, size):
    spare = -len(lines) % size
    return jnp.pad(lines, [(0, spare)] + [(0, 0)] * (lines.ndim - 1))


def sent_to_all(value, axis):
    copies = jnp.broadcast_to(value, (lax.axis_size(axis), *value.shape))
    return lax.all_to_all(copies, axis, split_axis=0, concat_axis=0, tiled=True)


def laid_out(tiles, dim):
    tiles = jnp.moveaxis(tiles, 0, dim)
    shape = tiles.shape
    return tiles.reshape(*shape[:dim], shape[dim] * shape[dim + 1], *shape[dim + 2 :])


def gather_axes(value, axes, dim):
    far, near = axes
    tiles = sent_to_all(sent_to_all(value, far), near)
    return laid_out(tiles.swapaxes(0, 1).reshape(-1, *value.shape), dim)


def sum_by_parts(value, axes):
    own = sum_in_two_steps(
        rows_for(value, lax.axis_size(axes[0]) * lax.axis_size(axes[1])), axes, 0
    )
    whole = gather_axes(own, axes, 0)
    return whole[: len(value)].reshape(value.shape)


def packed_total(arrays, axis):
    ends = [0]
    for a in arrays:
        ends.append(ends[-1] + a.size)
    so_far = sum_by_parts(jnp.concatenate([a.ravel() for a in arrays]), axis)
    return tuple((so_far[b:e].reshape(a.shape) for a, b, e in zip(arrays, ends, ends[1:])))


def of_everyone(value, axis):
    return sent_to_all(value, axis).max(axis=0)


def local(queries, keys, values, cluster_ids, out_weight):
    token_rows = queries.shape[0]
    head_count = queries.shape[1] // HDIM
    query_three = queries.reshape(token_rows, head_count, HDIM)
    key_three = keys.reshape(token_rows, head_count, HDIM)
    value_three = values.reshape(token_rows, head_count, HDIM)
    labels = jnp.arange(CLUSTERS, dtype=jnp.int32)
    member = (cluster_ids[:, :, None] == labels[None, None, :]).astype(jnp.bfloat16)
    totals = jnp.einsum("thc,thd->hcd", member, query_three, preferred_element_type=jnp.float32)
    counts = jnp.sum(member, axis=0, dtype=jnp.float32)
    all_totals, all_counts = packed_total((totals, counts), (("seq_0", "seq_1"), "seq_2"))
    centre = (all_totals / all_counts[:, :, None]).astype(jnp.bfloat16)
    scores = jnp.einsum("hcd,thd->hct", centre, key_three, preferred_element_type=jnp.float32)
    scores = scores * (1.0 / HDIM**0.5)
    block_peak = jnp.max(scores, axis=2)
    weights = jnp.exp(scores - block_peak[:, :, None]).astype(jnp.bfloat16)
    block_mass = jnp.sum(weights, axis=2, dtype=jnp.float32)
    block_output = jnp.einsum(
        "hct,thd->hcd", weights, value_three, preferred_element_type=jnp.float32
    )
    global_peak = of_everyone(block_peak, SEQ)
    factor = jnp.exp(block_peak - global_peak)
    mass_sum, output_sum = packed_total(
        (block_mass * factor, block_output * factor[:, :, None]), (("seq_0", "seq_1"), "seq_2")
    )
    centroid_out = (output_sum / mass_sum[:, :, None]).astype(jnp.bfloat16)
    attended = jnp.einsum("thc,hcd->thd", member, centroid_out, preferred_element_type=jnp.float32)
    attended = attended.astype(jnp.bfloat16).reshape(token_rows, head_count * HDIM)
    head_part = jnp.dot(
        attended,
        lax.all_gather(out_weight, SEQ, axis=1, tiled=True),
        preferred_element_type=jnp.float32,
    )
    mixed_out = lax.psum_scatter(
        head_part.astype(jnp.bfloat16), "head", scatter_dimension=1, tiled=True
    )
    return mixed_out


def solution(mesh):
    finer = Mesh(
        mesh.devices.reshape(4, 4, 2, mesh.shape["head"]), ("seq_0", "seq_1", "seq_2", "head")
    )
    in_specs = (P(SEQ, "head"), P(SEQ, "head"), P(SEQ, "head"), P(SEQ, "head"), P("head", SEQ))
    out_specs = P(SEQ, "head")
    return jax.shard_map(local, mesh=finer, in_specs=in_specs, out_specs=out_specs, check_vma=False)
```

profile of v0, /device:TPU:1, one launch (start us, length us, event | category | flops | bytes accessed | tf_op | source)
XLA Modules:
  0.0 254.9 jit_solution(5969950927807449599)
XLA Ops:
  6.5 0.0 copy-start
  6.5 0.0 all-gather.2.cloned.1.call-start
  6.5 0.7 all-gather.2.cloned.1.call-update
  7.3 3.6 %convert_reduce_fusion.1 = f32[8,256]{1,0:T(8,128)S(1)} fusion(s32[1024,8]{0,1:T(8,128)} %param.8), kind=kLoop, calls=%fused_computation.2 | loop fusion | flops 8386560 | bytes 40960 | tf_op jit(solution)/shard_map/reduce_sum | solution.py:81
  10.9 5.4 %fusion.2 = f32[8,256,128]{2,1,0:T(8,128)S(1)} fusion(s32[1024,8]{0,1:T(8,128)} %param.8, bf16[1024,1024]{1,0:T(8,128)(2,1)} %param.5), kind=kOutput, calls=%fused_computation.6 | convolution fusion | flops 538968064 | bytes 3178496 | tf_op jit(solution)/shard_map/thc,thd->hcd/dot_general | solution.py:80
  16.3 1.0 pad_maximum_fusion
  17.3 2.0 reshape_reshape.12
  19.3 0.1 copy.33
  19.4 5.6 %all_to_all.61 = f32[2,16,8256]{2,1,0:T(8,128)S(1)} all-to-all(f32[2,16,8256]{2,1,0:T(8,128)S(1)} %copy.33), channel_id=1, replica_groups=mesh['seq_0'=4,'seq_1'=4,'seq_2'=2,'head'=4] {'seq_2'}, dimensions={0} | all-to-all | bytes 2113536 | tf_op jit(solution)/shard_map/all_to_all | solution.py:20
  25.0 0.9 reduce_sum.55
  25.9 1.4 all_to_all.40
  27.3 17.9 %all_to_all.62 = f32[16,1,8256]{2,1,0:T(1,128)S(1)} all-to-all(f32[16,1,8256]{2,1,0:T(1,128)S(1)} %all_to_all.40), channel_id=1, replica_groups=mesh['seq_0'=4,'seq_1'=4,'seq_2'=2,'head'=4] {'seq_0','seq_1'}, dimensions={0} | all-to-all | bytes 1056768 | tf_op jit(solution)/shard_map/all_to_all | solution.py:27
  45.2 0.3 reduce_sum.56
  45.6 0.3 broadcast_in_dim.19
  45.9 16.0 %all_to_all.63 = f32[16,1,8256]{2,1,0:T(1,128)S(1)} all-to-all(f32[16,1,8256]{2,1,0:T(1,128)S(1)} %broadcast_in_dim.19), channel_id=1, replica_groups=mesh['seq_0'=4,'seq_1'=4,'seq_2'=2,'head'=4] {'seq_0','seq_1'}, dimensions={0} | all-to-all | bytes 1056768 | tf_op jit(solution)/shard_map/all_to_all | solution.py:37
  61.9 0.1 broadcast_in_dim.20
  62.0 8.6 %all_to_all.64 = f32[2,16,8256]{2,1,0:T(8,128)S(1)} all-to-all(f32[2,16,8256]{2,1,0:T(8,128)S(1)} %broadcast_in_dim.20), channel_id=1, replica_groups=mesh['seq_0'=4,'seq_1'=4,'seq_2'=2,'head'=4] {'seq_2'}, dimensions={0} | all-to-all | bytes 2113536 | tf_op jit(solution)/shard_map/all_to_all | solution.py:37
  70.6 0.5 copy.34
  71.2 2.0 slice.19
  73.1 1.7 reshape_reshape.13
  74.9 0.0 slice-start
  74.9 0.8 slice_bitcast_fusion.1
  75.7 0.0 copy-done
  75.7 0.4 slice-done
  76.1 4.0 %multiply_reduce_fusion = (f32[8,256]{1,0:T(8,128)S(1)}, f32[8,256,1024]{2,1,0:T(8,128)}) fusion(f32[8,256,128]{2,1,0:T(8,128)S(1)} %bitcast.57, f32[8,256]{1,0:T(8,128)S(1)} %slice_bitcast_fusion.1, bf16[1024,1024]{1,0:T(8,128)(2,1)S(1)} %copy-done), kind=kOutput, calls=%fused_computation.7 | convolution fusion | flops 541587456 | bytes 11550720 | tf_op jit(solution)/shard_map/hcd,thd->hct/dot_general | solution.py:84
  80.1 0.7 broadcast_in_dim.21
  80.8 4.1 %all-to-all-start.4 = ((f32[32,8,256]{2,1,0:T(8,128)}), f32[32,8,256]{2,1,0:T(8,128)S(1)}, u32[]{:S(2)}, u32[]{:S(2)}) async-start(f32[32,8,256]{2,1,0:T(8,128)} %broadcast_in_dim.21), calls=%async_computation.4 | async-start | bytes 524288 | tf_op jit(solution)/shard_map/all_to_all | solution.py:37
  84.9 0.0 reduce-scatter.2.cloned.1.call-start
  85.0 4.4 %convert_reduce_fusion = f32[8,256]{1,0:T(8,128)S(1)} fusion(f32[8,256]{1,0:T(8,128)S(1)} %get-tuple-element.7, f32[8,256,1024]{2,1,0:T(8,128)} %get-tuple-element.8), kind=kLoop, calls=%fused_computation | loop fusion | flops 10483712 | bytes 8404992 | tf_op jit(solution)/shard_map/reduce_sum | solution.py:88
  89.3 4.7 %all-to-all-done.4 = f32[32,8,256]{2,1,0:T(8,128)S(1)} async-done(((f32[32,8,256]{2,1,0:T(8,128)}), f32[32,8,256]{2,1,0:T(8,128)S(1)}, u32[]{:S(2)}, u32[]{:S(2)}) %all-to-all-start.4) | async-done | bytes 262176 | tf_op jit(solution)/shard_map/all_to_all | solution.py:37
  94.1 5.3 %fusion.14 = f32[8,256,128]{2,1,0:T(8,128)S(1)} fusion(f32[8,256,1024]{2,1,0:T(8,128)} %get-tuple-element.8, f32[8,256]{1,0:T(8,128)S(1)} %get-tuple-element.7, f32[8,256]{1,0:T(8,128)S(1)} %get-tuple-element.6, bf16[1024,1024]{1,0:T(8,128)(2,1)} %param.7), kind=kOutput, calls=%fused_computation.20 | convolution fusion | flops 543424512 | bytes 11550720 | tf_op jit(solution)/shard_map/hct,thd->hcd/dot_general | solution.py:89
  99.4 1.0 pad_maximum_fusion.1
  100.4 2.0 reshape_reshape.14
  102.4 0.1 copy.38
  102.5 4.4 %all_to_all.65 = f32[2,16,8256]{2,1,0:T(8,128)S(1)} all-to-all(f32[2,16,8256]{2,1,0:T(8,128)S(1)} %copy.38), channel_id=1, replica_groups=mesh['seq_0'=4,'seq_1'=4,'seq_2'=2,'head'=4] {'seq_2'}, dimensions={0} | all-to-all | bytes 2113536 | tf_op jit(solution)/shard_map/all_to_all | solution.py:20
  106.9 0.9 reduce_sum.58
  107.8 1.4 all_to_all.47
  109.2 14.2 %all_to_all.66 = f32[16,1,8256]{2,1,0:T(1,128)S(1)} all-to-all(f32[16,1,8256]{2,1,0:T(1,128)S(1)} %all_to_all.47), channel_id=1, replica_groups=mesh['seq_0'=4,'seq_1'=4,'seq_2'=2,'head'=4] {'seq_0','seq_1'}, dimensions={0} | all-to-all | bytes 1056768 | tf_op jit(solution)/shard_map/all_to_all | solution.py:27
  123.4 0.3 reduce_sum.59
  123.7 0.3 broadcast_in_dim.22
  124.0 12.7 %all_to_all.67 = f32[16,1,8256]{2,1,0:T(1,128)S(1)} all-to-all(f32[16,1,8256]{2,1,0:T(1,128)S(1)} %broadcast_in_dim.22), channel_id=1, replica_groups=mesh['seq_0'=4,'seq_1'=4,'seq_2'=2,'head'=4] {'seq_0','seq_1'}, dimensions={0} | all-to-all | bytes 1056768 | tf_op jit(solution)/shard_map/all_to_all | solution.py:37
  136.7 0.1 broadcast_in_dim.23
  136.8 7.0 %all_to_all.68 = f32[2,16,8256]{2,1,0:T(8,128)S(1)} all-to-all(f32[2,16,8256]{2,1,0:T(8,128)S(1)} %broadcast_in_dim.23), channel_id=1, replica_groups=mesh['seq_0'=4,'seq_1'=4,'seq_2'=2,'head'=4] {'seq_2'}, dimensions={0} | all-to-all | bytes 2113536 | tf_op jit(solution)/shard_map/all_to_all | solution.py:37
  143.8 0.5 copy.39
  144.4 2.0 slice.22
  146.4 0.0 copy-start.1
  146.4 1.7 reshape_reshape.15
  148.1 0.0 slice-start.1
  148.1 0.8 slice_bitcast_fusion
  148.9 0.0 copy-done.1
  148.9 0.4 slice-done.1
  149.3 4.1 %fusion.13 = bf16[8,128,1024]{2,1,0:T(8,128)(2,1)} fusion(s32[1024,8]{0,1:T(8,128)S(1)} %copy-done.1, f32[8,256,128]{2,1,0:T(8,128)S(1)} %bitcast.58, f32[8,256]{1,0:T(8,128)S(1)} %slice_bitcast_fusion), kind=kOutput, calls=%fused_computation.19 | convolution fusion | flops 540540928 | bytes 3186688 | tf_op jit(solution)/shard_map/thc,hcd->thd/dot_general | solution.py:98
  153.5 0.0 all-gather.2.cloned.1.call-done
  153.5 14.8 %convolution_convert_fusion = bf16[1024,4096]{1,0:T(8,128)(2,1)} fusion(bf16[1024,1024]{0,1:T(8,128)(2,1)} %bitcast.66, bf16[1024,4096]{1,0:T(8,128)(2,1)} %all-gather.2.cloned.1.call-done), kind=kOutput, calls=%fused_computation.8 | convolution fusion | flops 8594128896 | bytes 18874368 | tf_op jit(solution)/shard_map/dot_general | solution.py:100
  168.3 0.0 reduce-scatter.2.cloned.1.call-update
  168.3 79.7 %reduce-scatter.2.cloned.1.call-done = bf16[1024,1024]{1,0:T(8,128)(2,1)} async-done(((bf16[1024,4096]{1,0:T(8,128)(2,1)}), bf16[1024,1024]{1,0:T(8,128)(2,1)}) %reduce-scatter.2.cloned.1.call-update) | async-done | bytes 2097168 | tf_op jit(solution)/shard_map/reduce_scatter | solution.py:105
  (6 shorter events, 0.1 us)
Async XLA Ops:
  6.5 69.1 %copy-start = (bf16[1024,1024]{1,0:T(8,128)(2,1)S(1)}, bf16[1024,1024]{1,0:T(8,128)(2,1)}, u32[]{:S(2)}) copy-start(bf16[1024,1024]{1,0:T(8,128)(2,1)} %param.6) | copy-start | bytes 6291460
  6.5 146.9 %all-gather.2.cloned.1.call-start = ((), (), s32[]{:S(2)}) async-start(), calls=%async_computation.10 | async-start | bytes 8650752 | tf_op jit(solution)/shard_map/all_gather | solution.py:102
  74.9 1.2 slice-start
  80.8 13.2 %all-to-all-start.4 = ((f32[32,8,256]{2,1,0:T(8,128)}), f32[32,8,256]{2,1,0:T(8,128)S(1)}, u32[]{:S(2)}, u32[]{:S(2)}) async-start(f32[32,8,256]{2,1,0:T(8,128)} %broadcast_in_dim.21), calls=%async_computation.4 | async-start | bytes 524288 | tf_op jit(solution)/shard_map/all_to_all | solution.py:37
  84.9 163.1 %reduce-scatter.2.cloned.1.call-start = ((), (), s32[]{:S(2)}) async-start(), calls=%async_computation.11 | async-start | bytes 10485760 | tf_op jit(solution)/shard_map/reduce_scatter | solution.py:105
  146.4 2.5 copy-start.1
  148.1 1.2 slice-start.1
Sparse Core Ops, SparseCore 0:
  9.5 67.2 all-gather.1
  168.5 79.5 reduce-scatter.1
where the time goes:
time: 256 us; the launch traced here: 255 us
  blocking collectives  86.4 us (34%)
  waiting for transfers between devices  85.1 us (33%)
  matrix products  33.6 us (13%)
  local copies, waits for them, and re-layouts  19.4 us (8%)
  between operations  13.6 us (5%)
  other arithmetic  12.6 us (5%)
  starting transfers between devices  4.11 us (2%)
    reduce_scatter x1, waiting for transfers between devices, local(): lax.psum_scatter(head_part.astype(jnp.bfloat16), 'head', scatter_dimensio...  79.7 us
    all_to_all x4, blocking collectives, sent_to_all(): return lax.all_to_all(copies, axis, split_axis=0, concat_axis=0, tiled=True)  44.3 us
    all_to_all x2, blocking collectives, sum_in_two_steps(): return jnp.sum(lax.all_to_all(own, far, 0, 0, tiled=True), axis=0)  32.1 us
    dot_general x1, matrix products, local(): jnp.dot(attended, lax.all_gather(out_weight, SEQ, axis=1, tiled=True), pr...  14.8 us
    all_to_all x2, blocking collectives, summed_on_arrival(): lax.all_to_all(tiles, axis, split_axis=0, concat_axis=0, tiled=True)  9.99 us
    dot_general x1, matrix products, local(): jnp.einsum('thc,thd->hcd', member, query_three, preferred_element_type=jn...  5.37 us
    dot_general x1, matrix products, local(): jnp.einsum('hct,thd->hcd', weights, value_three, preferred_element_type=j...  5.3 us
  transfers between devices with their start and end apart: 3, of which 2 were waited for; matrix products, arithmetic and copies ran while one was open for 18% of the time, Pallas kernels for 0%

commit v1 on v0

v1 whole, which is shorter than its diff:
```python
import functools
import math

import jax
import jax.numpy as jnp
from jax import lax
from jax.experimental import pallas as pl
from jax.experimental.pallas import tpu as pltpu
from jax.sharding import Mesh
from jax.sharding import PartitionSpec as P

HDIM = 128
CLUSTERS = 256
HALF = 4
QUARTER = CLUSTERS // 4
SEQ = ("x", "y", "c")
PLANE = ("x", "y")
CUBE = ("z", "x", "y")
EXTRA = 8
TAIL = 16
LOG2_SCALE = math.log2(math.e) / math.sqrt(HDIM)
F32 = jnp.float32
BF16 = jnp.bfloat16
NT = (((1,), (1,)), ((), ()))


def params(mib):
    return pltpu.CompilerParams(vmem_limit_bytes=mib * 2**20)


def eye(rows, cols):
    r = lax.broadcasted_iota(jnp.int32, (rows, cols), 0)
    c = lax.broadcasted_iota(jnp.int32, (rows, cols), 1)
    return r == c


def totals_of_head(row, query):
    labels = lax.broadcasted_iota(jnp.int32, (CLUSTERS, row.shape[1]), 0)
    member = (labels == row).astype(F32).astype(BF16)
    total = jnp.dot(member, query, preferred_element_type=F32)
    ones = jnp.ones((EXTRA, row.shape[1]), BF16)
    count = lax.dot_general(ones, member, NT, preferred_element_type=F32)
    return total, count


def owners(total, count):
    spare = jnp.zeros((EXTRA, HDIM - QUARTER), F32)
    for k in range(4):
        lines = slice(k * QUARTER, (k + 1) * QUARTER)
        yield k, total[lines], jnp.concatenate([count[:, lines], spare], axis=1)


def theirs_kernel(side_ref, ids_ref, q_ref, out_ref):
    row = ids_ref[pl.ds(side_ref[0] * HALF + pl.program_id(0), 1), :]
    for k, upper, lower in owners(*totals_of_head(row, q_ref[...])):
        out_ref[k, :QUARTER, :] = upper
        out_ref[k, QUARTER:, :] = lower


def mine_kernel(side_ref, ids_ref, q_ref, in_ref, w_ref, *rest):
    del w_ref
    out_ref = rest[-2]
    row = ids_ref[pl.ds(side_ref[0] * HALF + pl.program_id(0), 1), :]
    for k, upper, lower in owners(*totals_of_head(row, q_ref[...])):
        out_ref[k, :QUARTER, :] = upper + in_ref[k, :QUARTER, :]
        out_ref[k, QUARTER:, :] = lower + in_ref[k, QUARTER:, :]


BY_OWNER = jax.ShapeDtypeStruct((4 * HALF, QUARTER + EXTRA, HDIM), F32)
OWNER_BLOCK = pl.BlockSpec((4, QUARTER + EXTRA, HDIM), lambda i, s: (i, 0, 0))
ANYWHERE = pl.BlockSpec(memory_space=pl.ANY)


def head_specs(ids, rows):
    return [
        pl.BlockSpec(ids.shape, lambda i, s: (0, 0)),
        pl.BlockSpec((rows, HDIM), lambda i, s: (0, s[0] * HALF + i)),
    ]


def theirs_of(side, ids, queries):
    return pl.pallas_call(
        theirs_kernel,
        out_shape=BY_OWNER,
        grid_spec=pltpu.PrefetchScalarGridSpec(
            num_scalar_prefetch=1,
            grid=(HALF,),
            in_specs=head_specs(ids, queries.shape[0]),
            out_specs=OWNER_BLOCK,
        ),
        compiler_params=params(56),
    )(side, ids, queries)


def mine_of(side, ids, queries, arrived, passed):
    others = passed[1:]
    return pl.pallas_call(
        mine_kernel,
        out_shape=(BY_OWNER, jax.ShapeDtypeStruct(passed[0].shape, passed[0].dtype)),
        grid_spec=pltpu.PrefetchScalarGridSpec(
            num_scalar_prefetch=1,
            grid=(HALF,),
            in_specs=head_specs(ids, queries.shape[0])
            + [OWNER_BLOCK]
            + [ANYWHERE] * len(passed),
            out_specs=(OWNER_BLOCK, ANYWHERE),
        ),
        input_output_aliases={4: 1},
        compiler_params=params(56),
    )(side, ids, queries, arrived, passed[0], *others)


def centre_kernel(in_ref, out_ref):
    whole = in_ref[0]
    for k in range(1, in_ref.shape[0]):
        whole += in_ref[k]
    count_row = whole[QUARTER : QUARTER + 1, :]
    spread = jnp.where(eye(QUARTER, HDIM), count_row, 0.0)
    count = jnp.sum(spread, axis=1, keepdims=True)
    centre = (whole[:QUARTER] / count).astype(BF16)
    for k in range(out_ref.shape[0]):
        out_ref[k] = centre


def attention_kernel(side_ref, centre_ref, k_ref, k_other_ref, v_ref, v_other_ref, out_ref):
    del side_ref
    centre = centre_ref[...]
    own = lax.dot_general(centre, k_ref[...], NT, preferred_element_type=F32)
    other = lax.dot_general(centre, k_other_ref[...], NT, preferred_element_type=F32)
    peak = jnp.maximum(
        jnp.max(own, axis=1, keepdims=True), jnp.max(other, axis=1, keepdims=True)
    )
    own_w = jnp.exp2((own - peak) * LOG2_SCALE).astype(BF16)
    other_w = jnp.exp2((other - peak) * LOG2_SCALE).astype(BF16)
    ones = jnp.ones(v_ref.shape, BF16)
    both = jnp.dot(
        own_w, jnp.concatenate([v_ref[...], ones], axis=1), preferred_element_type=F32
    ) + jnp.dot(
        other_w, jnp.concatenate([v_other_ref[...], ones], axis=1), preferred_element_type=F32
    )
    mass = both[:, HDIM:]
    part = (both[:, :HDIM] / mass).astype(BF16)
    level = peak * LOG2_SCALE + jnp.log2(mass)
    diagonal = eye(QUARTER, HDIM)
    line = lax.broadcasted_iota(jnp.int32, (TAIL, HDIM), 0)
    for k in range(4):
        lines = slice(k * QUARTER, (k + 1) * QUARTER)
        row = jnp.sum(jnp.where(diagonal, level[lines], 0.0), axis=0, keepdims=True)
        high = row.astype(BF16).astype(F32)
        mid = (row - high).astype(BF16).astype(F32)
        low = row - high - mid
        tail = jnp.where(line == 0, high, jnp.where(line == 1, mid, jnp.where(line == 2, low, 0.0)))
        out_ref[k, :QUARTER, :] = part[lines]
        out_ref[k, QUARTER:, :] = tail.astype(BF16)


def attention_of(side, centre, keys, keys_other, values, values_other):
    rows = keys.shape[0]
    wide = pl.BlockSpec((rows, HDIM), lambda i, s: (0, s[0] * HALF + i))
    narrow = pl.BlockSpec((rows, HDIM), lambda i, s: (0, i))
    return pl.pallas_call(
        attention_kernel,
        out_shape=jax.ShapeDtypeStruct((4 * HALF, QUARTER + TAIL, HDIM), BF16),
        grid_spec=pltpu.PrefetchScalarGridSpec(
            num_scalar_prefetch=1,
            grid=(HALF,),
            in_specs=[
                pl.BlockSpec((None, CLUSTERS, HDIM), lambda i, s: (i, 0, 0)),
                wide,
                narrow,
                wide,
                narrow,
            ],
            out_specs=pl.BlockSpec((4, QUARTER + TAIL, HDIM), lambda i, s: (i, 0, 0)),
        ),
        compiler_params=params(32),
    )(side, centre, keys, keys_other, values, values_other)


def combine_kernel(in_ref, out_ref):
    count = in_ref.shape[0]
    tails = [in_ref[k, QUARTER:, :].astype(F32) for k in range(count)]
    levels = [t[0:1] + t[1:2] + t[2:3] for t in tails]
    top = functools.reduce(jnp.maximum, levels)
    shares = [jnp.exp2(level - top) for level in levels]
    mass = functools.reduce(jnp.add, shares)
    diagonal = eye(QUARTER, HDIM)
    whole = jnp.zeros((QUARTER, HDIM), F32)
    for k in range(count):
        spread = jnp.where(diagonal, shares[k] / mass, 0.0)
        share = jnp.sum(spread, axis=1, keepdims=True)
        whole += share * in_ref[k, :QUARTER, :].astype(F32)
    whole = whole.astype(BF16)
    for k in range(out_ref.shape[0]):
        out_ref[k] = whole


def one_hot(column):
    labels = lax.broadcasted_iota(jnp.int32, (column.shape[0], CLUSTERS), 1)
    return (labels == column).astype(F32).astype(BF16)


def columns_of(ids, upper):
    turned = jnp.where(upper == 0, ids, pltpu.roll(ids, HALF, 0))
    return turned.T


def gather_kernel(place_ref, ids_ref, table_ref, out_ref):
    columns = columns_of(ids_ref[...], place_ref[0])
    for j in range(HALF):
        rows = jnp.dot(one_hot(columns[:, j : j + 1]), table_ref[j], preferred_element_type=F32)
        out_ref[:, j * HDIM : (j + 1) * HDIM] = rows.astype(BF16)


def group_at(i, place, groups):
    return lax.rem(place[1] + groups - i, groups)


def gather_of(place, ids, table):
    groups, lines, tokens = ids.shape
    return pl.pallas_call(
        gather_kernel,
        out_shape=jax.ShapeDtypeStruct((tokens, groups * HALF * HDIM), BF16),
        grid_spec=pltpu.PrefetchScalarGridSpec(
            num_scalar_prefetch=1,
            grid=(groups,),
            in_specs=[
                pl.BlockSpec((None, lines, tokens), lambda i, s: (i, 0, 0)),
                pl.BlockSpec(
                    (HALF, CLUSTERS, HDIM), lambda i, s: (group_at(i, s, groups), 0, 0)
                ),
            ],
            out_specs=pl.BlockSpec((tokens, HALF * HDIM), lambda i, s: (0, i)),
        ),
        compiler_params=params(24),
    )(place, ids, table)


def project_kernel(groups, place_ref, near_ref, ids_ref, table_ref, w_ref, out_ref, far_ref, acc_ref):
    step = pl.program_id(0)
    weight = jnp.concatenate([w_ref[k] for k in range(w_ref.shape[0])], axis=1)

    @pl.when(step == 0)
    def _():
        acc_ref[...] = jnp.dot(near_ref[...], weight, preferred_element_type=F32)

    @pl.when((step > 0) & (step < groups))
    def _():
        acc_ref[...] += jnp.dot(near_ref[...], weight, preferred_element_type=F32)

    @pl.when(step >= groups)
    def _():
        columns = columns_of(ids_ref[...], 1 - place_ref[0])
        for j in range(HALF):
            rows = jnp.dot(one_hot(columns[:, j : j + 1]), table_ref[j], preferred_element_type=F32)
            far_ref[:, j * HDIM : (j + 1) * HDIM] = rows.astype(BF16)
        acc_ref[...] += jnp.dot(far_ref[...], weight, preferred_element_type=F32)

    @pl.when(step == 2 * groups - 1)
    def _():
        out_ref[...] = acc_ref[...].astype(BF16)


def project_of(place, near, ids, table, weight):
    groups, lines, tokens = ids.shape
    depth = HALF * HDIM
    blocks = weight.shape[1]
    cols = blocks * weight.shape[3]

    def early(i):
        return jnp.minimum(i, groups - 1)

    def late(i):
        return jnp.maximum(i - groups, 0)

    def weight_at(i, s):
        near_half = i < groups
        group = group_at(jnp.where(near_half, i, i - groups), s, groups)
        return (group, 0, jnp.where(near_half, s[0], 1 - s[0]), 0)

    return pl.pallas_call(
        functools.partial(project_kernel, groups),
        out_shape=jax.ShapeDtypeStruct((tokens, cols), BF16),
        grid_spec=pltpu.PrefetchScalarGridSpec(
            num_scalar_prefetch=1,
            grid=(2 * groups,),
            in_specs=[
                pl.BlockSpec((tokens, depth), lambda i, s: (0, early(i))),
                pl.BlockSpec((None, lines, tokens), lambda i, s: (late(i), 0, 0)),
                pl.BlockSpec(
                    (HALF, CLUSTERS, HDIM), lambda i, s: (group_at(late(i), s, groups), 0, 0)
                ),
                pl.BlockSpec((None, blocks, depth, weight.shape[3]), weight_at),
            ],
            out_specs=pl.BlockSpec((tokens, cols), lambda i, s: (0, 0)),
            scratch_shapes=[pltpu.VMEM((tokens, depth), BF16), pltpu.VMEM((tokens, cols), F32)],
        ),
        compiler_params=params(50),
    )(place, near, ids, table, weight)


def other_core(value):
    return lax.ppermute(value, "c", [(0, 1), (1, 0)])


def exchanged(value, axes):
    return lax.all_to_all(value, axes, split_axis=0, concat_axis=0, tiled=True)


def from_all_groups(value):
    size = lax.axis_size("z")
    found = [value]
    for d in range(1, size):
        found.append(lax.ppermute(value, "z", [(i, (i + d) % size) for i in range(size)]))
    return found


def local(queries, keys, values, cluster_ids, out_weight):
    core = lax.axis_index("c").astype(jnp.int32)
    side = core[None]
    place = jnp.stack([core, lax.axis_index("z").astype(jnp.int32)])
    half_cols = HALF * HDIM
    ids = cluster_ids.T
    rows = keys.shape[0]
    far_cols = (1 - core) * half_cols

    arrived = other_core(theirs_of(1 - side, ids, queries))
    keys_other = other_core(lax.dynamic_slice(keys, (0, far_cols), (rows, half_cols)))
    values_other = other_core(lax.dynamic_slice(values, (0, far_cols), (rows, half_cols)))
    size = lax.axis_size("z")
    turned = [(a * size + b, b * size + a) for a in range(size) for b in range(size)]
    turned_weight = lax.ppermute(out_weight, ("x", "z"), turned)
    all_ids = from_all_groups(ids)

    totals, turned_weight = mine_of(side, ids, queries, arrived, [turned_weight, *all_ids[1:]])
    weight = lax.all_gather(turned_weight, SEQ, axis=0)
    weight = weight.reshape(size, -1, *weight.shape[1:])
    totals = exchanged(totals, PLANE)
    copies = lax.axis_size(PLANE)
    centre = pl.pallas_call(
        centre_kernel,
        out_shape=jax.ShapeDtypeStruct((copies, QUARTER, HDIM), BF16),
        compiler_params=params(8),
    )(totals)
    centre = exchanged(centre, PLANE).reshape(HALF, CLUSTERS, HDIM)
    parts = exchanged(
        attention_of(side, centre, keys, keys_other, values, values_other), PLANE
    )
    table = pl.pallas_call(
        combine_kernel,
        out_shape=jax.ShapeDtypeStruct((lax.axis_size(CUBE), QUARTER, HDIM), BF16),
        compiler_params=params(8),
    )(parts)
    table = exchanged(table, CUBE).reshape(size * HALF, CLUSTERS, HDIM)
    far_table = other_core(table)
    stacked = jnp.stack(all_ids)
    near = gather_of(place, stacked, table)
    return project_of(place, near, stacked, far_table, weight)


def solution(mesh):
    head = mesh.shape["head"]
    finer = Mesh(mesh.devices.reshape(4, 4, 2, head), ("x", "y", "c", "z"))
    in_specs = (P(SEQ, "z"), P(SEQ, "z"), P(SEQ, "z"), P(SEQ, "z"), P("z", SEQ))
    return jax.shard_map(
        local, mesh=finer, in_specs=in_specs, out_specs=P(SEQ, "z"), check_vma=False
    )
```

time: 256 us -> 157 us (0.61)
  waiting for transfers between devices: 85.1 us -> 16.5 us
  Pallas kernels: 0 us -> 40.4 us
  matrix products: 33.6 us -> 0 us
  blocking collectives: 86.4 us -> 59.8 us
  starting transfers between devices: 4.11 us -> 17.1 us
  other arithmetic: 12.6 us -> 0.09 us
  local copies, waits for them, and re-layouts: 19.4 us -> 8.56 us
    reduce_scatter x1 -> x0, waiting for transfers between devices: 79.7 us -> none  [local(): lax.psum_scatter(head_part.astype(jnp.bfloat16), 'head', scatter_dimensio...]
    pallas_call x0 -> x7, Pallas kernels: none -> 40.4 us  [the longest x1 18.7 us: project_of(): pl.pallas_call(functools.partial(project_kernel, groups), out_shape=jax.S...]
    dot_general x5 -> x0, matrix products: 33.6 us -> none  [the longest x1 14.8 us: local(): jnp.dot(attended, lax.all_gather(out_weight, SEQ, axis=1, tiled=True), pr...]
    all_to_all x8 -> x3, blocking collectives: 86.4 us -> 59.8 us  [exchanged(): return lax.all_to_all(value, axes, split_axis=0, concat_axis=0, tiled=True)]
    ppermute x0 -> x8, starting transfers between devices: none -> 13.6 us  [the longest x3 7.67 us: from_all_groups(): lax.ppermute(value, 'z', [(i, (i + d) % size) for i in range(size)])]
    reduce_sum x6 -> x0, other arithmetic: 10.5 us -> none  [the longest x1 4.36 us: local(): block_mass = jnp.sum(weights, axis=2, dtype=jnp.float32)]
    ppermute x0 -> x8, waiting for transfers between devices: none -> 9.21 us  [the longest x3 9.2 us: from_all_groups(): lax.ppermute(value, 'z', [(i, (i + d) % size) for i in range(size)])]
    another operation x4 -> x0, local copies, waits for them, and re-layouts: 7.41 us -> none  [the longest x2 3.93 us: split_up(): value.reshape(*shape[:dim], size, shape[dim] // size, *shape[dim + 1:])]
  transfers between devices with their start and end apart: 3 -> 10, of which waited for: 2 -> 3; matrix products, arithmetic and copies ran while one was open for 18% -> 2% of each run, Pallas kernels for 0% -> 9%
where the time goes in v1:
time: 157 us; the launch traced here: 156 us
  blocking collectives  59.8 us (38%)
  Pallas kernels  40.4 us (26%)
  starting transfers between devices  17.1 us (11%)
  waiting for transfers between devices  16.5 us (11%)
  between operations  13.6 us (9%)
  local copies, waits for them, and re-layouts  8.56 us (5%)
    all_to_all x3, blocking collectives, exchanged(): return lax.all_to_all(value, axes, split_axis=0, concat_axis=0, tiled=True)  59.8 us
    pallas_call x1, Pallas kernels, project_of(): pl.pallas_call(functools.partial(project_kernel, groups), out_shape=jax.S...  18.7 us
    ppermute x3, waiting for transfers between devices, from_all_groups(): lax.ppermute(value, 'z', [(i, (i + d) % size) for i in range(size)])  9.2 us
    ppermute x3, starting transfers between devices, from_all_groups(): lax.ppermute(value, 'z', [(i, (i + d) % size) for i in range(size)])  7.67 us
    all_to_all x1, waiting for transfers between devices, exchanged(): return lax.all_to_all(value, axes, split_axis=0, concat_axis=0, tiled=True)  7.29 us
    pallas_call x1, Pallas kernels, attention_of(): pl.pallas_call(attention_kernel, out_shape=jax.ShapeDtypeStruct((4 * HALF...  7.05 us
    ppermute x4, starting transfers between devices, other_core(): return lax.ppermute(value, 'c', [(0, 1), (1, 0)])  5.27 us
    unnamed x30, local copies, waits for them, and re-layouts  5.13 us
  transfers between devices with their start and end apart: 10, of which 3 were waited for; matrix products, arithmetic and copies ran while one was open for 2% of the time, Pallas kernels for 9%

profile of v1, /device:TPU:1, one launch (start us, length us, event | category | flops | bytes accessed | tf_op | source)
XLA Modules:
  0.0 156.1 jit_solution(7333317198519472793)
XLA Ops:
  6.5 0.0 copy-start.6
  6.5 0.0 copy-start.14
  6.5 0.0 all-gather.3.cloned.1.call-start
  6.5 4.2 %shard_map.55 = f32[16,72,128]{2,1,0:T(8,128)} custom-call(s32[1]{0:T(128)S(6)} %sub.6.side_ref, s32[8,1024]{1,0:T(8,128)} %bitcast.15, bf16[1024,1024]{1,0:T(8,128)(2,1)} %q_ref.3), custom_call_target="tpu_custom_call" | custom-call | tf_op jit(solution)/shard_map/pallas_call | solution.py:82
  10.7 0.0 copy-start.1
  10.7 1.4 collective-permute-start.3
  12.2 0.0 copy-done.14
  12.2 0.7 collective-permute-start.4
  12.8 0.0 copy-done.6
  12.8 6.3 %collective-permute-start.2 = (s32[8,1024]{1,0:T(8,128)S(1)}, s32[8,1024]{1,0:T(8,128)S(1)}, u32[]{:S(2)}, u32[]{:S(2)}) collective-permute-start(s32[8,1024]{1,0:T(8,128)S(1)} %bitcast.17), channel_id=1, source_target_pairs={{0,3},{1,0},{2,1},{3,2},{4,7},{5,4},{6,5},{7,6},{8,11},{9,8},{10,9... | collective-permute-start | bytes 98312 | tf_op jit(solution)/shard_map/ppermute | solution.py:314
  19.1 0.7 collective-permute-start.1
  19.7 0.8 collective-permute-start
  20.5 0.0 collective-permute-done.2.rest_2_
  20.5 0.0 copy-start.8
  20.5 8.4 %collective-permute-done.1.rest_1_ = s32[8,1024]{1,0:T(8,128)S(1)} collective-permute-done((s32[8,1024]{1,0:T(8,128)S(1)}, s32[8,1024]{1,0:T(8,128)S(1)}, u32[]{:S(2)}, u32[]{:S(2)}) %collective-permute-start.1) | collective-permute-done | bytes 32800 | tf_op jit(solution)/shard_map/ppermute | solution.py:314
  28.9 0.0 copy-start.10
  28.9 0.8 collective-permute-done.rest_0_
  29.7 0.0 copy-start.12
  29.7 0.0 collective-permute-done.4.w_ref
  29.7 0.0 copy-start.3
  29.7 0.0 collective-permute-done.3.in_ref
  29.7 0.0 copy-done.8
  29.7 0.0 copy-done.10
  29.8 0.6 copy-done.12
  30.3 0.1 copy-done.3
  30.5 0.0 copy-start.4
  30.5 0.8 copy-done.4
  31.3 4.2 %shard_map.56 = (f32[16,72,128]{2,1,0:T(8,128)}, bf16[1024,128]{1,0:T(8,128)(2,1)}) custom-call(s32[1]{0:T(128)} %bitcast.side_ref, s32[8,1024]{1,0:T(8,128)} %bitcast.16, bf16[1024,1024]{1,0:T(8,128)(2,1)} %q_ref.3, f32[16,72,128]{2,1,0:T(8,128)} %copy-done.4, bf16[1024,128]{1,0:T(8,128)(2,1)} %copy-done.3, ...), custom_call_target="tpu_custom_call", output_to_operand_aliasing={{1}: (4, {})} | custom-call | tf_op jit(solution)/shard_map/pallas_call | solution.py:97
  35.5 0.0 all-gather.3.cloned.1.call-update
  35.5 0.0 copy-start.5
  35.5 2.4 %constant_dynamic-slice_fusion = bf16[1024,512]{1,0:T(8,128)(2,1)} fusion(bf16[1024,1024]{1,0:T(8,128)(2,1)} %v_ref.1, s32[]{:T(128)S(6)} %select_n.4), kind=kLoop, calls=%fused_computation.2 | loop fusion | bytes 2097156 | tf_op jit(solution)/shard_map/dynamic_slice | solution.py:329
  37.9 0.5 collective-permute-start.6
  38.4 0.0 copy-done.1
  38.4 1.1 constant_dynamic-slice_fusion.1
  39.4 0.0 collective-permute-start.5
  39.5 0.0 copy-done.5
  39.5 24.6 %all_to_all.20.in_ref = f32[16,72,128]{2,1,0:T(8,128)S(1)} all-to-all(f32[16,72,128]{2,1,0:T(8,128)S(1)} %copy-done.5), channel_id=1, replica_groups=mesh['x'=4,'y'=4,'c'=2,'z'=4] {'x','y'}, dimensions={0} | all-to-all | bytes 1179648 | tf_op jit(solution)/shard_map/all_to_all | solution.py:307
  64.1 0.8 shard_map.57
  64.9 3.5 %all-to-all-start.1 = ((bf16[16,64,128]{2,1,0:T(8,128)(2,1)}), bf16[16,64,128]{2,1,0:T(8,128)(2,1)S(1)}, u32[]{:S(2)}, u32[]{:S(2)}) async-start(bf16[16,64,128]{2,1,0:T(8,128)(2,1)} %shard_map.57), calls=%async_computation.1 | async-start | bytes 524288 | tf_op jit(solution)/shard_map/all_to_all | solution.py:307
  68.5 0.0 collective-permute-done.6.v_other_ref
  68.5 0.0 collective-permute-done.5.k_other_ref
  68.5 7.3 %all-to-all-done.1 = bf16[16,64,128]{2,1,0:T(8,128)(2,1)S(1)} async-done(((bf16[16,64,128]{2,1,0:T(8,128)(2,1)}), bf16[16,64,128]{2,1,0:T(8,128)(2,1)S(1)}, u32[]{:S(2)}, u32[]{:S(2)}) %all-to-all-start.1) | async-done | bytes 262176 | tf_op jit(solution)/shard_map/all_to_all | solution.py:307
  75.8 0.0 copy-start.2
  75.8 1.6 %copy-done.2 = bf16[1024,1024]{1,0:T(8,128)(2,1)S(1)} copy-done((bf16[1024,1024]{1,0:T(8,128)(2,1)S(1)}, bf16[1024,1024]{1,0:T(8,128)(2,1)}, u32[]{:S(2)}) %copy-start.2) | copy-done | bytes 2097176
  77.4 7.1 %shard_map.58 = bf16[16,80,128]{2,1,0:T(8,128)(2,1)S(1)} custom-call(s32[1]{0:T(128)} %bitcast.side_ref, bf16[4,256,128]{2,1,0:T(8,128)(2,1)S(1)} %bitcast.13, bf16[1024,1024]{1,0:T(8,128)(2,1)S(1)} %copy-done.1, bf16[1024,512]{1,0:T(8,128)(2,1)} %collective-permute-done.5.k_other_ref, bf16[1024,1024]{1,0:T(8,128)(2,1)S(1)} %copy-done.2, ...), custom_call_target="tpu_custom_call" | custom-call | tf_op jit(solution)/shard_map/pallas_call | solution.py:161
  84.4 0.0 copy-start.7
  84.4 0.0 copy-start.9
  84.4 0.0 copy-start.11
  84.5 0.0 copy-start.13
  84.5 11.9 %all_to_all.21.in_ref = bf16[16,80,128]{2,1,0:T(8,128)(2,1)S(1)} all-to-all(bf16[16,80,128]{2,1,0:T(8,128)(2,1)S(1)} %shard_map.58), channel_id=1, replica_groups=mesh['x'=4,'y'=4,'c'=2,'z'=4] {'x','y'}, dimensions={0} | all-to-all | bytes 655360 | tf_op jit(solution)/shard_map/all_to_all | solution.py:307
  96.4 0.4 shard_map.59
  96.7 23.3 %all_to_all.22 = bf16[64,64,128]{2,1,0:T(8,128)(2,1)S(1)} all-to-all(bf16[64,64,128]{2,1,0:T(8,128)(2,1)S(1)} %shard_map.59), channel_id=1, replica_groups=mesh['x'=4,'y'=4,'c'=2,'z'=4] {'z','x','y'}, dimensions={0} | all-to-all | bytes 2097152 | tf_op jit(solution)/shard_map/all_to_all | solution.py:307
  120.1 3.3 %collective-permute-start.7 = (bf16[16,256,128]{2,1,0:T(8,128)(2,1)S(1)}, bf16[16,256,128]{2,1,0:T(8,128)(2,1)S(1)}, u32[]{:S(2)}, u32[]{:S(2)}) collective-permute-start(bf16[16,256,128]{2,1,0:T(8,128)(2,1)S(1)} %bitcast.11), channel_id=1, source_target_pairs={{0,4},{4,0},{1,5},{5,1},{2,6},{6,2},{3,7},{7,3},{8,12},{12,8},{9,1... | collective-permute-start | bytes 3145736 | tf_op jit(solution)/shard_map/ppermute | solution.py:303
  123.4 0.1 pad_add_fusion.1.place_ref
  123.5 0.0 copy-done.7
  123.5 0.0 copy-done.9
  123.5 0.0 copy-done.11
  123.5 0.0 copy-done.13
  123.5 5.0 %shard_map.60.near_ref = bf16[1024,2048]{1,0:T(8,128)(2,1)S(1)} custom-call(s32[2]{0:T(128)S(1)} %pad_add_fusion.1.place_ref, s32[4,8,1024]{2,1,0:T(8,128)S(1)} %pad_add_fusion.ids_ref, bf16[16,256,128]{2,1,0:T(8,128)(2,1)S(1)} %bitcast.12), custom_call_target="tpu_custom_call" | custom-call | tf_op jit(solution)/shard_map/pallas_call | solution.py:221
  128.5 0.0 copy-start
  128.5 2.0 %copy-done = bf16[1024,2048]{1,0:T(8,128)(2,1)} copy-done((bf16[1024,2048]{1,0:T(8,128)(2,1)}, bf16[1024,2048]{1,0:T(8,128)(2,1)S(1)}, u32[]{:S(2)}) %copy-start) | copy-done | bytes 4194328
  130.5 0.0 collective-permute-done.7.table_ref
  130.5 0.0 all-gather.3.cloned.1.call-done
  130.5 18.7 %shard_map.61 = bf16[1024,1024]{1,0:T(8,128)(2,1)} custom-call(s32[2]{0:T(128)S(1)} %pad_add_fusion.1.place_ref, bf16[1024,2048]{1,0:T(8,128)(2,1)} %copy-done, s32[4,8,1024]{2,1,0:T(8,128)S(1)} %pad_add_fusion.ids_ref, bf16[16,256,128]{2,1,0:T(8,128)(2,1)S(1)} %collective-permute-done.7.table_ref, bf16[4,8,1024,128]{3,2,1,0:T(8,128)(2,1)} %bitcast.14), custom_call_target="tpu_custom_call" | custom-call | tf_op jit(solution)/shard_map/pallas_call | solution.py:281
  (1 shorter events, 0.0 us)
Async XLA Ops:
  6.5 6.3 %copy-start.6 = (s32[1024,8]{0,1:T(8,128)S(1)}, s32[1024,8]{0,1:T(8,128)}, u32[]{:S(2)}) copy-start(s32[1024,8]{0,1:T(8,128)} %param.8) | copy-start | bytes 98308
  6.5 5.6 %copy-start.14 = (bf16[1024,128]{1,0:T(8,128)(2,1)S(1)}, bf16[1024,128]{1,0:T(8,128)(2,1)}, u32[]{:S(2)}) copy-start(bf16[1024,128]{1,0:T(8,128)(2,1)} %param.9) | copy-start | bytes 786436
  6.5 124.0 %all-gather.3.cloned.1.call-start = ((), (), s32[]{:S(2)}) async-start(), calls=%async_computation.4 | async-start | bytes 8650752 | tf_op jit(solution)/shard_map/all_gather | solution.py:336
  10.7 27.6 %copy-start.1 = (bf16[1024,1024]{1,0:T(8,128)(2,1)S(1)}, bf16[1024,1024]{1,0:T(8,128)(2,1)}, u32[]{:S(2)}) copy-start(bf16[1024,1024]{1,0:T(8,128)(2,1)} %k_ref.1) | copy-start | bytes 6291460
  10.7 19.0 %collective-permute-start.3 = (f32[16,72,128]{2,1,0:T(8,128)}, f32[16,72,128]{2,1,0:T(8,128)S(1)}, u32[]{:S(2)}, u32[]{:S(2)}) collective-permute-start(f32[16,72,128]{2,1,0:T(8,128)} %shard_map.55), channel_id=1, source_target_pairs={{0,4},{4,0},{1,5},{5,1},{2,6},{6,2},{3,7},{7,3},{8,12},{12,8},{9,1... | collective-permute-start | bytes 1769480 | tf_op jit(solution)/shard_map/ppermute | solution.py:303
  12.2 17.6 %collective-permute-start.4 = (bf16[1024,128]{1,0:T(8,128)(2,1)S(1)}, bf16[1024,128]{1,0:T(8,128)(2,1)S(1)}, u32[]{:S(2)}, u32[]{:S(2)}) collective-permute-start(bf16[1024,128]{1,0:T(8,128)(2,1)S(1)} %copy-done.14), channel_id=1, source_target_pairs={{0,0},{1,32},{2,64},{3,96},{32,1},{33,33},{34,65},{35,97},{64,2},{... | collective-permute-start | bytes 786440 | tf_op jit(solution)/shard_map/ppermute | solution.py:332
  12.8 7.7 %collective-permute-start.2 = (s32[8,1024]{1,0:T(8,128)S(1)}, s32[8,1024]{1,0:T(8,128)S(1)}, u32[]{:S(2)}, u32[]{:S(2)}) collective-permute-start(s32[8,1024]{1,0:T(8,128)S(1)} %bitcast.17), channel_id=1, source_target_pairs={{0,3},{1,0},{2,1},{3,2},{4,7},{5,4},{6,5},{7,6},{8,11},{9,8},{10,9... | collective-permute-start | bytes 98312 | tf_op jit(solution)/shard_map/ppermute | solution.py:314
  19.1 9.8 %collective-permute-start.1 = (s32[8,1024]{1,0:T(8,128)S(1)}, s32[8,1024]{1,0:T(8,128)S(1)}, u32[]{:S(2)}, u32[]{:S(2)}) collective-permute-start(s32[8,1024]{1,0:T(8,128)S(1)} %bitcast.18), channel_id=1, source_target_pairs={{0,2},{1,3},{2,0},{3,1},{4,6},{5,7},{6,4},{7,5},{8,10},{9,11},{10,... | collective-permute-start | bytes 98312 | tf_op jit(solution)/shard_map/ppermute | solution.py:314
  19.7 10.0 %collective-permute-start = (s32[8,1024]{1,0:T(8,128)S(1)}, s32[8,1024]{1,0:T(8,128)S(1)}, u32[]{:S(2)}, u32[]{:S(2)}) collective-permute-start(s32[8,1024]{1,0:T(8,128)S(1)} %bitcast.19), channel_id=1, source_target_pairs={{0,1},{1,2},{2,3},{3,0},{4,5},{5,6},{6,7},{7,4},{8,9},{9,10},{10,1... | collective-permute-start | bytes 98312 | tf_op jit(solution)/shard_map/ppermute | solution.py:314
  20.5 9.2 %copy-start.8 = (s32[8,1024]{1,0:T(8,128)}, s32[8,1024]{1,0:T(8,128)S(1)}, u32[]{:S(2)}) copy-start(s32[8,1024]{1,0:T(8,128)S(1)} %collective-permute-done.2.rest_2_) | copy-start | bytes 98308
  28.9 0.9 copy-start.10
  29.7 0.6 copy-start.12
  29.7 0.7 copy-start.3
  30.5 0.8 copy-start.4
  35.5 4.0 %copy-start.5 = (f32[16,72,128]{2,1,0:T(8,128)S(1)}, f32[16,72,128]{2,1,0:T(8,128)}, u32[]{:S(2)}) copy-start(f32[16,72,128]{2,1,0:T(8,128)} %get-tuple-element.7) | copy-start | bytes 1769476
  37.9 30.6 %collective-permute-start.6 = (bf16[1024,512]{1,0:T(8,128)(2,1)}, bf16[1024,512]{1,0:T(8,128)(2,1)S(1)}, u32[]{:S(2)}, u32[]{:S(2)}) collective-permute-start(bf16[1024,512]{1,0:T(8,128)(2,1)} %constant_dynamic-slice_fusion), channel_id=1, source_target_pairs={{0,4},{4,0},{1,5},{5,1},{2,6},{6,2},{3,7},{7,3},{8,12},{12,8},{9,1... | collective-permute-start | bytes 3145736 | tf_op jit(solution)/shard_map/ppermute | solution.py:303
  39.4 29.0 %collective-permute-start.5 = (bf16[1024,512]{1,0:T(8,128)(2,1)}, bf16[1024,512]{1,0:T(8,128)(2,1)}, u32[]{:S(2)}, u32[]{:S(2)}) collective-permute-start(bf16[1024,512]{1,0:T(8,128)(2,1)} %constant_dynamic-slice_fusion.1), channel_id=1, source_target_pairs={{0,4},{4,0},{1,5},{5,1},{2,6},{6,2},{3,7},{7,3},{8,12},{12,8},{9,1... | collective-permute-start | bytes 3145736 | tf_op jit(solution)/shard_map/ppermute | solution.py:303
  64.9 10.8 %all-to-all-start.1 = ((bf16[16,64,128]{2,1,0:T(8,128)(2,1)}), bf16[16,64,128]{2,1,0:T(8,128)(2,1)S(1)}, u32[]{:S(2)}, u32[]{:S(2)}) async-start(bf16[16,64,128]{2,1,0:T(8,128)(2,1)} %shard_map.57), calls=%async_computation.1 | async-start | bytes 524288 | tf_op jit(solution)/shard_map/all_to_all | solution.py:307
  75.8 1.6 %copy-start.2 = (bf16[1024,1024]{1,0:T(8,128)(2,1)S(1)}, bf16[1024,1024]{1,0:T(8,128)(2,1)}, u32[]{:S(2)}) copy-start(bf16[1024,1024]{1,0:T(8,128)(2,1)} %v_ref.1) | copy-start | bytes 6291460
  84.4 39.1 %copy-start.7 = (s32[1024,8]{0,1:T(8,128)S(1)}, s32[1024,8]{0,1:T(8,128)}, u32[]{:S(2)}) copy-start(s32[1024,8]{0,1:T(8,128)} %param.8) | copy-start | bytes 98308
  84.4 39.0 %copy-start.9 = (s32[8,1024]{1,0:T(8,128)S(1)}, s32[8,1024]{1,0:T(8,128)}, u32[]{:S(2)}) copy-start(s32[8,1024]{1,0:T(8,128)} %copy-done.8) | copy-start | bytes 98308
  84.4 39.0 %copy-start.11 = (s32[8,1024]{1,0:T(8,128)S(1)}, s32[8,1024]{1,0:T(8,128)}, u32[]{:S(2)}) copy-start(s32[8,1024]{1,0:T(8,128)} %copy-done.10) | copy-start | bytes 98308
  84.5 39.0 %copy-start.13 = (s32[8,1024]{1,0:T(8,128)S(1)}, s32[8,1024]{1,0:T(8,128)}, u32[]{:S(2)}) copy-start(s32[8,1024]{1,0:T(8,128)} %copy-done.12) | copy-start | bytes 98308
  120.1 10.5 %collective-permute-start.7 = (bf16[16,256,128]{2,1,0:T(8,128)(2,1)S(1)}, bf16[16,256,128]{2,1,0:T(8,128)(2,1)S(1)}, u32[]{:S(2)}, u32[]{:S(2)}) collective-permute-start(bf16[16,256,128]{2,1,0:T(8,128)(2,1)S(1)} %bitcast.11), channel_id=1, source_target_pairs={{0,4},{4,0},{1,5},{5,1},{2,6},{6,2},{3,7},{7,3},{8,12},{12,8},{9,1... | collective-permute-start | bytes 3145736 | tf_op jit(solution)/shard_map/ppermute | solution.py:303
  128.5 2.0 %copy-start = (bf16[1024,2048]{1,0:T(8,128)(2,1)}, bf16[1024,2048]{1,0:T(8,128)(2,1)S(1)}, u32[]{:S(2)}) copy-start(bf16[1024,2048]{1,0:T(8,128)(2,1)S(1)} %shard_map.60.near_ref) | copy-start | bytes 12582916
Sparse Core Ops, SparseCore 0:
  35.6 60.5 all-gather.2

commit v2 on v0

v2 whole, which is shorter than its diff:
```python
import functools
import math

import jax
import jax.numpy as jnp
from jax import lax
from jax.experimental import pallas as pl
from jax.experimental.pallas import tpu as pltpu
from jax.sharding import Mesh
from jax.sharding import PartitionSpec as P

HDIM = 128
CLUSTERS = 256
HALF = 4
QUARTER = CLUSTERS // 4
SEQ = ("x", "y", "c")
PLANE = ("x", "y")
CUBE = ("z", "x", "y")
EXTRA = 8
TAIL = 16
LARGE = 61
LOG2_SCALE = math.log2(math.e) / math.sqrt(HDIM)
F32 = jnp.float32
BF16 = jnp.bfloat16
NT = (((1,), (1,)), ((), ()))
TN = (((0,), (0,)), ((), ()))


def params(mib):
    return pltpu.CompilerParams(vmem_limit_bytes=mib * 2**20)


def eye(rows, cols):
    r = lax.broadcasted_iota(jnp.int32, (rows, cols), 0)
    c = lax.broadcasted_iota(jnp.int32, (rows, cols), 1)
    return r == c


def member_of(row):
    labels = lax.broadcasted_iota(jnp.int32, (CLUSTERS, row.shape[1]), 0)
    return (labels == row).astype(F32).astype(BF16)


def totals_kernel(halves, side_ref, ids_ref, q_ref, *rest):
    sources, out_ref, copies = rest[:halves], rest[halves], rest[halves + 1 : 2 * halves + 1]
    held, arrived, copied = rest[2 * halves + 1 :]
    rows = q_ref.shape[0]
    first = side_ref[0] * HALF

    def fetch(i):
        start = pl.multiple_of((first + i) * HDIM, HDIM)
        return pltpu.make_async_copy(q_ref.at[:, pl.ds(start, HDIM)], held.at[i], arrived.at[i])

    def copy(k):
        start = pl.multiple_of((HALF - first) * HDIM, HALF * HDIM)
        return pltpu.make_async_copy(
            sources[k].at[:, pl.ds(start, HALF * HDIM)], copies[k], copied.at[k]
        )

    for i in range(HALF):
        fetch(i).start()
    for k in range(halves):
        copy(k).start()
    ones = jnp.ones((rows, HDIM), BF16)
    diagonal = eye(QUARTER, HDIM)
    for i in range(HALF):
        member = member_of(ids_ref[pl.ds(first + i, 1), :])
        fetch(i).wait()
        both = jnp.dot(
            member, jnp.concatenate([held[i], ones], axis=1), preferred_element_type=F32
        )
        for k in range(4):
            lines = slice(k * QUARTER, (k + 1) * QUARTER)
            count = jnp.sum(jnp.where(diagonal, both[lines, HDIM:], 0.0), axis=0, keepdims=True)
            out_ref[i * 4 + k, :QUARTER, :] = both[lines, :HDIM]
            out_ref[i * 4 + k, QUARTER:, :] = jnp.broadcast_to(count, (EXTRA, HDIM))
    for k in range(halves):
        copy(k).wait()


SCALARS = pl.BlockSpec(memory_space=pltpu.SMEM)
IN_VMEM = pl.BlockSpec(memory_space=pltpu.VMEM)
IN_HBM = pl.BlockSpec(memory_space=pltpu.HBM)


def totals_of(side, ids, queries, split=()):
    rows = queries.shape[0]
    halves = len(split)
    return pl.pallas_call(
        functools.partial(totals_kernel, halves),
        out_shape=[jax.ShapeDtypeStruct((4 * HALF, QUARTER + EXTRA, HDIM), F32)]
        + [jax.ShapeDtypeStruct((rows, HALF * HDIM), BF16)] * halves,
        in_specs=[SCALARS, IN_VMEM, IN_HBM] + [IN_HBM] * halves,
        out_specs=[IN_VMEM] + [IN_HBM] * halves,
        scratch_shapes=[
            pltpu.VMEM((HALF, rows, HDIM), BF16),
            pltpu.SemaphoreType.DMA((HALF,)),
            pltpu.SemaphoreType.DMA((max(halves, 1),)),
        ],
        compiler_params=params(LARGE),
    )(side, ids, queries, *split)


def add_kernel(a_ref, b_ref, passed_ref, out_ref, handed_ref):
    del passed_ref, handed_ref
    out_ref[...] = a_ref[...] + b_ref[...]


def add_after(a, b, passed):
    return pl.pallas_call(
        add_kernel,
        out_shape=(
            jax.ShapeDtypeStruct(a.shape, a.dtype),
            jax.ShapeDtypeStruct(passed.shape, passed.dtype),
        ),
        in_specs=[IN_VMEM, IN_VMEM, IN_HBM],
        out_specs=(IN_VMEM, IN_HBM),
        input_output_aliases={2: 1},
        compiler_params=params(8),
    )(a, b, passed)


def centre_kernel(in_ref, ids_ref, out_ref, ids_out_ref):
    whole = in_ref[0]
    for k in range(1, in_ref.shape[0]):
        whole += in_ref[k]
    spread = jnp.where(eye(QUARTER, HDIM), whole[QUARTER : QUARTER + 1, :], 0.0)
    count = jnp.sum(spread, axis=1, keepdims=True)
    centre = (whole[:QUARTER] / count).astype(BF16)
    for k in range(out_ref.shape[0]):
        out_ref[k] = centre
    ids_out_ref[...] = ids_ref[...]


def centre_of(totals, ids):
    return pl.pallas_call(
        centre_kernel,
        out_shape=(
            jax.ShapeDtypeStruct((totals.shape[0], QUARTER, HDIM), BF16),
            jax.ShapeDtypeStruct(ids.shape, ids.dtype),
        ),
        compiler_params=params(8),
    )(totals, ids)


def attention_kernel(groups, side_ref, centre_ref, *rest):
    ids_refs, sources = rest[:groups], rest[groups : groups + 4]
    out_ref, ids_out_ref, held, arrived, copied = rest[groups + 4 :]
    first = side_ref[0] * HALF

    def fetch(i):
        for k in range(4):
            start = i * HDIM if k % 2 else pl.multiple_of((first + i) * HDIM, HDIM)
            yield pltpu.make_async_copy(
                sources[k].at[:, pl.ds(start, HDIM)], held.at[i, k], arrived.at[i, k]
            )

    for i in range(HALF):
        for copy in fetch(i):
            copy.start()
    copies = [
        pltpu.make_async_copy(ids_refs[d], ids_out_ref.at[d], copied.at[d]) for d in range(groups)
    ]
    for copy in copies:
        copy.start()
    ones = jnp.ones(held.shape[2:], BF16)
    diagonal = eye(QUARTER, HDIM)
    line = lax.broadcasted_iota(jnp.int32, (TAIL, HDIM), 0)
    for i in range(HALF):
        for copy in fetch(i):
            copy.wait()
        centre = centre_ref[i]
        own = lax.dot_general(centre, held[i, 0], NT, preferred_element_type=F32)
        other = lax.dot_general(centre, held[i, 1], NT, preferred_element_type=F32)
        peak = jnp.maximum(
            jnp.max(own, axis=1, keepdims=True), jnp.max(other, axis=1, keepdims=True)
        )
        own_w = jnp.exp2((own - peak) * LOG2_SCALE).astype(BF16)
        other_w = jnp.exp2((other - peak) * LOG2_SCALE).astype(BF16)
        both = jnp.dot(
            own_w, jnp.concatenate([held[i, 2], ones], axis=1), preferred_element_type=F32
        ) + jnp.dot(
            other_w, jnp.concatenate([held[i, 3], ones], axis=1), preferred_element_type=F32
        )
        mass = both[:, HDIM:]
        part = (both[:, :HDIM] / mass).astype(BF16)
        level = peak * LOG2_SCALE + jnp.log2(mass)
        for k in range(4):
            lines = slice(k * QUARTER, (k + 1) * QUARTER)
            row = jnp.sum(jnp.where(diagonal, level[lines], 0.0), axis=0, keepdims=True)
            high = row.astype(BF16).astype(F32)
            mid = (row - high).astype(BF16).astype(F32)
            low = row - high - mid
            tail = jnp.where(
                line == 0, high, jnp.where(line == 1, mid, jnp.where(line == 2, low, 0.0))
            )
            out_ref[i * 4 + k, :QUARTER, :] = part[lines]
            out_ref[i * 4 + k, QUARTER:, :] = tail.astype(BF16)
    for copy in copies:
        copy.wait()


def attention_of(side, centre, all_ids, keys, keys_other, values, values_other):
    rows = keys.shape[0]
    groups = len(all_ids)
    return pl.pallas_call(
        functools.partial(attention_kernel, groups),
        out_shape=(
            jax.ShapeDtypeStruct((4 * HALF, QUARTER + TAIL, HDIM), BF16),
            jax.ShapeDtypeStruct((groups, *all_ids[0].shape), jnp.int32),
        ),
        in_specs=[SCALARS, IN_VMEM] + [IN_HBM] * groups + [IN_HBM] * 4,
        out_specs=(IN_VMEM, IN_VMEM),
        scratch_shapes=[
            pltpu.VMEM((HALF, 4, rows, HDIM), BF16),
            pltpu.SemaphoreType.DMA((HALF, 4)),
            pltpu.SemaphoreType.DMA((groups,)),
        ],
        compiler_params=params(LARGE),
    )(side, centre, *all_ids, keys, keys_other, values, values_other)


def combine_kernel(in_ref, out_ref):
    count = in_ref.shape[0]
    tails = [in_ref[k, QUARTER:, :].astype(F32) for k in range(count)]
    levels = [t[0:1] + t[1:2] + t[2:3] for t in tails]
    top = functools.reduce(jnp.maximum, levels)
    shares = [jnp.exp2(level - top) for level in levels]
    mass = functools.reduce(jnp.add, shares)
    diagonal = eye(QUARTER, HDIM)
    whole = jnp.zeros((QUARTER, HDIM), F32)
    for k in range(count):
        spread = jnp.where(diagonal, shares[k] / mass, 0.0)
        share = jnp.sum(spread, axis=1, keepdims=True)
        whole += share * in_ref[k, :QUARTER, :].astype(F32)
    whole = whole.astype(BF16)
    for k in range(out_ref.shape[0]):
        out_ref[k] = whole


def rows_of(ids_row, table):
    return lax.dot_general(member_of(ids_row), table, TN, preferred_element_type=F32).astype(BF16)


def group_at(i, place_ref, groups):
    return lax.rem(place_ref[1] + groups - i, groups)


def gather_kernel(place_ref, ids_ref, table_ref, out_ref):
    group = group_at(pl.program_id(0), place_ref, pl.num_programs(0))
    for j in range(HALF):
        row = ids_ref[pl.program_id(0), pl.ds(place_ref[0] * HALF + j, 1), :]
        out_ref[:, j * HDIM : (j + 1) * HDIM] = rows_of(row, table_ref[group * HALF + j])


def gather_of(place, ids, table):
    groups, lines, tokens = ids.shape
    return pl.pallas_call(
        gather_kernel,
        out_shape=jax.ShapeDtypeStruct((groups, tokens, HALF * HDIM), BF16),
        grid=(groups,),
        in_specs=[SCALARS, IN_VMEM, IN_VMEM],
        out_specs=pl.BlockSpec((None, tokens, HALF * HDIM), lambda i: (i, 0, 0)),
        compiler_params=params(LARGE),
    )(place, ids, table)


def project_kernel(
    place_ref, near_ref, ids_ref, table_ref, w_ref, out_ref, held, near, far, acc, arrived, come
):
    groups, blocks = w_ref.shape[:2]
    depth = HALF * HDIM

    def fetch(i):
        group = group_at(lax.rem(i, groups), place_ref, groups)
        entry = lax.rem(2 * place_ref[1] + groups - group, groups)
        side = jnp.where(i < groups, place_ref[0], 1 - place_ref[0])
        lines = pl.ds(pl.multiple_of(side * depth, depth), depth)
        return pltpu.make_async_copy(w_ref.at[entry, :, lines, :], held.at[i], arrived.at[i])

    def weight(i):
        return jnp.concatenate([held[i, k] for k in range(blocks)], axis=1)

    def bring(i):
        return pltpu.make_async_copy(near_ref.at[i], near.at[i], come.at[i])

    for i in range(groups):
        fetch(i).start()
        bring(i).start()
    for i in range(groups, 2 * groups):
        fetch(i).start()
    fetch(0).wait()
    bring(0).wait()
    acc[...] = jnp.dot(near[0], weight(0), preferred_element_type=F32)

    @pl.loop(1, groups)
    def _(i):
        fetch(i).wait()
        bring(i).wait()
        acc[...] += jnp.dot(near[i], weight(i), preferred_element_type=F32)

    @pl.loop(groups, 2 * groups)
    def _(i):
        group = group_at(i - groups, place_ref, groups)
        for j in range(HALF):
            row = ids_ref[i - groups, pl.ds((1 - place_ref[0]) * HALF + j, 1), :]
            far[:, j * HDIM : (j + 1) * HDIM] = rows_of(row, table_ref[group * HALF + j])
        fetch(i).wait()
        acc[...] += jnp.dot(far[...], weight(i), preferred_element_type=F32)

    out_ref[...] = acc[...].astype(BF16)


def project_of(place, near, ids, table, weight):
    groups, lines, tokens = ids.shape
    depth = HALF * HDIM
    blocks, width = weight.shape[1], weight.shape[3]
    cols = blocks * width
    return pl.pallas_call(
        project_kernel,
        out_shape=jax.ShapeDtypeStruct((tokens, cols), BF16),
        in_specs=[SCALARS, IN_HBM, IN_VMEM, IN_VMEM, IN_HBM],
        out_specs=IN_VMEM,
        scratch_shapes=[
            pltpu.VMEM((2 * groups, blocks, depth, width), BF16),
            pltpu.VMEM((groups, tokens, depth), BF16),
            pltpu.VMEM((tokens, depth), BF16),
            pltpu.VMEM((tokens, cols), F32),
            pltpu.SemaphoreType.DMA((2 * groups,)),
            pltpu.SemaphoreType.DMA((groups,)),
        ],
        compiler_params=params(56),
    )(place, near, ids, table, weight)


def other_core(value):
    return lax.ppermute(value, "c", [(0, 1), (1, 0)])


def exchanged(value, axes):
    return lax.all_to_all(value, axes, split_axis=0, concat_axis=0, tiled=True)


def from_all_groups(value):
    size = lax.axis_size("z")
    found = [value]
    for d in range(1, size):
        found.append(lax.ppermute(value, "z", [(i, (i + d) % size) for i in range(size)]))
    return found


def local(queries, keys, values, cluster_ids, out_weight):
    core = lax.axis_index("c").astype(jnp.int32)
    side = core[None]
    place = jnp.stack([core, lax.axis_index("z").astype(jnp.int32)])
    ids = cluster_ids.T
    size = lax.axis_size("z")
    turned = [
        (x * size + z, (2 * x - z) % size * size + x) for x in range(size) for z in range(size)
    ]
    turned_weight = lax.ppermute(out_weight, ("x", "z"), turned)

    (theirs,) = totals_of(1 - side, ids, queries)
    arrived = other_core(theirs)
    mine, keys_far, values_far = totals_of(side, ids, queries, (keys, values))
    keys_other, values_other = other_core(keys_far), other_core(values_far)
    totals, turned_weight = add_after(mine, arrived, turned_weight)
    weight = lax.all_gather(turned_weight, SEQ, axis=0)
    weight = weight.reshape(size, -1, *weight.shape[1:])

    centre, ids = centre_of(exchanged(totals, PLANE), ids)
    all_ids = from_all_groups(ids)
    centre = exchanged(centre, PLANE).reshape(HALF, CLUSTERS, HDIM)
    parts, all_ids = attention_of(
        side, centre, all_ids, keys, keys_other, values, values_other
    )
    parts = exchanged(parts, PLANE)
    table = pl.pallas_call(
        combine_kernel,
        out_shape=jax.ShapeDtypeStruct((lax.axis_size(CUBE), QUARTER, HDIM), BF16),
        compiler_params=params(8),
    )(parts)
    table = exchanged(table, CUBE).reshape(size * HALF, CLUSTERS, HDIM)
    far_table = other_core(table)
    near = gather_of(place, all_ids, table)
    return project_of(place, near, all_ids, far_table, weight)


def solution(mesh):
    head = mesh.shape["head"]
    finer = Mesh(mesh.devices.reshape(4, 4, 2, head), ("x", "y", "c", "z"))
    in_specs = (P(SEQ, "z"), P(SEQ, "z"), P(SEQ, "z"), P(SEQ, "z"), P("z", SEQ))
    return jax.shard_map(
        local, mesh=finer, in_specs=in_specs, out_specs=P(SEQ, "z"), check_vma=False
    )
```

time: 256 us -> 202 us (0.79)
  Pallas kernels: 0 us -> 105 us
  waiting for transfers between devices: 85.1 us -> 4.51 us
  matrix products: 33.6 us -> 0 us
  blocking collectives: 86.4 us -> 61.5 us
  local copies, waits for them, and re-layouts: 19.4 us -> 2.76 us
  other arithmetic: 12.6 us -> 0.66 us
  starting transfers between devices: 4.11 us -> 13.5 us
    pallas_call x0 -> x8, Pallas kernels: none -> 105 us  [the longest x2 71 us: totals_of(): pl.pallas_call(functools.partial(totals_kernel, halves), out_shape=[jax.S...]
    reduce_scatter x1 -> x0, waiting for transfers between devices: 79.7 us -> none  [local(): lax.psum_scatter(head_part.astype(jnp.bfloat16), 'head', scatter_dimensio...]
    dot_general x5 -> x0, matrix products: 33.6 us -> none  [the longest x1 14.8 us: local(): jnp.dot(attended, lax.all_gather(out_weight, SEQ, axis=1, tiled=True), pr...]
    all_to_all x8 -> x3, blocking collectives: 86.4 us -> 61.5 us  [exchanged(): return lax.all_to_all(value, axes, split_axis=0, concat_axis=0, tiled=True)]
    reduce_sum x6 -> x0, other arithmetic: 10.5 us -> none  [the longest x1 4.36 us: local(): block_mass = jnp.sum(weights, axis=2, dtype=jnp.float32)]
    ppermute x0 -> x8, starting transfers between devices: none -> 9.99 us  [the longest x4 5.82 us: other_core(): return lax.ppermute(value, 'c', [(0, 1), (1, 0)])]
    another operation x4 -> x0, local copies, waits for them, and re-layouts: 7.41 us -> none  [the longest x2 3.93 us: split_up(): value.reshape(*shape[:dim], size, shape[dim] // size, *shape[dim + 1:])]
    slice x6 -> x0, local copies, waits for them, and re-layouts: 4.89 us -> none  [packed_total(): so_far[b:e].reshape(a.shape)]
  transfers between devices with their start and end apart: 3 -> 10, of which waited for: 2 -> 3; matrix products, arithmetic and copies ran while one was open for 18% -> 0% of each run, Pallas kernels for 0% -> 41%
where the time goes in v2:
time: 202 us
  Pallas kernels  105 us (52%)
  blocking collectives  61.5 us (30%)
  between operations  13.6 us (7%)
  starting transfers between devices  13.5 us (7%)
  waiting for transfers between devices  4.51 us (2%)
  local copies, waits for them, and re-layouts  2.76 us (1%)
    pallas_call x2, Pallas kernels, totals_of(): pl.pallas_call(functools.partial(totals_kernel, halves), out_shape=[jax.S...  71 us
    all_to_all x3, blocking collectives, exchanged(): return lax.all_to_all(value, axes, split_axis=0, concat_axis=0, tiled=True)  61.5 us
    pallas_call x1, Pallas kernels, project_of(): pl.pallas_call(project_kernel, out_shape=jax.ShapeDtypeStruct((tokens, co...  18.3 us
    pallas_call x1, Pallas kernels, attention_of(): pl.pallas_call(functools.partial(attention_kernel, groups), out_shape=(ja...  8.74 us
    ppermute x4, starting transfers between devices, other_core(): return lax.ppermute(value, 'c', [(0, 1), (1, 0)])  5.82 us
    pallas_call x1, Pallas kernels, gather_of(): pl.pallas_call(gather_kernel, out_shape=jax.ShapeDtypeStruct((groups, tok...  5.74 us
    ppermute x3, waiting for transfers between devices, from_all_groups(): lax.ppermute(value, 'z', [(i, (i + d) % size) for i in range(size)])  4.22 us
  transfers between devices with their start and end apart: 10, of which 3 were waited for; matrix products, arithmetic and copies ran while one was open for 0% of the time, Pallas kernels for 41%

profile of v2, /device:TPU:1, one launch (start us, length us, event | category | flops | bytes accessed | tf_op | source)
XLA Modules:
  0.0 201.6 jit_solution(11198652573097255544)
XLA Ops:
  6.5 0.0 copy-start.11
  6.5 0.0 all-gather.3.cloned.1.call-start
  6.5 4.6 %shard_map.56 = f32[16,72,128]{2,1,0:T(8,128)} custom-call(s32[1]{0:T(128)S(6)} %sub.3.side_ref, s32[8,1024]{1,0:T(8,128)} %bitcast.6, bf16[1024,1024]{1,0:T(8,128)(2,1)} %q_ref.3), custom_call_target="tpu_custom_call" | custom-call | tf_op jit(solution)/shard_map/pallas_call | solution.py:89
  11.2 1.5 collective-permute-start
  12.7 0.0 copy-done.11
  12.7 1.3 collective-permute-start.1
  14.0 0.0 copy-start.1
  14.0 66.4 %shard_map.55 = (f32[16,72,128]{2,1,0:T(8,128)}, bf16[1024,512]{1,0:T(8,128)(2,1)}, bf16[1024,512]{1,0:T(8,128)(2,1)}) custom-call(s32[1]{0:T(128)} %bitcast.side_ref, s32[8,1024]{1,0:T(8,128)} %bitcast.7, bf16[1024,1024]{1,0:T(8,128)(2,1)} %q_ref.3, bf16[1024,1024]{1,0:T(8,128)(2,1)} %rest_4_.1, bf16[1024,1024]{1,0:T(8,128)(2,1)} %rest_6_.1), custom_call_target="tpu_custom_call" | custom-call | tf_op jit(solution)/shard_map/pallas_call | solution.py:89
  80.4 0.0 collective-permute-done.1.passed_ref
  80.4 0.0 collective-permute-done.b_ref
  80.4 0.0 copy-start
  80.4 1.1 copy-done
  81.5 0.1 shard_map.57
  81.5 0.0 all-gather.3.cloned.1.call-update
  81.6 0.1 collective-permute-start.5
  81.7 0.5 collective-permute-start.6
  82.2 24.2 %all_to_all.20.in_ref = f32[16,72,128]{2,1,0:T(8,128)S(1)} all-to-all(f32[16,72,128]{2,1,0:T(8,128)S(1)} %get-tuple-element.15), channel_id=1, replica_groups=mesh['x'=4,'y'=4,'c'=2,'z'=4] {'x','y'}, dimensions={0} | all-to-all | bytes 1179648 | tf_op jit(solution)/shard_map/all_to_all | solution.py:341
  106.3 0.0 copy-done.1
  106.3 0.8 shard_map.58
  107.2 0.0 copy-start.2
  107.2 3.5 %all-to-all-start.1 = ((bf16[16,64,128]{2,1,0:T(8,128)(2,1)}), bf16[16,64,128]{2,1,0:T(8,128)(2,1)S(1)}, u32[]{:S(2)}, u32[]{:S(2)}) async-start(bf16[16,64,128]{2,1,0:T(8,128)(2,1)} %get-tuple-element.16), calls=%async_computation.1 | async-start | bytes 524288 | tf_op jit(solution)/shard_map/all_to_all | solution.py:341
  110.7 0.1 collective-permute-start.4
  110.8 2.8 %collective-permute-start.3 = (s32[8,1024]{1,0:T(8,128)S(1)}, s32[8,1024]{1,0:T(8,128)S(1)}, u32[]{:S(2)}, u32[]{:S(2)}) collective-permute-start(s32[8,1024]{1,0:T(8,128)S(1)} %get-tuple-element.17.rest_0_), channel_id=1, source_target_pairs={{0,2},{1,3},{2,0},{3,1},{4,6},{5,7},{6,4},{7,5},{8,10},{9,11},{10,... | collective-permute-start | bytes 98312 | tf_op jit(solution)/shard_map/ppermute | solution.py:348
  113.6 0.0 collective-permute-start.2
  113.6 0.0 collective-permute-done.5.rest_5_
  113.6 0.0 copy-start.5
  113.6 0.0 collective-permute-done.6.rest_7_
  113.6 0.0 copy-start.6
  113.6 0.0 collective-permute-done.4.rest_3_
  113.6 0.0 copy-start.8
  113.6 1.5 collective-permute-done.3.rest_2_
  115.2 0.0 copy-start.9
  115.2 2.7 %collective-permute-done.2.rest_1_ = s32[8,1024]{1,0:T(8,128)S(1)} collective-permute-done((s32[8,1024]{1,0:T(8,128)S(1)}, s32[8,1024]{1,0:T(8,128)S(1)}, u32[]{:S(2)}, u32[]{:S(2)}) %collective-permute-start.2) | collective-permute-done | bytes 32800 | tf_op jit(solution)/shard_map/ppermute | solution.py:348
  117.8 0.0 copy-start.10
  117.8 0.2 all-to-all-done.1
  118.1 0.0 copy-start.7
  118.1 0.0 copy-done.2
  118.1 0.0 copy-done.5
  118.1 0.0 copy-done.6
  118.1 0.0 copy-done.8
  118.1 0.0 copy-done.9
  118.1 0.3 copy-done.10
  118.4 0.3 copy-done.7
  118.8 8.7 %shard_map.59 = (bf16[16,80,128]{2,1,0:T(8,128)(2,1)}, s32[4,8,1024]{2,1,0:T(8,128)}) custom-call(s32[1]{0:T(128)} %bitcast.side_ref, bf16[4,256,128]{2,1,0:T(8,128)(2,1)} %bitcast.12, s32[8,1024]{1,0:T(8,128)} %copy-done.2, s32[8,1024]{1,0:T(8,128)} %copy-done.10, s32[8,1024]{1,0:T(8,128)} %copy-done.9, s32[8,1024]{1,0:T(8,128)} %copy-done.8, ...), custom_call_target="tpu_custom_call" | custom-call | tf_op jit(solution)/shard_map/pallas_call | solution.py:206
  127.5 14.4 %all_to_all.21.in_ref = bf16[16,80,128]{2,1,0:T(8,128)(2,1)S(1)} all-to-all(bf16[16,80,128]{2,1,0:T(8,128)(2,1)} %get-tuple-element.21), channel_id=1, replica_groups=mesh['x'=4,'y'=4,'c'=2,'z'=4] {'x','y'}, dimensions={0} | all-to-all | bytes 655360 | tf_op jit(solution)/shard_map/all_to_all | solution.py:341
  141.9 0.4 shard_map.60
  142.3 23.0 %all_to_all.22 = bf16[64,64,128]{2,1,0:T(8,128)(2,1)S(1)} all-to-all(bf16[64,64,128]{2,1,0:T(8,128)(2,1)S(1)} %shard_map.60), channel_id=1, replica_groups=mesh['x'=4,'y'=4,'c'=2,'z'=4] {'z','x','y'}, dimensions={0} | all-to-all | bytes 2097152 | tf_op jit(solution)/shard_map/all_to_all | solution.py:341
  165.3 0.0 copy-start.3
  165.3 3.7 %collective-permute-start.7 = (bf16[16,256,128]{2,1,0:T(8,128)(2,1)S(1)}, bf16[16,256,128]{2,1,0:T(8,128)(2,1)S(1)}, u32[]{:S(2)}, u32[]{:S(2)}) collective-permute-start(bf16[16,256,128]{2,1,0:T(8,128)(2,1)S(1)} %bitcast.10), channel_id=1, source_target_pairs={{0,4},{4,0},{1,5},{5,1},{2,6},{6,2},{3,7},{7,3},{8,12},{12,8},{9,1... | collective-permute-start | bytes 3145736 | tf_op jit(solution)/shard_map/ppermute | solution.py:337
  169.0 0.7 pad_add_fusion.place_ref
  169.7 0.0 copy-done.3
  169.7 5.7 %shard_map.61.near_ref = bf16[4,1024,512]{2,1,0:T(8,128)(2,1)} custom-call(s32[2]{0:T(128)} %pad_add_fusion.place_ref, s32[4,8,1024]{2,1,0:T(8,128)} %get-tuple-element.20.ids_ref, bf16[16,256,128]{2,1,0:T(8,128)(2,1)} %bitcast.11), custom_call_target="tpu_custom_call" | custom-call | tf_op jit(solution)/shard_map/pallas_call | solution.py:258
  175.4 0.0 collective-permute-done.7.table_ref
  175.4 0.0 copy-start.4
  175.4 0.0 all-gather.3.cloned.1.call-done
  175.4 1.0 copy-done.4
  176.4 18.3 %shard_map.62 = bf16[1024,1024]{1,0:T(8,128)(2,1)} custom-call(s32[2]{0:T(128)} %pad_add_fusion.place_ref, bf16[4,1024,512]{2,1,0:T(8,128)(2,1)} %shard_map.61.near_ref, s32[4,8,1024]{2,1,0:T(8,128)} %get-tuple-element.20.ids_ref, bf16[16,256,128]{2,1,0:T(8,128)(2,1)} %copy-done.4, bf16[4,8,1024,128]{3,2,1,0:T(8,128)(2,1)} %bitcast.9), custom_call_target="tpu_custom_call" | custom-call | tf_op jit(solution)/shard_map/pallas_call | solution.py:319
Async XLA Ops:
  6.5 6.2 %copy-start.11 = (bf16[1024,128]{1,0:T(8,128)(2,1)S(1)}, bf16[1024,128]{1,0:T(8,128)(2,1)}, u32[]{:S(2)}) copy-start(bf16[1024,128]{1,0:T(8,128)(2,1)} %param.9) | copy-start | bytes 786436
  6.5 168.9 %all-gather.3.cloned.1.call-start = ((), (), s32[]{:S(2)}) async-start(), calls=%async_computation.4 | async-start | bytes 8650752 | tf_op jit(solution)/shard_map/all_gather | solution.py:368
  11.2 69.2 %collective-permute-start = (f32[16,72,128]{2,1,0:T(8,128)}, f32[16,72,128]{2,1,0:T(8,128)S(1)}, u32[]{:S(2)}, u32[]{:S(2)}) collective-permute-start(f32[16,72,128]{2,1,0:T(8,128)} %shard_map.56), channel_id=1, source_target_pairs={{0,4},{4,0},{1,5},{5,1},{2,6},{6,2},{3,7},{7,3},{8,12},{12,8},{9,1... | collective-permute-start | bytes 1769480 | tf_op jit(solution)/shard_map/ppermute | solution.py:337
  12.7 67.7 %collective-permute-start.1 = (bf16[1024,128]{1,0:T(8,128)(2,1)S(1)}, bf16[1024,128]{1,0:T(8,128)(2,1)}, u32[]{:S(2)}, u32[]{:S(2)}) collective-permute-start(bf16[1024,128]{1,0:T(8,128)(2,1)S(1)} %copy-done.11), channel_id=1, source_target_pairs={{0,0},{1,96},{2,64},{3,32},{32,65},{33,33},{34,1},{35,97},{64,2},{... | collective-permute-start | bytes 786440 | tf_op jit(solution)/shard_map/ppermute | solution.py:361
  14.0 92.3 %copy-start.1 = (s32[1024,8]{0,1:T(8,128)S(1)}, s32[1024,8]{0,1:T(8,128)}, u32[]{:S(2)}) copy-start(s32[1024,8]{0,1:T(8,128)} %param.8) | copy-start | bytes 98308
  80.4 1.1 copy-start
  81.6 32.0 %collective-permute-start.5 = (bf16[1024,512]{1,0:T(8,128)(2,1)}, bf16[1024,512]{1,0:T(8,128)(2,1)S(1)}, u32[]{:S(2)}, u32[]{:S(2)}) collective-permute-start(bf16[1024,512]{1,0:T(8,128)(2,1)} %get-tuple-element.18), channel_id=1, source_target_pairs={{0,4},{4,0},{1,5},{5,1},{2,6},{6,2},{3,7},{7,3},{8,12},{12,8},{9,1... | collective-permute-start | bytes 3145736 | tf_op jit(solution)/shard_map/ppermute | solution.py:337
  81.7 31.9 %collective-permute-start.6 = (bf16[1024,512]{1,0:T(8,128)(2,1)}, bf16[1024,512]{1,0:T(8,128)(2,1)S(1)}, u32[]{:S(2)}, u32[]{:S(2)}) collective-permute-start(bf16[1024,512]{1,0:T(8,128)(2,1)} %get-tuple-element.19), channel_id=1, source_target_pairs={{0,4},{4,0},{1,5},{5,1},{2,6},{6,2},{3,7},{7,3},{8,12},{12,8},{9,1... | collective-permute-start | bytes 3145736 | tf_op jit(solution)/shard_map/ppermute | solution.py:337
  107.2 10.9 %copy-start.2 = (s32[8,1024]{1,0:T(8,128)}, s32[8,1024]{1,0:T(8,128)S(1)}, u32[]{:S(2)}) copy-start(s32[8,1024]{1,0:T(8,128)S(1)} %get-tuple-element.17.rest_0_) | copy-start | bytes 98308
  107.2 10.9 %all-to-all-start.1 = ((bf16[16,64,128]{2,1,0:T(8,128)(2,1)}), bf16[16,64,128]{2,1,0:T(8,128)(2,1)S(1)}, u32[]{:S(2)}, u32[]{:S(2)}) async-start(bf16[16,64,128]{2,1,0:T(8,128)(2,1)} %get-tuple-element.16), calls=%async_computation.1 | async-start | bytes 524288 | tf_op jit(solution)/shard_map/all_to_all | solution.py:341
  110.7 2.9 %collective-permute-start.4 = (s32[8,1024]{1,0:T(8,128)S(1)}, s32[8,1024]{1,0:T(8,128)S(1)}, u32[]{:S(2)}, u32[]{:S(2)}) collective-permute-start(s32[8,1024]{1,0:T(8,128)S(1)} %get-tuple-element.17.rest_0_), channel_id=1, source_target_pairs={{0,3},{1,0},{2,1},{3,2},{4,7},{5,4},{6,5},{7,6},{8,11},{9,8},{10,9... | collective-permute-start | bytes 98312 | tf_op jit(solution)/shard_map/ppermute | solution.py:348
  110.8 4.3 %collective-permute-start.3 = (s32[8,1024]{1,0:T(8,128)S(1)}, s32[8,1024]{1,0:T(8,128)S(1)}, u32[]{:S(2)}, u32[]{:S(2)}) collective-permute-start(s32[8,1024]{1,0:T(8,128)S(1)} %get-tuple-element.17.rest_0_), channel_id=1, source_target_pairs={{0,2},{1,3},{2,0},{3,1},{4,6},{5,7},{6,4},{7,5},{8,10},{9,11},{10,... | collective-permute-start | bytes 98312 | tf_op jit(solution)/shard_map/ppermute | solution.py:348
  113.6 4.3 %collective-permute-start.2 = (s32[8,1024]{1,0:T(8,128)S(1)}, s32[8,1024]{1,0:T(8,128)S(1)}, u32[]{:S(2)}, u32[]{:S(2)}) collective-permute-start(s32[8,1024]{1,0:T(8,128)S(1)} %get-tuple-element.17.rest_0_), channel_id=1, source_target_pairs={{0,1},{1,2},{2,3},{3,0},{4,5},{5,6},{6,7},{7,4},{8,9},{9,10},{10,1... | collective-permute-start | bytes 98312 | tf_op jit(solution)/shard_map/ppermute | solution.py:348
  113.6 4.5 %copy-start.5 = (bf16[1024,512]{1,0:T(8,128)(2,1)}, bf16[1024,512]{1,0:T(8,128)(2,1)S(1)}, u32[]{:S(2)}) copy-start(bf16[1024,512]{1,0:T(8,128)(2,1)S(1)} %collective-permute-done.5.rest_5_) | copy-start | bytes 3145732
  113.6 4.5 %copy-start.6 = (bf16[1024,512]{1,0:T(8,128)(2,1)}, bf16[1024,512]{1,0:T(8,128)(2,1)S(1)}, u32[]{:S(2)}) copy-start(bf16[1024,512]{1,0:T(8,128)(2,1)S(1)} %collective-permute-done.6.rest_7_) | copy-start | bytes 3145732
  113.6 4.5 %copy-start.8 = (s32[8,1024]{1,0:T(8,128)}, s32[8,1024]{1,0:T(8,128)S(1)}, u32[]{:S(2)}) copy-start(s32[8,1024]{1,0:T(8,128)S(1)} %collective-permute-done.4.rest_3_) | copy-start | bytes 98308
  115.2 2.9 %copy-start.9 = (s32[8,1024]{1,0:T(8,128)}, s32[8,1024]{1,0:T(8,128)S(1)}, u32[]{:S(2)}) copy-start(s32[8,1024]{1,0:T(8,128)S(1)} %collective-permute-done.3.rest_2_) | copy-start | bytes 98308
  117.8 0.6 copy-start.10
  118.1 0.7 copy-start.7
  165.3 4.4 %copy-start.3 = (bf16[64,64,128]{2,1,0:T(8,128)(2,1)}, bf16[64,64,128]{2,1,0:T(8,128)(2,1)S(1)}, u32[]{:S(2)}) copy-start(bf16[64,64,128]{2,1,0:T(8,128)(2,1)S(1)} %all_to_all.22) | copy-start | bytes 3145732
  165.3 10.1 %collective-permute-start.7 = (bf16[16,256,128]{2,1,0:T(8,128)(2,1)S(1)}, bf16[16,256,128]{2,1,0:T(8,128)(2,1)S(1)}, u32[]{:S(2)}, u32[]{:S(2)}) collective-permute-start(bf16[16,256,128]{2,1,0:T(8,128)(2,1)S(1)} %bitcast.10), channel_id=1, source_target_pairs={{0,4},{4,0},{1,5},{5,1},{2,6},{6,2},{3,7},{7,3},{8,12},{12,8},{9,1... | collective-permute-start | bytes 3145736 | tf_op jit(solution)/shard_map/ppermute | solution.py:337
  175.4 1.0 copy-start.4
Sparse Core Ops, SparseCore 0:
  81.7 59.2 all-gather.2

commit v3 on v2

--- a/solution.py
+++ b/solution.py
@@ -41,41 +41,35 @@
     return (labels == row).astype(F32).astype(BF16)
 
 
-def totals_kernel(halves, side_ref, ids_ref, q_ref, *rest):
-    sources, out_ref, copies = rest[:halves], rest[halves], rest[halves + 1 : 2 * halves + 1]
-    held, arrived, copied = rest[2 * halves + 1 :]
+def totals_kernel(side_ref, ids_ref, q_ref, theirs_ref, mine_ref, held, arrived):
     rows = q_ref.shape[0]
-    first = side_ref[0] * HALF
-
-    def fetch(i):
-        start = pl.multiple_of((first + i) * HDIM, HDIM)
-        return pltpu.make_async_copy(q_ref.at[:, pl.ds(start, HDIM)], held.at[i], arrived.at[i])
-
-    def copy(k):
-        start = pl.multiple_of((HALF - first) * HDIM, HALF * HDIM)
+    firsts = (HALF - side_ref[0] * HALF, side_ref[0] * HALF)
+
+    def fetch(k):
+        start = pl.multiple_of(firsts[k] * HDIM, HALF * HDIM)
         return pltpu.make_async_copy(
-            sources[k].at[:, pl.ds(start, HALF * HDIM)], copies[k], copied.at[k]
+            q_ref.at[:, pl.ds(start, HALF * HDIM)], held.at[k], arrived.at[k]
         )
 
-    for i in range(HALF):
-        fetch(i).start()
-    for k in range(halves):
-        copy(k).start()
+    for k in range(2):
+        fetch(k).start()
     ones = jnp.ones((rows, HDIM), BF16)
     diagonal = eye(QUARTER, HDIM)
-    for i in range(HALF):
-        member = member_of(ids_ref[pl.ds(first + i, 1), :])
-        fetch(i).wait()
-        both = jnp.dot(
-            member, jnp.concatenate([held[i], ones], axis=1), preferred_element_type=F32
-        )
-        for k in range(4):
-            lines = slice(k * QUARTER, (k + 1) * QUARTER)
-            count = jnp.sum(jnp.where(diagonal, both[lines, HDIM:], 0.0), axis=0, keepdims=True)
-            out_ref[i * 4 + k, :QUARTER, :] = both[lines, :HDIM]
-            out_ref[i * 4 + k, QUARTER:, :] = jnp.broadcast_to(count, (EXTRA, HDIM))
-    for k in range(halves):
-        copy(k).wait()
+    for k, out_ref in enumerate((theirs_ref, mine_ref)):
+        fetch(k).wait()
+        for i in range(HALF):
+            member = member_of(ids_ref[pl.ds(firsts[k] + i, 1), :])
+            query = held[k, :, i * HDIM : (i + 1) * HDIM]
+            both = jnp.dot(
+                member, jnp.concatenate([query, ones], axis=1), preferred_element_type=F32
+            )
+            for q in range(4):
+                lines = slice(q * QUARTER, (q + 1) * QUARTER)
+                count = jnp.sum(
+                    jnp.where(diagonal, both[lines, HDIM:], 0.0), axis=0, keepdims=True
+                )
+                out_ref[i * 4 + q, :QUARTER, :] = both[lines, :HDIM]
+                out_ref[i * 4 + q, QUARTER:, :] = jnp.broadcast_to(count, (EXTRA, HDIM))
 
 
 SCALARS = pl.BlockSpec(memory_space=pltpu.SMEM)
@@ -83,22 +77,57 @@
 IN_HBM = pl.BlockSpec(memory_space=pltpu.HBM)
 
 
-def totals_of(side, ids, queries, split=()):
+def totals_of(side, ids, queries):
     rows = queries.shape[0]
-    halves = len(split)
-    return pl.pallas_call(
-        functools.partial(totals_kernel, halves),
-        out_shape=[jax.ShapeDtypeStruct((4 * HALF, QUARTER + EXTRA, HDIM), F32)]
-        + [jax.ShapeDtypeStruct((rows, HALF * HDIM), BF16)] * halves,
-        in_specs=[SCALARS, IN_VMEM, IN_HBM] + [IN_HBM] * halves,
-        out_specs=[IN_VMEM] + [IN_HBM] * halves,
+    return pl.pallas_call(
+        totals_kernel,
+        out_shape=[jax.ShapeDtypeStruct((4 * HALF, QUARTER + EXTRA, HDIM), F32)] * 2,
+        in_specs=[SCALARS, IN_VMEM, IN_HBM],
+        out_specs=[IN_VMEM] * 2,
         scratch_shapes=[
-            pltpu.VMEM((HALF, rows, HDIM), BF16),
-            pltpu.SemaphoreType.DMA((HALF,)),
-            pltpu.SemaphoreType.DMA((max(halves, 1),)),
+            pltpu.VMEM((2, rows, HALF * HDIM), BF16),
+            pltpu.SemaphoreType.DMA((2,)),
         ],
         compiler_params=params(LARGE),
-    )(side, ids, queries, *split)
+    )(side, ids, queries)
+
+
+def halves_kernel(side_ref, after_ref, k_ref, v_ref, k_out_ref, v_out_ref, held, come, gone):
+    del after_ref
+    start = pl.multiple_of((1 - side_ref[0]) * HALF * HDIM, HALF * HDIM)
+
+    def fetch(k, source):
+        return pltpu.make_async_copy(
+            source.at[:, pl.ds(start, HALF * HDIM)], held.at[k], come.at[k]
+        )
+
+    def put(k, target):
+        return pltpu.make_async_copy(held.at[k], target, gone.at[k])
+
+    fetch(0, k_ref).start()
+    fetch(1, v_ref).start()
+    fetch(0, k_ref).wait()
+    put(0, k_out_ref).start()
+    fetch(1, v_ref).wait()
+    put(1, v_out_ref).start()
+    put(0, k_out_ref).wait()
+    put(1, v_out_ref).wait()
+
+
+def halves_of(side, after, keys, values):
+    half = jax.ShapeDtypeStruct((keys.shape[0], HALF * HDIM), BF16)
+    return pl.pallas_call(
+        halves_kernel,
+        out_shape=(half, half),
+        in_specs=[SCALARS, IN_HBM, IN_HBM, IN_HBM],
+        out_specs=(IN_HBM, IN_HBM),
+        scratch_shapes=[
+            pltpu.VMEM((2, *half.shape), BF16),
+            pltpu.SemaphoreType.DMA((2,)),
+            pltpu.SemaphoreType.DMA((2,)),
+        ],
+        compiler_params=params(LARGE),
+    )(side, after, keys, values)
 
 
 def add_kernel(a_ref, b_ref, passed_ref, out_ref, handed_ref):
@@ -148,39 +177,42 @@
     out_ref, ids_out_ref, held, arrived, copied = rest[groups + 4 :]
     first = side_ref[0] * HALF
 
-    def fetch(i):
-        for k in range(4):
-            start = i * HDIM if k % 2 else pl.multiple_of((first + i) * HDIM, HDIM)
-            yield pltpu.make_async_copy(
-                sources[k].at[:, pl.ds(start, HDIM)], held.at[i, k], arrived.at[i, k]
-            )
-
-    for i in range(HALF):
-        for copy in fetch(i):
-            copy.start()
+    def fetch(k):
+        source = sources[k]
+        if k % 2 == 0:
+            source = source.at[:, pl.ds(pl.multiple_of(first * HDIM, HALF * HDIM), HALF * HDIM)]
+        return pltpu.make_async_copy(source, held.at[k], arrived.at[k])
+
+    for k in range(4):
+        fetch(k).start()
     copies = [
         pltpu.make_async_copy(ids_refs[d], ids_out_ref.at[d], copied.at[d]) for d in range(groups)
     ]
     for copy in copies:
         copy.start()
-    ones = jnp.ones(held.shape[2:], BF16)
+    ones = jnp.ones((held.shape[1], HDIM), BF16)
     diagonal = eye(QUARTER, HDIM)
     line = lax.broadcasted_iota(jnp.int32, (TAIL, HDIM), 0)
     for i in range(HALF):
-        for copy in fetch(i):
-            copy.wait()
+        if i == 0:
+            fetch(0).wait()
+            fetch(1).wait()
+        cols = slice(i * HDIM, (i + 1) * HDIM)
         centre = centre_ref[i]
-        own = lax.dot_general(centre, held[i, 0], NT, preferred_element_type=F32)
-        other = lax.dot_general(centre, held[i, 1], NT, preferred_element_type=F32)
+        own = lax.dot_general(centre, held[0, :, cols], NT, preferred_element_type=F32)
+        other = lax.dot_general(centre, held[1, :, cols], NT, preferred_element_type=F32)
         peak = jnp.maximum(
             jnp.max(own, axis=1, keepdims=True), jnp.max(other, axis=1, keepdims=True)
         )
         own_w = jnp.exp2((own - peak) * LOG2_SCALE).astype(BF16)
         other_w = jnp.exp2((other - peak) * LOG2_SCALE).astype(BF16)
+        if i == 0:
+            fetch(2).wait()
+            fetch(3).wait()
         both = jnp.dot(
-            own_w, jnp.concatenate([held[i, 2], ones], axis=1), preferred_element_type=F32
+            own_w, jnp.concatenate([held[2, :, cols], ones], axis=1), preferred_element_type=F32
         ) + jnp.dot(
-            other_w, jnp.concatenate([held[i, 3], ones], axis=1), preferred_element_type=F32
+            other_w, jnp.concatenate([held[3, :, cols], ones], axis=1), preferred_element_type=F32
         )
         mass = both[:, HDIM:]
         part = (both[:, :HDIM] / mass).astype(BF16)
@@ -212,8 +244,8 @@
         in_specs=[SCALARS, IN_VMEM] + [IN_HBM] * groups + [IN_HBM] * 4,
         out_specs=(IN_VMEM, IN_VMEM),
         scratch_shapes=[
-            pltpu.VMEM((HALF, 4, rows, HDIM), BF16),
-            pltpu.SemaphoreType.DMA((HALF, 4)),
+            pltpu.VMEM((4, rows, HALF * HDIM), BF16),
+            pltpu.SemaphoreType.DMA((4,)),
             pltpu.SemaphoreType.DMA((groups,)),
         ],
         compiler_params=params(LARGE),
@@ -242,39 +274,52 @@
     return lax.dot_general(member_of(ids_row), table, TN, preferred_element_type=F32).astype(BF16)
 
 
-def group_at(i, place_ref, groups):
-    return lax.rem(place_ref[1] + groups - i, groups)
-
-
-def gather_kernel(place_ref, ids_ref, table_ref, out_ref):
-    group = group_at(pl.program_id(0), place_ref, pl.num_programs(0))
+def group_at(i, z_ref, groups):
+    return lax.rem(z_ref[0] + groups - i, groups)
+
+
+def gather_kernel(side_ref, z_ref, ids_ref, table_ref, after_ref, out_ref):
+    del after_ref
+    group = group_at(pl.program_id(0), z_ref, pl.num_programs(0))
     for j in range(HALF):
-        row = ids_ref[pl.program_id(0), pl.ds(place_ref[0] * HALF + j, 1), :]
+        row = ids_ref[pl.program_id(0), pl.ds(side_ref[0] * HALF + j, 1), :]
         out_ref[:, j * HDIM : (j + 1) * HDIM] = rows_of(row, table_ref[group * HALF + j])
 
 
-def gather_of(place, ids, table):
+def gather_of(side, z, ids, table, after):
     groups, lines, tokens = ids.shape
     return pl.pallas_call(
         gather_kernel,
         out_shape=jax.ShapeDtypeStruct((groups, tokens, HALF * HDIM), BF16),
         grid=(groups,),
-        in_specs=[SCALARS, IN_VMEM, IN_VMEM],
+        in_specs=[SCALARS, SCALARS, IN_VMEM, IN_VMEM, IN_HBM],
         out_specs=pl.BlockSpec((None, tokens, HALF * HDIM), lambda i: (i, 0, 0)),
-        compiler_params=params(LARGE),
-    )(place, ids, table)
+        compiler_params=params(24),
+    )(side, z, ids, table, after)
 
 
 def project_kernel(
-    place_ref, near_ref, ids_ref, table_ref, w_ref, out_ref, held, near, far, acc, arrived, come
+    side_ref,
+    z_ref,
+    near_ref,
+    ids_ref,
+    table_ref,
+    w_ref,
+    out_ref,
+    held,
+    near,
+    far,
+    acc,
+    arrived,
+    come,
 ):
     groups, blocks = w_ref.shape[:2]
     depth = HALF * HDIM
 
     def fetch(i):
-        group = group_at(lax.rem(i, groups), place_ref, groups)
-        entry = lax.rem(2 * place_ref[1] + groups - group, groups)
-        side = jnp.where(i < groups, place_ref[0], 1 - place_ref[0])
+        group = group_at(lax.rem(i, groups), z_ref, groups)
+        entry = lax.rem(2 * z_ref[0] + groups - group, groups)
+        side = jnp.where(i < groups, side_ref[0], 1 - side_ref[0])
         lines = pl.ds(pl.multiple_of(side * depth, depth), depth)
         return pltpu.make_async_copy(w_ref.at[entry, :, lines, :], held.at[i], arrived.at[i])
 
@@ -301,9 +346,9 @@
 
     @pl.loop(groups, 2 * groups)
     def _(i):
-        group = group_at(i - groups, place_ref, groups)
+        group = group_at(i - groups, z_ref, groups)
         for j in range(HALF):
-            row = ids_ref[i - groups, pl.ds((1 - place_ref[0]) * HALF + j, 1), :]
+            row = ids_ref[i - groups, pl.ds((1 - side_ref[0]) * HALF + j, 1), :]
             far[:, j * HDIM : (j + 1) * HDIM] = rows_of(row, table_ref[group * HALF + j])
         fetch(i).wait()
         acc[...] += jnp.dot(far[...], weight(i), preferred_element_type=F32)
@@ -311,7 +356,7 @@
     out_ref[...] = acc[...].astype(BF16)
 
 
-def project_of(place, near, ids, table, weight):
+def project_of(side, z, near, ids, table, weight):
     groups, lines, tokens = ids.shape
     depth = HALF * HDIM
     blocks, width = weight.shape[1], weight.shape[3]
@@ -319,7 +364,7 @@
     return pl.pallas_call(
         project_kernel,
         out_shape=jax.ShapeDtypeStruct((tokens, cols), BF16),
-        in_specs=[SCALARS, IN_HBM, IN_VMEM, IN_VMEM, IN_HBM],
+        in_specs=[SCALARS, SCALARS, IN_HBM, IN_VMEM, IN_VMEM, IN_HBM],
         out_specs=IN_VMEM,
         scratch_shapes=[
             pltpu.VMEM((2 * groups, blocks, depth, width), BF16),
@@ -329,8 +374,8 @@
             pltpu.SemaphoreType.DMA((2 * groups,)),
             pltpu.SemaphoreType.DMA((groups,)),
         ],
-        compiler_params=params(56),
-    )(place, near, ids, table, weight)
+        compiler_params=params(40),
+    )(side, z, near, ids, table, weight)
 
 
 def other_core(value):
@@ -352,7 +397,7 @@
 def local(queries, keys, values, cluster_ids, out_weight):
     core = lax.axis_index("c").astype(jnp.int32)
     side = core[None]
-    place = jnp.stack([core, lax.axis_index("z").astype(jnp.int32)])
+    z = lax.axis_index("z").astype(jnp.int32)[None]
     ids = cluster_ids.T
     size = lax.axis_size("z")
     turned = [
@@ -360,9 +405,9 @@
     ]
     turned_weight = lax.ppermute(out_weight, ("x", "z"), turned)
 
-    (theirs,) = totals_of(1 - side, ids, queries)
+    theirs, mine = totals_of(side, ids, queries)
     arrived = other_core(theirs)
-    mine, keys_far, values_far = totals_of(side, ids, queries, (keys, values))
+    keys_far, values_far = halves_of(side, theirs, keys, values)
     keys_other, values_other = other_core(keys_far), other_core(values_far)
     totals, turned_weight = add_after(mine, arrived, turned_weight)
     weight = lax.all_gather(turned_weight, SEQ, axis=0)
@@ -382,8 +427,8 @@
     )(parts)
     table = exchanged(table, CUBE).reshape(size * HALF, CLUSTERS, HDIM)
     far_table = other_core(table)
-    near = gather_of(place, all_ids, table)
-    return project_of(place, near, all_ids, far_table, weight)
+    near = gather_of(side, z, all_ids, table, weight[0, 0, :16])
+    return project_of(side, z, near, all_ids, far_table, weight)
 
 
 def solution(mesh):

time: 202 us -> 144 us (0.71)
  Pallas kernels: 105 us -> 33.9 us
  blocking collectives: 61.5 us -> 70.7 us
  local copies, waits for them, and re-layouts: 2.76 us -> 5.82 us
    pallas_call x2, Pallas kernels: 71 us -> 6.96 us  [the longest x1 4.3 us: totals_of(): pl.pallas_call(totals_kernel, out_shape=[jax.ShapeDtypeStruct((4 * HALF,...]
    all_to_all x3, blocking collectives: 61.5 us -> 70.7 us  [exchanged(): return lax.all_to_all(value, axes, split_axis=0, concat_axis=0, tiled=True)]
    pallas_call x1, Pallas kernels: 5.74 us -> 3.11 us  [gather_of(): pl.pallas_call(gather_kernel, out_shape=jax.ShapeDtypeStruct((groups, tok...]
    pallas_call x1, Pallas kernels: 18.3 us -> 15.7 us  [project_of(): pl.pallas_call(project_kernel, out_shape=jax.ShapeDtypeStruct((tokens, co...]
    unnamed x24, local copies, waits for them, and re-layouts: 2.76 us -> 5.13 us
  transfers between devices with their start and end apart: 10 -> 10, of which waited for: 3 -> 3; matrix products, arithmetic and copies ran while one was open for 0% -> 0% of each run, Pallas kernels for 41% -> 10%
where the time goes in v3:
time: 144 us; the launch traced here: 143 us
  blocking collectives  70.7 us (49%)
  Pallas kernels  33.9 us (24%)
  starting transfers between devices  14.4 us (10%)
  between operations  13.6 us (9%)
  local copies, waits for them, and re-layouts  5.82 us (4%)
  waiting for transfers between devices  4.71 us (3%)
    all_to_all x3, blocking collectives, exchanged(): return lax.all_to_all(value, axes, split_axis=0, concat_axis=0, tiled=True)  70.7 us
    pallas_call x1, Pallas kernels, project_of(): pl.pallas_call(project_kernel, out_shape=jax.ShapeDtypeStruct((tokens, co...  15.7 us
    pallas_call x1, Pallas kernels, attention_of(): pl.pallas_call(functools.partial(attention_kernel, groups), out_shape=(ja...  6.92 us
    ppermute x4, starting transfers between devices, other_core(): return lax.ppermute(value, 'c', [(0, 1), (1, 0)])  5.89 us
    unnamed x24, local copies, waits for them, and re-layouts  5.13 us
    pallas_call x1, Pallas kernels, totals_of(): pl.pallas_call(totals_kernel, out_shape=[jax.ShapeDtypeStruct((4 * HALF,...  4.3 us
    ppermute x3, waiting for transfers between devices, from_all_groups(): lax.ppermute(value, 'z', [(i, (i + d) % size) for i in range(size)])  4.22 us
    ppermute x3, starting transfers between devices, from_all_groups(): lax.ppermute(value, 'z', [(i, (i + d) % size) for i in range(size)])  3.65 us
  transfers between devices with their start and end apart: 10, of which 3 were waited for; matrix products, arithmetic and copies ran while one was open for 0% of the time, Pallas kernels for 10%

profile of v3, /device:TPU:1, one launch (start us, length us, event | category | flops | bytes accessed | tf_op | source)
XLA Modules:
  0.0 143.1 jit_solution(1442423259752740117)
XLA Ops:
  6.5 0.0 copy-start.11
  6.5 0.0 all-gather.3.cloned.1.call-start
  6.5 4.3 %shard_map.55 = (f32[16,72,128]{2,1,0:T(8,128)}, f32[16,72,128]{2,1,0:T(8,128)}) custom-call(s32[1]{0:T(128)} %bitcast.side_ref, s32[8,1024]{1,0:T(8,128)} %bitcast.12, bf16[1024,1024]{1,0:T(8,128)(2,1)} %q_ref.1), custom_call_target="tpu_custom_call" | custom-call | tf_op jit(solution)/shard_map/pallas_call | solution.py:82
  10.8 1.5 %collective-permute-start = (f32[16,72,128]{2,1,0:T(8,128)}, f32[16,72,128]{2,1,0:T(8,128)S(1)}, u32[]{:S(2)}, u32[]{:S(2)}) collective-permute-start(f32[16,72,128]{2,1,0:T(8,128)} %get-tuple-element.16.after_ref), channel_id=1, source_target_pairs={{0,4},{4,0},{1,5},{5,1},{2,6},{6,2},{3,7},{7,3},{8,12},{12,8},{9,1... | collective-permute-start | bytes 1769480 | tf_op jit(solution)/shard_map/ppermute | solution.py:382
  12.3 0.0 copy-done.11
  12.3 1.4 collective-permute-start.1
  13.7 0.0 collective-permute-done.1.passed_ref
  13.7 0.5 collective-permute-done.b_ref
  14.2 0.0 copy-start.1
  14.2 1.1 copy-done.1
  15.3 0.1 shard_map.56
  15.3 0.0 all-gather.3.cloned.1.call-update
  15.3 0.0 copy-start.3
  15.4 2.7 %shard_map.58 = (bf16[1024,512]{1,0:T(8,128)(2,1)}, bf16[1024,512]{1,0:T(8,128)(2,1)}) custom-call(s32[1]{0:T(128)} %bitcast.side_ref, f32[16,72,128]{2,1,0:T(8,128)} %get-tuple-element.16.after_ref, bf16[1024,1024]{1,0:T(8,128)(2,1)} %rest_4_.1, bf16[1024,1024]{1,0:T(8,128)(2,1)} %rest_6_.1), custom_call_target="tpu_custom_call" | custom-call | tf_op jit(solution)/shard_map/pallas_call | solution.py:119
  18.0 0.5 collective-permute-start.5
  18.5 0.1 collective-permute-start.6
  18.6 33.1 %all_to_all.20.in_ref = f32[16,72,128]{2,1,0:T(8,128)S(1)} all-to-all(f32[16,72,128]{2,1,0:T(8,128)S(1)} %get-tuple-element.17), channel_id=1, replica_groups=mesh['x'=4,'y'=4,'c'=2,'z'=4] {'x','y'}, dimensions={0} | all-to-all | bytes 1179648 | tf_op jit(solution)/shard_map/all_to_all | solution.py:386
  51.7 0.0 copy-done.3
  51.7 0.8 shard_map.57
  52.5 0.0 copy-start.4
  52.5 3.5 %all-to-all-start.1 = ((bf16[16,64,128]{2,1,0:T(8,128)(2,1)}), bf16[16,64,128]{2,1,0:T(8,128)(2,1)S(1)}, u32[]{:S(2)}, u32[]{:S(2)}) async-start(bf16[16,64,128]{2,1,0:T(8,128)(2,1)} %get-tuple-element.18), calls=%async_computation.1 | async-start | bytes 524288 | tf_op jit(solution)/shard_map/all_to_all | solution.py:386
  56.0 2.1 %collective-permute-start.4 = (s32[8,1024]{1,0:T(8,128)S(1)}, s32[8,1024]{1,0:T(8,128)S(1)}, u32[]{:S(2)}, u32[]{:S(2)}) collective-permute-start(s32[8,1024]{1,0:T(8,128)S(1)} %get-tuple-element.19.rest_0_), channel_id=1, source_target_pairs={{0,3},{1,0},{2,1},{3,2},{4,7},{5,4},{6,5},{7,6},{8,11},{9,8},{10,9... | collective-permute-start | bytes 98312 | tf_op jit(solution)/shard_map/ppermute | solution.py:393
  58.1 1.6 %collective-permute-start.3 = (s32[8,1024]{1,0:T(8,128)S(1)}, s32[8,1024]{1,0:T(8,128)S(1)}, u32[]{:S(2)}, u32[]{:S(2)}) collective-permute-start(s32[8,1024]{1,0:T(8,128)S(1)} %get-tuple-element.19.rest_0_), channel_id=1, source_target_pairs={{0,2},{1,3},{2,0},{3,1},{4,6},{5,7},{6,4},{7,5},{8,10},{9,11},{10,... | collective-permute-start | bytes 98312 | tf_op jit(solution)/shard_map/ppermute | solution.py:393
  59.7 0.0 collective-permute-start.2
  59.7 0.0 collective-permute-done.5.rest_5_
  59.7 0.0 copy-start.5
  59.7 0.0 collective-permute-done.6.rest_7_
  59.7 0.0 copy-start.6
  59.7 0.0 collective-permute-done.4.rest_3_
  59.7 0.0 copy-start.8
  59.7 2.6 %collective-permute-done.3.rest_2_ = s32[8,1024]{1,0:T(8,128)S(1)} collective-permute-done((s32[8,1024]{1,0:T(8,128)S(1)}, s32[8,1024]{1,0:T(8,128)S(1)}, u32[]{:S(2)}, u32[]{:S(2)}) %collective-permute-start.3) | collective-permute-done | bytes 32800 | tf_op jit(solution)/shard_map/ppermute | solution.py:393
  62.4 0.0 copy-start.9
  62.4 1.6 %collective-permute-done.2.rest_1_ = s32[8,1024]{1,0:T(8,128)S(1)} collective-permute-done((s32[8,1024]{1,0:T(8,128)S(1)}, s32[8,1024]{1,0:T(8,128)S(1)}, u32[]{:S(2)}, u32[]{:S(2)}) %collective-permute-start.2) | collective-permute-done | bytes 32800 | tf_op jit(solution)/shard_map/ppermute | solution.py:393
  64.0 0.0 copy-start.10
  64.0 0.0 all-to-all-done.1
  64.0 0.0 copy-start.7
  64.0 0.0 copy-done.4
  64.0 0.0 copy-done.5
  64.0 0.0 copy-done.6
  64.0 0.0 copy-done.8
  64.0 0.0 copy-done.9
  64.0 0.5 copy-done.10
  64.6 0.1 copy-done.7
  64.7 6.9 %shard_map.59 = (bf16[16,80,128]{2,1,0:T(8,128)(2,1)}, s32[4,8,1024]{2,1,0:T(8,128)}) custom-call(s32[1]{0:T(128)} %bitcast.side_ref, bf16[4,256,128]{2,1,0:T(8,128)(2,1)} %bitcast.14, s32[8,1024]{1,0:T(8,128)} %copy-done.4, s32[8,1024]{1,0:T(8,128)} %copy-done.10, s32[8,1024]{1,0:T(8,128)} %copy-done.9, s32[8,1024]{1,0:T(8,128)} %copy-done.8, ...), custom_call_target="tpu_custom_call" | custom-call | tf_op jit(solution)/shard_map/pallas_call | solution.py:238
  71.6 0.0 copy-start.2
  71.6 14.6 %all_to_all.21.in_ref = bf16[16,80,128]{2,1,0:T(8,128)(2,1)S(1)} all-to-all(bf16[16,80,128]{2,1,0:T(8,128)(2,1)} %get-tuple-element.23), channel_id=1, replica_groups=mesh['x'=4,'y'=4,'c'=2,'z'=4] {'x','y'}, dimensions={0} | all-to-all | bytes 655360 | tf_op jit(solution)/shard_map/all_to_all | solution.py:386
  86.2 0.4 shard_map.60
  86.6 23.0 %all_to_all.22 = bf16[64,64,128]{2,1,0:T(8,128)(2,1)S(1)} all-to-all(bf16[64,64,128]{2,1,0:T(8,128)(2,1)S(1)} %shard_map.60), channel_id=1, replica_groups=mesh['x'=4,'y'=4,'c'=2,'z'=4] {'z','x','y'}, dimensions={0} | all-to-all | bytes 2097152 | tf_op jit(solution)/shard_map/all_to_all | solution.py:386
  109.6 3.8 %collective-permute-start.7 = (bf16[16,256,128]{2,1,0:T(8,128)(2,1)S(1)}, bf16[16,256,128]{2,1,0:T(8,128)(2,1)S(1)}, u32[]{:S(2)}, u32[]{:S(2)}) collective-permute-start(bf16[16,256,128]{2,1,0:T(8,128)(2,1)S(1)} %bitcast.10), channel_id=1, source_target_pairs={{0,4},{4,0},{1,5},{5,1},{2,6},{6,2},{3,7},{7,3},{8,12},{12,8},{9,1... | collective-permute-start | bytes 3145736 | tf_op jit(solution)/shard_map/ppermute | solution.py:382
  113.4 0.0 all-gather.3.cloned.1.call-done
  113.4 0.7 slice_bitcast_fusion.after_ref
  114.1 0.0 copy-done.2
  114.1 3.1 %shard_map.61.near_ref = bf16[4,1024,512]{2,1,0:T(8,128)(2,1)S(1)} custom-call(s32[1]{0:T(128)} %bitcast.side_ref, s32[1]{0:T(128)} %bitcast.1.z_ref, s32[4,8,1024]{2,1,0:T(8,128)S(1)} %copy-done.2, bf16[16,256,128]{2,1,0:T(8,128)(2,1)S(1)} %bitcast.11, bf16[16,128]{1,0:T(8,128)(2,1)S(1)} %slice_bitcast_fusion.after_ref), custom_call_target="tpu_custom_call" | custom-call | tf_op jit(solution)/shard_map/pallas_call | solution.py:291
  117.2 0.0 collective-permute-done.7.table_ref
  117.2 0.0 copy-start
  117.2 3.4 %copy-done = bf16[32768,128]{1,0:T(8,128)(2,1)S(1)} copy-done((bf16[32768,128]{1,0:T(8,128)(2,1)S(1)}, bf16[32768,128]{1,0:T(8,128)(2,1)}, u32[]{:S(2)}) %copy-start) | copy-done | bytes 8388632
  120.6 15.7 %shard_map.62 = bf16[1024,1024]{1,0:T(8,128)(2,1)} custom-call(s32[1]{0:T(128)} %bitcast.side_ref, s32[1]{0:T(128)} %bitcast.1.z_ref, bf16[4,1024,512]{2,1,0:T(8,128)(2,1)S(1)} %shard_map.61.near_ref, s32[4,8,1024]{2,1,0:T(8,128)S(1)} %copy-done.2, bf16[16,256,128]{2,1,0:T(8,128)(2,1)S(1)} %collective-permute-done.7.table_ref, ...), custom_call_target="tpu_custom_call" | custom-call | tf_op jit(solution)/shard_map/pallas_call | solution.py:364
Async XLA Ops:
  6.5 5.8 %copy-start.11 = (bf16[1024,128]{1,0:T(8,128)(2,1)S(1)}, bf16[1024,128]{1,0:T(8,128)(2,1)}, u32[]{:S(2)}) copy-start(bf16[1024,128]{1,0:T(8,128)(2,1)} %param.9) | copy-start | bytes 786436
  6.5 106.9 %all-gather.3.cloned.1.call-start = ((), (), s32[]{:S(2)}) async-start(), calls=%async_computation.4 | async-start | bytes 8650752 | tf_op jit(solution)/shard_map/all_gather | solution.py:413
  10.8 3.3 %collective-permute-start = (f32[16,72,128]{2,1,0:T(8,128)}, f32[16,72,128]{2,1,0:T(8,128)S(1)}, u32[]{:S(2)}, u32[]{:S(2)}) collective-permute-start(f32[16,72,128]{2,1,0:T(8,128)} %get-tuple-element.16.after_ref), channel_id=1, source_target_pairs={{0,4},{4,0},{1,5},{5,1},{2,6},{6,2},{3,7},{7,3},{8,12},{12,8},{9,1... | collective-permute-start | bytes 1769480 | tf_op jit(solution)/shard_map/ppermute | solution.py:382
  12.3 1.4 collective-permute-start.1
  14.2 1.1 copy-start.1
  15.3 36.3 %copy-start.3 = (s32[1024,8]{0,1:T(8,128)S(1)}, s32[1024,8]{0,1:T(8,128)}, u32[]{:S(2)}) copy-start(s32[1024,8]{0,1:T(8,128)} %param.8) | copy-start | bytes 98308
  18.0 41.7 %collective-permute-start.5 = (bf16[1024,512]{1,0:T(8,128)(2,1)}, bf16[1024,512]{1,0:T(8,128)(2,1)S(1)}, u32[]{:S(2)}, u32[]{:S(2)}) collective-permute-start(bf16[1024,512]{1,0:T(8,128)(2,1)} %get-tuple-element.20), channel_id=1, source_target_pairs={{0,4},{4,0},{1,5},{5,1},{2,6},{6,2},{3,7},{7,3},{8,12},{12,8},{9,1... | collective-permute-start | bytes 3145736 | tf_op jit(solution)/shard_map/ppermute | solution.py:382
  18.5 41.2 %collective-permute-start.6 = (bf16[1024,512]{1,0:T(8,128)(2,1)}, bf16[1024,512]{1,0:T(8,128)(2,1)S(1)}, u32[]{:S(2)}, u32[]{:S(2)}) collective-permute-start(bf16[1024,512]{1,0:T(8,128)(2,1)} %get-tuple-element.21), channel_id=1, source_target_pairs={{0,4},{4,0},{1,5},{5,1},{2,6},{6,2},{3,7},{7,3},{8,12},{12,8},{9,1... | collective-permute-start | bytes 3145736 | tf_op jit(solution)/shard_map/ppermute | solution.py:382
  52.5 11.5 %copy-start.4 = (s32[8,1024]{1,0:T(8,128)}, s32[8,1024]{1,0:T(8,128)S(1)}, u32[]{:S(2)}) copy-start(s32[8,1024]{1,0:T(8,128)S(1)} %get-tuple-element.19.rest_0_) | copy-start | bytes 98308
  52.5 11.5 %all-to-all-start.1 = ((bf16[16,64,128]{2,1,0:T(8,128)(2,1)}), bf16[16,64,128]{2,1,0:T(8,128)(2,1)S(1)}, u32[]{:S(2)}, u32[]{:S(2)}) async-start(bf16[16,64,128]{2,1,0:T(8,128)(2,1)} %get-tuple-element.18), calls=%async_computation.1 | async-start | bytes 524288 | tf_op jit(solution)/shard_map/all_to_all | solution.py:386
  56.0 3.7 %collective-permute-start.4 = (s32[8,1024]{1,0:T(8,128)S(1)}, s32[8,1024]{1,0:T(8,128)S(1)}, u32[]{:S(2)}, u32[]{:S(2)}) collective-permute-start(s32[8,1024]{1,0:T(8,128)S(1)} %get-tuple-element.19.rest_0_), channel_id=1, source_target_pairs={{0,3},{1,0},{2,1},{3,2},{4,7},{5,4},{6,5},{7,6},{8,11},{9,8},{10,9... | collective-permute-start | bytes 98312 | tf_op jit(solution)/shard_map/ppermute | solution.py:393
  58.1 4.3 %collective-permute-start.3 = (s32[8,1024]{1,0:T(8,128)S(1)}, s32[8,1024]{1,0:T(8,128)S(1)}, u32[]{:S(2)}, u32[]{:S(2)}) collective-permute-start(s32[8,1024]{1,0:T(8,128)S(1)} %get-tuple-element.19.rest_0_), channel_id=1, source_target_pairs={{0,2},{1,3},{2,0},{3,1},{4,6},{5,7},{6,4},{7,5},{8,10},{9,11},{10,... | collective-permute-start | bytes 98312 | tf_op jit(solution)/shard_map/ppermute | solution.py:393
  59.7 4.3 %collective-permute-start.2 = (s32[8,1024]{1,0:T(8,128)S(1)}, s32[8,1024]{1,0:T(8,128)S(1)}, u32[]{:S(2)}, u32[]{:S(2)}) collective-permute-start(s32[8,1024]{1,0:T(8,128)S(1)} %get-tuple-element.19.rest_0_), channel_id=1, source_target_pairs={{0,1},{1,2},{2,3},{3,0},{4,5},{5,6},{6,7},{7,4},{8,9},{9,10},{10,1... | collective-permute-start | bytes 98312 | tf_op jit(solution)/shard_map/ppermute | solution.py:393
  59.7 4.3 %copy-start.5 = (bf16[1024,512]{1,0:T(8,128)(2,1)}, bf16[1024,512]{1,0:T(8,128)(2,1)S(1)}, u32[]{:S(2)}) copy-start(bf16[1024,512]{1,0:T(8,128)(2,1)S(1)} %collective-permute-done.5.rest_5_) | copy-start | bytes 3145732
  59.7 4.3 %copy-start.6 = (bf16[1024,512]{1,0:T(8,128)(2,1)}, bf16[1024,512]{1,0:T(8,128)(2,1)S(1)}, u32[]{:S(2)}) copy-start(bf16[1024,512]{1,0:T(8,128)(2,1)S(1)} %collective-permute-done.6.rest_7_) | copy-start | bytes 3145732
  59.7 4.3 %copy-start.8 = (s32[8,1024]{1,0:T(8,128)}, s32[8,1024]{1,0:T(8,128)S(1)}, u32[]{:S(2)}) copy-start(s32[8,1024]{1,0:T(8,128)S(1)} %collective-permute-done.4.rest_3_) | copy-start | bytes 98308
  62.4 1.6 %copy-start.9 = (s32[8,1024]{1,0:T(8,128)}, s32[8,1024]{1,0:T(8,128)S(1)}, u32[]{:S(2)}) copy-start(s32[8,1024]{1,0:T(8,128)S(1)} %collective-permute-done.3.rest_2_) | copy-start | bytes 98308
  64.0 0.6 copy-start.10
  64.0 0.7 copy-start.7
  71.6 42.5 %copy-start.2 = (s32[4,8,1024]{2,1,0:T(8,128)S(1)}, s32[4,8,1024]{2,1,0:T(8,128)}, u32[]{:S(2)}) copy-start(s32[4,8,1024]{2,1,0:T(8,128)} %get-tuple-element.22.ids_ref) | copy-start | bytes 393220
  109.6 7.6 %collective-permute-start.7 = (bf16[16,256,128]{2,1,0:T(8,128)(2,1)S(1)}, bf16[16,256,128]{2,1,0:T(8,128)(2,1)S(1)}, u32[]{:S(2)}, u32[]{:S(2)}) collective-permute-start(bf16[16,256,128]{2,1,0:T(8,128)(2,1)S(1)} %bitcast.10), channel_id=1, source_target_pairs={{0,4},{4,0},{1,5},{5,1},{2,6},{6,2},{3,7},{7,3},{8,12},{12,8},{9,1... | collective-permute-start | bytes 3145736 | tf_op jit(solution)/shard_map/ppermute | solution.py:382
  117.2 3.4 %copy-start = (bf16[32768,128]{1,0:T(8,128)(2,1)S(1)}, bf16[32768,128]{1,0:T(8,128)(2,1)}, u32[]{:S(2)}) copy-start(bf16[32768,128]{1,0:T(8,128)(2,1)} %all-gather.3.cloned.1.call-done) | copy-start | bytes 25165828
Sparse Core Ops, SparseCore 0:
  15.5 69.9 all-gather.2

commit v4 on v3

--- a/solution.py
+++ b/solution.py
@@ -88,7 +88,7 @@
             pltpu.VMEM((2, rows, HALF * HDIM), BF16),
             pltpu.SemaphoreType.DMA((2,)),
         ],
-        compiler_params=params(LARGE),
+        compiler_params=params(60),
     )(side, ids, queries)
 
 
@@ -130,26 +130,8 @@
     )(side, after, keys, values)
 
 
-def add_kernel(a_ref, b_ref, passed_ref, out_ref, handed_ref):
+def centre_kernel(in_ref, ids_ref, passed_ref, out_ref, ids_out_ref, handed_ref):
     del passed_ref, handed_ref
-    out_ref[...] = a_ref[...] + b_ref[...]
-
-
-def add_after(a, b, passed):
-    return pl.pallas_call(
-        add_kernel,
-        out_shape=(
-            jax.ShapeDtypeStruct(a.shape, a.dtype),
-            jax.ShapeDtypeStruct(passed.shape, passed.dtype),
-        ),
-        in_specs=[IN_VMEM, IN_VMEM, IN_HBM],
-        out_specs=(IN_VMEM, IN_HBM),
-        input_output_aliases={2: 1},
-        compiler_params=params(8),
-    )(a, b, passed)
-
-
-def centre_kernel(in_ref, ids_ref, out_ref, ids_out_ref):
     whole = in_ref[0]
     for k in range(1, in_ref.shape[0]):
         whole += in_ref[k]
@@ -161,15 +143,19 @@
     ids_out_ref[...] = ids_ref[...]
 
 
-def centre_of(totals, ids):
+def centre_of(totals, ids, passed):
     return pl.pallas_call(
         centre_kernel,
         out_shape=(
             jax.ShapeDtypeStruct((totals.shape[0], QUARTER, HDIM), BF16),
             jax.ShapeDtypeStruct(ids.shape, ids.dtype),
+            jax.ShapeDtypeStruct(passed.shape, passed.dtype),
         ),
+        in_specs=[IN_VMEM, IN_VMEM, IN_HBM],
+        out_specs=(IN_VMEM, IN_VMEM, IN_HBM),
+        input_output_aliases={2: 2},
         compiler_params=params(8),
-    )(totals, ids)
+    )(totals, ids, passed)
 
 
 def attention_kernel(groups, side_ref, centre_ref, *rest):
@@ -294,7 +280,7 @@
         grid=(groups,),
         in_specs=[SCALARS, SCALARS, IN_VMEM, IN_VMEM, IN_HBM],
         out_specs=pl.BlockSpec((None, tokens, HALF * HDIM), lambda i: (i, 0, 0)),
-        compiler_params=params(24),
+        compiler_params=params(57),
     )(side, z, ids, table, after)
 
 
@@ -374,7 +360,7 @@
             pltpu.SemaphoreType.DMA((2 * groups,)),
             pltpu.SemaphoreType.DMA((groups,)),
         ],
-        compiler_params=params(40),
+        compiler_params=params(57),
     )(side, z, near, ids, table, weight)
 
 
@@ -409,11 +395,10 @@
     arrived = other_core(theirs)
     keys_far, values_far = halves_of(side, theirs, keys, values)
     keys_other, values_other = other_core(keys_far), other_core(values_far)
-    totals, turned_weight = add_after(mine, arrived, turned_weight)
+    totals = exchanged(mine + arrived, PLANE)
+    centre, ids, turned_weight = centre_of(totals, ids, turned_weight)
     weight = lax.all_gather(turned_weight, SEQ, axis=0)
     weight = weight.reshape(size, -1, *weight.shape[1:])
-
-    centre, ids = centre_of(exchanged(totals, PLANE), ids)
     all_ids = from_all_groups(ids)
     centre = exchanged(centre, PLANE).reshape(HALF, CLUSTERS, HDIM)
     parts, all_ids = attention_of(
@@ -427,7 +412,7 @@
     )(parts)
     table = exchanged(table, CUBE).reshape(size * HALF, CLUSTERS, HDIM)
     far_table = other_core(table)
-    near = gather_of(side, z, all_ids, table, weight[0, 0, :16])
+    near = gather_of(side, z, all_ids, table, weight)
     return project_of(side, z, near, all_ids, far_table, weight)
 
 

time: 144 us -> 143 us (level)
  blocking collectives: 70.7 us -> 38.9 us
  starting transfers between devices: 14.4 us -> 29.6 us
  waiting for transfers between devices: 4.71 us -> 18.1 us
  Pallas kernels: 33.9 us -> 38.9 us
  local copies, waits for them, and re-layouts: 5.82 us -> 1.72 us
  other arithmetic: 0 us -> 1.94 us
    all_to_all x3 -> x2, blocking collectives: 70.7 us -> 38.9 us  [exchanged(): return lax.all_to_all(value, axes, split_axis=0, concat_axis=0, tiled=True)]
    all_to_all x1 -> x2, starting transfers between devices: 3.53 us -> 17.3 us  [exchanged(): return lax.all_to_all(value, axes, split_axis=0, concat_axis=0, tiled=True)]
    all_to_all x1 -> x2, waiting for transfers between devices: 0.01 us -> 11.9 us  [exchanged(): return lax.all_to_all(value, axes, split_axis=0, concat_axis=0, tiled=True)]
    unnamed x24 -> x22, local copies, waits for them, and re-layouts: 5.13 us -> 1.72 us
    pallas_call x1, Pallas kernels: 3.11 us -> 5.65 us  [gather_of(): pl.pallas_call(gather_kernel, out_shape=jax.ShapeDtypeStruct((groups, tok...]
    pallas_call x1, Pallas kernels: 15.7 us -> 18.2 us  [project_of(): pl.pallas_call(project_kernel, out_shape=jax.ShapeDtypeStruct((tokens, co...]
    add x0 -> x1, other arithmetic: none -> 1.94 us  [local(): totals = exchanged(mine + arrived, PLANE)]
    ppermute x4, starting transfers between devices: 5.89 us -> 7.73 us  [other_core(): return lax.ppermute(value, 'c', [(0, 1), (1, 0)])]
  transfers between devices with their start and end apart: 10 -> 11, of which waited for: 3 -> 5; matrix products, arithmetic and copies ran while one was open for 0% -> 0% of each run, Pallas kernels for 10% -> 11%
where the time goes in v4:
time: 143 us
  Pallas kernels  38.9 us (27%)
  blocking collectives  38.9 us (27%)
  starting transfers between devices  29.6 us (21%)
  waiting for transfers between devices  18.1 us (13%)
  between operations  13.6 us (10%)
  other arithmetic  1.94 us (1%)
  local copies, waits for them, and re-layouts  1.72 us (1%)
    all_to_all x2, blocking collectives, exchanged(): return lax.all_to_all(value, axes, split_axis=0, concat_axis=0, tiled=True)  38.9 us
    pallas_call x1, Pallas kernels, project_of(): pl.pallas_call(project_kernel, out_shape=jax.ShapeDtypeStruct((tokens, co...  18.2 us
    all_to_all x2, starting transfers between devices, exchanged(): return lax.all_to_all(value, axes, split_axis=0, concat_axis=0, tiled=True)  17.3 us
    all_to_all x2, waiting for transfers between devices, exchanged(): return lax.all_to_all(value, axes, split_axis=0, concat_axis=0, tiled=True)  11.9 us
    ppermute x4, starting transfers between devices, other_core(): return lax.ppermute(value, 'c', [(0, 1), (1, 0)])  7.73 us
    pallas_call x1, Pallas kernels, attention_of(): pl.pallas_call(functools.partial(attention_kernel, groups), out_shape=(ja...  6.89 us
    pallas_call x1, Pallas kernels, gather_of(): pl.pallas_call(gather_kernel, out_shape=jax.ShapeDtypeStruct((groups, tok...  5.65 us
    pallas_call x1, Pallas kernels, totals_of(): pl.pallas_call(totals_kernel, out_shape=[jax.ShapeDtypeStruct((4 * HALF,...  4.33 us
  transfers between devices with their start and end apart: 11, of which 5 were waited for; matrix products, arithmetic and copies ran while one was open for 0% of the time, Pallas kernels for 11%

profile of v4, /device:TPU:1, one launch (start us, length us, event | category | flops | bytes accessed | tf_op | source)
XLA Modules:
  0.0 142.7 jit_solution(7719244664503396570)
XLA Ops:
  6.5 0.0 copy-start.10
  6.5 0.0 copy-start
  6.5 4.3 %shard_map.55 = (f32[16,72,128]{2,1,0:T(8,128)}, f32[16,72,128]{2,1,0:T(8,128)}) custom-call(s32[1]{0:T(128)} %bitcast.side_ref, s32[8,1024]{1,0:T(8,128)} %bitcast.6, bf16[1024,1024]{1,0:T(8,128)(2,1)} %q_ref.1), custom_call_target="tpu_custom_call" | custom-call | tf_op jit(solution)/shard_map/pallas_call | solution.py:82
  10.9 1.5 %collective-permute-start = (f32[16,72,128]{2,1,0:T(8,128)}, f32[16,72,128]{2,1,0:T(8,128)S(1)}, u32[]{:S(2)}, u32[]{:S(2)}) collective-permute-start(f32[16,72,128]{2,1,0:T(8,128)} %get-tuple-element.15.after_ref), channel_id=1, source_target_pairs={{0,4},{4,0},{1,5},{5,1},{2,6},{6,2},{3,7},{7,3},{8,12},{12,8},{9,1... | collective-permute-start | bytes 1769480 | tf_op jit(solution)/shard_map/ppermute | solution.py:368
  12.4 1.8 %collective-permute-done = f32[16,72,128]{2,1,0:T(8,128)S(1)} collective-permute-done((f32[16,72,128]{2,1,0:T(8,128)}, f32[16,72,128]{2,1,0:T(8,128)S(1)}, u32[]{:S(2)}, u32[]{:S(2)}) %collective-permute-start) | collective-permute-done | bytes 589856 | tf_op jit(solution)/shard_map/ppermute | solution.py:368
  14.2 1.9 %add.3 = f32[16,72,128]{2,1,0:T(8,128)} add(f32[16,72,128]{2,1,0:T(8,128)} %get-tuple-element.14, f32[16,72,128]{2,1,0:T(8,128)S(1)} %collective-permute-done) | non-fusion elementwise | flops 147456 | bytes 1769472 | tf_op jit(solution)/shard_map/add | solution.py:398
  16.2 6.8 %all-to-all-start = ((f32[16,72,128]{2,1,0:T(8,128)}), f32[16,72,128]{2,1,0:T(8,128)S(1)}, u32[]{:S(2)}, u32[]{:S(2)}) async-start(f32[16,72,128]{2,1,0:T(8,128)} %add.3), calls=%async_computation | async-start | bytes 1179648 | tf_op jit(solution)/shard_map/all_to_all | solution.py:372
  23.0 0.0 all-gather.3.cloned.1.call-start
  23.1 0.0 copy-done.10
  23.1 1.4 collective-permute-start.1
  24.4 0.0 collective-permute-done.1.passed_ref
  24.4 9.4 %all-to-all-done.in_ref = f32[16,72,128]{2,1,0:T(8,128)S(1)} async-done(((f32[16,72,128]{2,1,0:T(8,128)}), f32[16,72,128]{2,1,0:T(8,128)S(1)}, u32[]{:S(2)}, u32[]{:S(2)}) %all-to-all-start) | async-done | bytes 589856 | tf_op jit(solution)/shard_map/all_to_all | solution.py:372
  33.9 0.0 copy-done
  33.9 0.9 shard_map.56
  34.7 0.0 copy-start.1
  34.7 0.0 all-gather.3.cloned.1.call-update
  34.8 2.7 %shard_map.57 = (bf16[1024,512]{1,0:T(8,128)(2,1)}, bf16[1024,512]{1,0:T(8,128)(2,1)}) custom-call(s32[1]{0:T(128)} %bitcast.side_ref, f32[16,72,128]{2,1,0:T(8,128)} %get-tuple-element.15.after_ref, bf16[1024,1024]{1,0:T(8,128)(2,1)} %rest_4_.1, bf16[1024,1024]{1,0:T(8,128)(2,1)} %rest_6_.1), custom_call_target="tpu_custom_call" | custom-call | tf_op jit(solution)/shard_map/pallas_call | solution.py:119
  37.4 3.0 %collective-permute-start.5 = (bf16[1024,512]{1,0:T(8,128)(2,1)}, bf16[1024,512]{1,0:T(8,128)(2,1)S(1)}, u32[]{:S(2)}, u32[]{:S(2)}) collective-permute-start(bf16[1024,512]{1,0:T(8,128)(2,1)} %get-tuple-element.18), channel_id=1, source_target_pairs={{0,4},{4,0},{1,5},{5,1},{2,6},{6,2},{3,7},{7,3},{8,12},{12,8},{9,1... | collective-permute-start | bytes 3145736 | tf_op jit(solution)/shard_map/ppermute | solution.py:368
  40.4 0.1 collective-permute-start.6
  40.5 10.4 %all-to-all-start.1 = ((bf16[16,64,128]{2,1,0:T(8,128)(2,1)}), bf16[16,64,128]{2,1,0:T(8,128)(2,1)S(1)}, u32[]{:S(2)}, u32[]{:S(2)}) async-start(bf16[16,64,128]{2,1,0:T(8,128)(2,1)} %get-tuple-element.16), calls=%async_computation.1 | async-start | bytes 524288 | tf_op jit(solution)/shard_map/all_to_all | solution.py:372
  50.9 0.5 collective-permute-start.4
  51.4 2.7 %collective-permute-start.3 = (s32[8,1024]{1,0:T(8,128)S(1)}, s32[8,1024]{1,0:T(8,128)S(1)}, u32[]{:S(2)}, u32[]{:S(2)}) collective-permute-start(s32[8,1024]{1,0:T(8,128)S(1)} %get-tuple-element.17.rest_0_), channel_id=1, source_target_pairs={{0,2},{1,3},{2,0},{3,1},{4,6},{5,7},{6,4},{7,5},{8,10},{9,11},{10,... | collective-permute-start | bytes 98312 | tf_op jit(solution)/shard_map/ppermute | solution.py:379
  54.1 0.0 copy-done.1
  54.1 0.0 collective-permute-start.2
  54.1 0.0 collective-permute-done.5.rest_5_
  54.1 0.0 copy-start.4
  54.1 0.0 collective-permute-done.6.rest_7_
  54.1 0.0 copy-start.5
  54.1 0.0 collective-permute-done.4.rest_3_
  54.1 0.0 copy-start.7
  54.1 1.6 %collective-permute-done.3.rest_2_ = s32[8,1024]{1,0:T(8,128)S(1)} collective-permute-done((s32[8,1024]{1,0:T(8,128)S(1)}, s32[8,1024]{1,0:T(8,128)S(1)}, u32[]{:S(2)}, u32[]{:S(2)}) %collective-permute-start.3) | collective-permute-done | bytes 32800 | tf_op jit(solution)/shard_map/ppermute | solution.py:379
  55.7 0.0 copy-start.8
  55.7 2.7 %collective-permute-done.2.rest_1_ = s32[8,1024]{1,0:T(8,128)S(1)} collective-permute-done((s32[8,1024]{1,0:T(8,128)S(1)}, s32[8,1024]{1,0:T(8,128)S(1)}, u32[]{:S(2)}, u32[]{:S(2)}) %collective-permute-start.2) | collective-permute-done | bytes 32800 | tf_op jit(solution)/shard_map/ppermute | solution.py:379
  58.5 0.0 copy-start.9
  58.5 2.4 %all-to-all-done.1 = bf16[16,64,128]{2,1,0:T(8,128)(2,1)S(1)} async-done(((bf16[16,64,128]{2,1,0:T(8,128)(2,1)}), bf16[16,64,128]{2,1,0:T(8,128)(2,1)S(1)}, u32[]{:S(2)}, u32[]{:S(2)}) %all-to-all-start.1) | async-done | bytes 262176 | tf_op jit(solution)/shard_map/all_to_all | solution.py:372
  60.9 0.0 copy-start.6
  60.9 0.0 copy-done.4
  60.9 0.0 copy-done.5
  60.9 0.0 copy-done.7
  60.9 0.0 copy-done.8
  60.9 0.0 copy-done.9
  60.9 0.7 copy-done.6
  61.6 6.9 %shard_map.58 = (bf16[16,80,128]{2,1,0:T(8,128)(2,1)}, s32[4,8,1024]{2,1,0:T(8,128)}) custom-call(s32[1]{0:T(128)} %bitcast.side_ref, bf16[4,256,128]{2,1,0:T(8,128)(2,1)} %bitcast.12, s32[8,1024]{1,0:T(8,128)} %copy-done.1, s32[8,1024]{1,0:T(8,128)} %copy-done.9, s32[8,1024]{1,0:T(8,128)} %copy-done.8, s32[8,1024]{1,0:T(8,128)} %copy-done.7, ...), custom_call_target="tpu_custom_call" | custom-call | tf_op jit(solution)/shard_map/pallas_call | solution.py:224
  68.5 14.0 %all_to_all.20.in_ref = bf16[16,80,128]{2,1,0:T(8,128)(2,1)S(1)} all-to-all(bf16[16,80,128]{2,1,0:T(8,128)(2,1)} %get-tuple-element.21), channel_id=1, replica_groups=mesh['x'=4,'y'=4,'c'=2,'z'=4] {'x','y'}, dimensions={0} | all-to-all | bytes 655360 | tf_op jit(solution)/shard_map/all_to_all | solution.py:372
  82.5 0.4 shard_map.59
  82.9 24.9 %all_to_all.21 = bf16[64,64,128]{2,1,0:T(8,128)(2,1)S(1)} all-to-all(bf16[64,64,128]{2,1,0:T(8,128)(2,1)S(1)} %shard_map.59), channel_id=1, replica_groups=mesh['x'=4,'y'=4,'c'=2,'z'=4] {'z','x','y'}, dimensions={0} | all-to-all | bytes 2097152 | tf_op jit(solution)/shard_map/all_to_all | solution.py:372
  107.8 0.0 copy-start.2
  107.8 3.2 %collective-permute-start.7 = (bf16[16,256,128]{2,1,0:T(8,128)(2,1)S(1)}, bf16[16,256,128]{2,1,0:T(8,128)(2,1)S(1)}, u32[]{:S(2)}, u32[]{:S(2)}) collective-permute-start(bf16[16,256,128]{2,1,0:T(8,128)(2,1)S(1)} %bitcast.10), channel_id=1, source_target_pairs={{0,4},{4,0},{1,5},{5,1},{2,6},{6,2},{3,7},{7,3},{8,12},{12,8},{9,1... | collective-permute-start | bytes 3145736 | tf_op jit(solution)/shard_map/ppermute | solution.py:368
  111.0 0.0 all-gather.3.cloned.1.call-done
  111.0 0.0 copy-done.2
  111.0 5.7 %shard_map.60.near_ref = bf16[4,1024,512]{2,1,0:T(8,128)(2,1)} custom-call(s32[1]{0:T(128)} %bitcast.side_ref, s32[1]{0:T(128)} %bitcast.1.z_ref, s32[4,8,1024]{2,1,0:T(8,128)} %get-tuple-element.20.ids_ref, bf16[16,256,128]{2,1,0:T(8,128)(2,1)} %bitcast.11, bf16[4,8,1024,128]{3,2,1,0:T(8,128)(2,1)} %bitcast.8), custom_call_target="tpu_custom_call" | custom-call | tf_op jit(solution)/shard_map/pallas_call | solution.py:277
  116.6 0.0 collective-permute-done.7.table_ref
  116.6 0.0 copy-start.3
  116.6 1.0 copy-done.3
  117.6 18.2 %shard_map.61 = bf16[1024,1024]{1,0:T(8,128)(2,1)} custom-call(s32[1]{0:T(128)} %bitcast.side_ref, s32[1]{0:T(128)} %bitcast.1.z_ref, bf16[4,1024,512]{2,1,0:T(8,128)(2,1)} %shard_map.60.near_ref, s32[4,8,1024]{2,1,0:T(8,128)} %get-tuple-element.20.ids_ref, bf16[16,256,128]{2,1,0:T(8,128)(2,1)} %copy-done.3, bf16[4,8,1024,128]{3,2,1,0:T(8,128)(2,1)} %bitcast.9), custom_call_target="tpu_custom_call" | custom-call | tf_op jit(solution)/shard_map/pallas_call | solution.py:350
Async XLA Ops:
  6.5 16.5 %copy-start.10 = (bf16[1024,128]{1,0:T(8,128)(2,1)S(1)}, bf16[1024,128]{1,0:T(8,128)(2,1)}, u32[]{:S(2)}) copy-start(bf16[1024,128]{1,0:T(8,128)(2,1)} %param.9) | copy-start | bytes 786436
  6.5 27.3 %copy-start = (s32[1024,8]{0,1:T(8,128)S(1)}, s32[1024,8]{0,1:T(8,128)}, u32[]{:S(2)}) copy-start(s32[1024,8]{0,1:T(8,128)} %param.8) | copy-start | bytes 98308
  10.9 3.3 %collective-permute-start = (f32[16,72,128]{2,1,0:T(8,128)}, f32[16,72,128]{2,1,0:T(8,128)S(1)}, u32[]{:S(2)}, u32[]{:S(2)}) collective-permute-start(f32[16,72,128]{2,1,0:T(8,128)} %get-tuple-element.15.after_ref), channel_id=1, source_target_pairs={{0,4},{4,0},{1,5},{5,1},{2,6},{6,2},{3,7},{7,3},{8,12},{12,8},{9,1... | collective-permute-start | bytes 1769480 | tf_op jit(solution)/shard_map/ppermute | solution.py:368
  16.2 17.7 %all-to-all-start = ((f32[16,72,128]{2,1,0:T(8,128)}), f32[16,72,128]{2,1,0:T(8,128)S(1)}, u32[]{:S(2)}, u32[]{:S(2)}) async-start(f32[16,72,128]{2,1,0:T(8,128)} %add.3), calls=%async_computation | async-start | bytes 1179648 | tf_op jit(solution)/shard_map/all_to_all | solution.py:372
  23.0 88.0 %all-gather.3.cloned.1.call-start = ((), (), s32[]{:S(2)}) async-start(), calls=%async_computation.4 | async-start | bytes 8650752 | tf_op jit(solution)/shard_map/all_gather | solution.py:400
  23.1 1.4 collective-permute-start.1
  34.7 19.3 %copy-start.1 = (s32[8,1024]{1,0:T(8,128)}, s32[8,1024]{1,0:T(8,128)S(1)}, u32[]{:S(2)}) copy-start(s32[8,1024]{1,0:T(8,128)S(1)} %get-tuple-element.17.rest_0_) | copy-start | bytes 98308
  37.4 16.7 %collective-permute-start.5 = (bf16[1024,512]{1,0:T(8,128)(2,1)}, bf16[1024,512]{1,0:T(8,128)(2,1)S(1)}, u32[]{:S(2)}, u32[]{:S(2)}) collective-permute-start(bf16[1024,512]{1,0:T(8,128)(2,1)} %get-tuple-element.18), channel_id=1, source_target_pairs={{0,4},{4,0},{1,5},{5,1},{2,6},{6,2},{3,7},{7,3},{8,12},{12,8},{9,1... | collective-permute-start | bytes 3145736 | tf_op jit(solution)/shard_map/ppermute | solution.py:368
  40.4 13.7 %collective-permute-start.6 = (bf16[1024,512]{1,0:T(8,128)(2,1)}, bf16[1024,512]{1,0:T(8,128)(2,1)S(1)}, u32[]{:S(2)}, u32[]{:S(2)}) collective-permute-start(bf16[1024,512]{1,0:T(8,128)(2,1)} %get-tuple-element.19), channel_id=1, source_target_pairs={{0,4},{4,0},{1,5},{5,1},{2,6},{6,2},{3,7},{7,3},{8,12},{12,8},{9,1... | collective-permute-start | bytes 3145736 | tf_op jit(solution)/shard_map/ppermute | solution.py:368
  40.5 20.4 %all-to-all-start.1 = ((bf16[16,64,128]{2,1,0:T(8,128)(2,1)}), bf16[16,64,128]{2,1,0:T(8,128)(2,1)S(1)}, u32[]{:S(2)}, u32[]{:S(2)}) async-start(bf16[16,64,128]{2,1,0:T(8,128)(2,1)} %get-tuple-element.16), calls=%async_computation.1 | async-start | bytes 524288 | tf_op jit(solution)/shard_map/all_to_all | solution.py:372
  50.9 3.2 %collective-permute-start.4 = (s32[8,1024]{1,0:T(8,128)S(1)}, s32[8,1024]{1,0:T(8,128)S(1)}, u32[]{:S(2)}, u32[]{:S(2)}) collective-permute-start(s32[8,1024]{1,0:T(8,128)S(1)} %get-tuple-element.17.rest_0_), channel_id=1, source_target_pairs={{0,3},{1,0},{2,1},{3,2},{4,7},{5,4},{6,5},{7,6},{8,11},{9,8},{10,9... | collective-permute-start | bytes 98312 | tf_op jit(solution)/shard_map/ppermute | solution.py:379
  51.4 4.3 %collective-permute-start.3 = (s32[8,1024]{1,0:T(8,128)S(1)}, s32[8,1024]{1,0:T(8,128)S(1)}, u32[]{:S(2)}, u32[]{:S(2)}) collective-permute-start(s32[8,1024]{1,0:T(8,128)S(1)} %get-tuple-element.17.rest_0_), channel_id=1, source_target_pairs={{0,2},{1,3},{2,0},{3,1},{4,6},{5,7},{6,4},{7,5},{8,10},{9,11},{10,... | collective-permute-start | bytes 98312 | tf_op jit(solution)/shard_map/ppermute | solution.py:379
  54.1 4.4 %collective-permute-start.2 = (s32[8,1024]{1,0:T(8,128)S(1)}, s32[8,1024]{1,0:T(8,128)S(1)}, u32[]{:S(2)}, u32[]{:S(2)}) collective-permute-start(s32[8,1024]{1,0:T(8,128)S(1)} %get-tuple-element.17.rest_0_), channel_id=1, source_target_pairs={{0,1},{1,2},{2,3},{3,0},{4,5},{5,6},{6,7},{7,4},{8,9},{9,10},{10,1... | collective-permute-start | bytes 98312 | tf_op jit(solution)/shard_map/ppermute | solution.py:379
  54.1 6.8 %copy-start.4 = (bf16[1024,512]{1,0:T(8,128)(2,1)}, bf16[1024,512]{1,0:T(8,128)(2,1)S(1)}, u32[]{:S(2)}) copy-start(bf16[1024,512]{1,0:T(8,128)(2,1)S(1)} %collective-permute-done.5.rest_5_) | copy-start | bytes 3145732
  54.1 6.8 %copy-start.5 = (bf16[1024,512]{1,0:T(8,128)(2,1)}, bf16[1024,512]{1,0:T(8,128)(2,1)S(1)}, u32[]{:S(2)}) copy-start(bf16[1024,512]{1,0:T(8,128)(2,1)S(1)} %collective-permute-done.6.rest_7_) | copy-start | bytes 3145732
  54.1 6.8 %copy-start.7 = (s32[8,1024]{1,0:T(8,128)}, s32[8,1024]{1,0:T(8,128)S(1)}, u32[]{:S(2)}) copy-start(s32[8,1024]{1,0:T(8,128)S(1)} %collective-permute-done.4.rest_3_) | copy-start | bytes 98308
  55.7 5.2 %copy-start.8 = (s32[8,1024]{1,0:T(8,128)}, s32[8,1024]{1,0:T(8,128)S(1)}, u32[]{:S(2)}) copy-start(s32[8,1024]{1,0:T(8,128)S(1)} %collective-permute-done.3.rest_2_) | copy-start | bytes 98308
  58.5 2.5 %copy-start.9 = (s32[8,1024]{1,0:T(8,128)}, s32[8,1024]{1,0:T(8,128)S(1)}, u32[]{:S(2)}) copy-start(s32[8,1024]{1,0:T(8,128)S(1)} %collective-permute-done.2.rest_1_) | copy-start | bytes 98308
  60.9 0.7 copy-start.6
  107.8 3.2 %copy-start.2 = (bf16[64,64,128]{2,1,0:T(8,128)(2,1)}, bf16[64,64,128]{2,1,0:T(8,128)(2,1)S(1)}, u32[]{:S(2)}) copy-start(bf16[64,64,128]{2,1,0:T(8,128)(2,1)S(1)} %all_to_all.21) | copy-start | bytes 3145732
  107.8 8.8 %collective-permute-start.7 = (bf16[16,256,128]{2,1,0:T(8,128)(2,1)S(1)}, bf16[16,256,128]{2,1,0:T(8,128)(2,1)S(1)}, u32[]{:S(2)}, u32[]{:S(2)}) collective-permute-start(bf16[16,256,128]{2,1,0:T(8,128)(2,1)S(1)} %bitcast.10), channel_id=1, source_target_pairs={{0,4},{4,0},{1,5},{5,1},{2,6},{6,2},{3,7},{7,3},{8,12},{12,8},{9,1... | collective-permute-start | bytes 3145736 | tf_op jit(solution)/shard_map/ppermute | solution.py:368
  116.6 1.0 copy-start.3
Sparse Core Ops, SparseCore 0:
  34.9 68.5 all-gather.2

commit v5 on v3

--- a/solution.py
+++ b/solution.py
@@ -11,6 +11,7 @@
 
 HDIM = 128
 CLUSTERS = 256
+PIECES = 4
 HALF = 4
 QUARTER = CLUSTERS // 4
 SEQ = ("x", "y", "c")
@@ -41,7 +42,9 @@
     return (labels == row).astype(F32).astype(BF16)
 
 
-def totals_kernel(side_ref, ids_ref, q_ref, theirs_ref, mine_ref, held, arrived):
+def totals_kernel(side_ref, ids_ref, q_ref, *rest):
+    theirs_refs, (mine_ref, held, arrived) = rest[:PIECES], rest[PIECES:]
+    each = HALF // PIECES
     rows = q_ref.shape[0]
     firsts = (HALF - side_ref[0] * HALF, side_ref[0] * HALF)
 
@@ -55,9 +58,10 @@
         fetch(k).start()
     ones = jnp.ones((rows, HDIM), BF16)
     diagonal = eye(QUARTER, HDIM)
-    for k, out_ref in enumerate((theirs_ref, mine_ref)):
+    for k in range(2):
         fetch(k).wait()
         for i in range(HALF):
+            out_ref, base = (mine_ref, i * 4) if k else (theirs_refs[i // each], i % each * 4)
             member = member_of(ids_ref[pl.ds(firsts[k] + i, 1), :])
             query = held[k, :, i * HDIM : (i + 1) * HDIM]
             both = jnp.dot(
@@ -68,8 +72,8 @@
                 count = jnp.sum(
                     jnp.where(diagonal, both[lines, HDIM:], 0.0), axis=0, keepdims=True
                 )
-                out_ref[i * 4 + q, :QUARTER, :] = both[lines, :HDIM]
-                out_ref[i * 4 + q, QUARTER:, :] = jnp.broadcast_to(count, (EXTRA, HDIM))
+                out_ref[base + q, :QUARTER, :] = both[lines, :HDIM]
+                out_ref[base + q, QUARTER:, :] = jnp.broadcast_to(count, (EXTRA, HDIM))
 
 
 SCALARS = pl.BlockSpec(memory_space=pltpu.SMEM)
@@ -81,19 +85,26 @@
     rows = queries.shape[0]
     return pl.pallas_call(
         totals_kernel,
-        out_shape=[jax.ShapeDtypeStruct((4 * HALF, QUARTER + EXTRA, HDIM), F32)] * 2,
+        out_shape=[
+            jax.ShapeDtypeStruct((4 * HALF // PIECES, QUARTER + EXTRA, HDIM), F32),
+        ]
+        * PIECES
+        + [jax.ShapeDtypeStruct((4 * HALF, QUARTER + EXTRA, HDIM), F32)],
         in_specs=[SCALARS, IN_VMEM, IN_HBM],
-        out_specs=[IN_VMEM] * 2,
+        out_specs=[IN_VMEM] * (PIECES + 1),
         scratch_shapes=[
             pltpu.VMEM((2, rows, HALF * HDIM), BF16),
             pltpu.SemaphoreType.DMA((2,)),
         ],
-        compiler_params=params(LARGE),
+        compiler_params=params(58),
     )(side, ids, queries)
 
 
-def halves_kernel(side_ref, after_ref, k_ref, v_ref, k_out_ref, v_out_ref, held, come, gone):
+def halves_kernel(
+    side_ref, after_ref, k_ref, v_ref, k_out_ref, v_out_ref, token_ref, held, come, gone
+):
     del after_ref
+    token_ref[...] = jnp.zeros(token_ref.shape, token_ref.dtype)
     start = pl.multiple_of((1 - side_ref[0]) * HALF * HDIM, HALF * HDIM)
 
     def fetch(k, source):
@@ -118,9 +129,9 @@
     half = jax.ShapeDtypeStruct((keys.shape[0], HALF * HDIM), BF16)
     return pl.pallas_call(
         halves_kernel,
-        out_shape=(half, half),
+        out_shape=(half, half, jax.ShapeDtypeStruct((8, HDIM), F32)),
         in_specs=[SCALARS, IN_HBM, IN_HBM, IN_HBM],
-        out_specs=(IN_HBM, IN_HBM),
+        out_specs=(IN_HBM, IN_HBM, IN_VMEM),
         scratch_shapes=[
             pltpu.VMEM((2, *half.shape), BF16),
             pltpu.SemaphoreType.DMA((2,)),
@@ -130,23 +141,26 @@
     )(side, after, keys, values)
 
 
-def add_kernel(a_ref, b_ref, passed_ref, out_ref, handed_ref):
-    del passed_ref, handed_ref
-    out_ref[...] = a_ref[...] + b_ref[...]
-
-
-def add_after(a, b, passed):
+def add_kernel(a_ref, *rest):
+    out_ref = rest[PIECES + 2]
+    size = a_ref.shape[0] // PIECES
+    for k in range(PIECES):
+        lines = slice(k * size, (k + 1) * size)
+        out_ref[lines] = a_ref[lines] + rest[k][...]
+
+
+def add_after(a, b, passed, after):
     return pl.pallas_call(
         add_kernel,
         out_shape=(
             jax.ShapeDtypeStruct(a.shape, a.dtype),
             jax.ShapeDtypeStruct(passed.shape, passed.dtype),
         ),
-        in_specs=[IN_VMEM, IN_VMEM, IN_HBM],
+        in_specs=[IN_VMEM] * (PIECES + 1) + [IN_HBM, IN_HBM],
         out_specs=(IN_VMEM, IN_HBM),
-        input_output_aliases={2: 1},
+        input_output_aliases={PIECES + 1: 1},
         compiler_params=params(8),
-    )(a, b, passed)
+    )(a, *b, passed, after)
 
 
 def centre_kernel(in_ref, ids_ref, out_ref, ids_out_ref):
@@ -294,7 +308,7 @@
         grid=(groups,),
         in_specs=[SCALARS, SCALARS, IN_VMEM, IN_VMEM, IN_HBM],
         out_specs=pl.BlockSpec((None, tokens, HALF * HDIM), lambda i: (i, 0, 0)),
-        compiler_params=params(24),
+        compiler_params=params(51),
     )(side, z, ids, table, after)
 
 
@@ -374,7 +388,7 @@
             pltpu.SemaphoreType.DMA((2 * groups,)),
             pltpu.SemaphoreType.DMA((groups,)),
         ],
-        compiler_params=params(40),
+        compiler_params=params(51),
     )(side, z, near, ids, table, weight)
 
 
@@ -405,15 +419,14 @@
     ]
     turned_weight = lax.ppermute(out_weight, ("x", "z"), turned)
 
-    theirs, mine = totals_of(side, ids, queries)
-    arrived = other_core(theirs)
-    keys_far, values_far = halves_of(side, theirs, keys, values)
+    *theirs, mine = totals_of(side, ids, queries)
+    arrived = [other_core(piece) for piece in theirs]
+    keys_far, values_far, token = halves_of(side, theirs[0], keys, values)
     keys_other, values_other = other_core(keys_far), other_core(values_far)
-    totals, turned_weight = add_after(mine, arrived, turned_weight)
+    totals, turned_weight = add_after(mine, arrived, turned_weight, token)
+    centre, ids = centre_of(exchanged(totals, PLANE), ids)
     weight = lax.all_gather(turned_weight, SEQ, axis=0)
     weight = weight.reshape(size, -1, *weight.shape[1:])
-
-    centre, ids = centre_of(exchanged(totals, PLANE), ids)
     all_ids = from_all_groups(ids)
     centre = exchanged(centre, PLANE).reshape(HALF, CLUSTERS, HDIM)
     parts, all_ids = attention_of(
@@ -427,7 +440,7 @@
     )(parts)
     table = exchanged(table, CUBE).reshape(size * HALF, CLUSTERS, HDIM)
     far_table = other_core(table)
-    near = gather_of(side, z, all_ids, table, weight[0, 0, :16])
+    near = gather_of(side, z, all_ids, table, weight)
     return project_of(side, z, near, all_ids, far_table, weight)
 
 

time: 144 us -> 134 us (0.931)
  blocking collectives: 70.7 us -> 58.2 us
  local copies, waits for them, and re-layouts: 5.82 us -> 1.66 us
  starting transfers between devices: 14.4 us -> 18 us
  Pallas kernels: 33.9 us -> 37.2 us
    all_to_all x3, blocking collectives: 70.7 us -> 58.2 us  [exchanged(): return lax.all_to_all(value, axes, split_axis=0, concat_axis=0, tiled=True)]
    unnamed x24 -> x20, local copies, waits for them, and re-layouts: 5.13 us -> 1.66 us
    ppermute x1, starting transfers between devices: 1.37 us -> 3.58 us  [local(): turned_weight = lax.ppermute(out_weight, ('x', 'z'), turned)]
    ppermute x4 -> x7, starting transfers between devices: 5.89 us -> 7.88 us  [other_core(): return lax.ppermute(value, 'c', [(0, 1), (1, 0)])]
  transfers between devices with their start and end apart: 10 -> 13, of which waited for: 3 -> 3; matrix products, arithmetic and copies ran while one was open for 0% -> 0% of each run, Pallas kernels for 10% -> 15%
where the time goes in v5:
time: 134 us; the launch traced here: 133 us
  blocking collectives  58.2 us (43%)
  Pallas kernels  37.2 us (28%)
  starting transfers between devices  18 us (13%)
  between operations  13.6 us (10%)
  waiting for transfers between devices  4.4 us (3%)
  local copies, waits for them, and re-layouts  1.66 us (1%)
    all_to_all x3, blocking collectives, exchanged(): return lax.all_to_all(value, axes, split_axis=0, concat_axis=0, tiled=True)  58.2 us
    pallas_call x1, Pallas kernels, project_of(): pl.pallas_call(project_kernel, out_shape=jax.ShapeDtypeStruct((tokens, co...  16.9 us
    ppermute x7, starting transfers between devices, other_core(): return lax.ppermute(value, 'c', [(0, 1), (1, 0)])  7.88 us
    pallas_call x1, Pallas kernels, attention_of(): pl.pallas_call(functools.partial(attention_kernel, groups), out_shape=(ja...  7 us
    pallas_call x1, Pallas kernels, gather_of(): pl.pallas_call(gather_kernel, out_shape=jax.ShapeDtypeStruct((groups, tok...  4.39 us
    pallas_call x1, Pallas kernels, totals_of(): pl.pallas_call(totals_kernel, out_shape=[jax.ShapeDtypeStruct((4 * HALF /...  4.28 us
    ppermute x3, waiting for transfers between devices, from_all_groups(): lax.ppermute(value, 'z', [(i, (i + d) % size) for i in range(size)])  4.26 us
    ppermute x1, starting transfers between devices, local(): turned_weight = lax.ppermute(out_weight, ('x', 'z'), turned)  3.58 us
  transfers between devices with their start and end apart: 13, of which 3 were waited for; matrix products, arithmetic and copies ran while one was open for 0% of the time, Pallas kernels for 15%

profile of v5, /device:TPU:1, one launch (start us, length us, event | category | flops | bytes accessed | tf_op | source)
XLA Modules:
  0.0 133.0 jit_solution(8747474082617593331)
XLA Ops:
  6.5 0.0 all-gather.3.cloned.1.call-start
  6.5 3.6 %collective-permute-start.4 = (bf16[1024,128]{1,0:T(8,128)(2,1)}, bf16[1024,128]{1,0:T(8,128)(2,1)}, u32[]{:S(2)}, u32[]{:S(2)}) collective-permute-start(bf16[1024,128]{1,0:T(8,128)(2,1)} %param.9), channel_id=1, source_target_pairs={{0,0},{1,96},{2,64},{3,32},{32,65},{33,33},{34,1},{35,97},{64,2},{... | collective-permute-start | bytes 786440 | tf_op jit(solution)/shard_map/ppermute | solution.py:420
  10.1 4.3 %shard_map.55 = (f32[4,72,128]{2,1,0:T(8,128)}, f32[4,72,128]{2,1,0:T(8,128)}, f32[4,72,128]{2,1,0:T(8,128)}, f32[4,72,128]{2,1,0:T(8,128)}, f32[16,72,128]{2,1,0:T(8,128)}) custom-call(s32[1]{0:T(128)} %bitcast.side_ref, s32[8,1024]{1,0:T(8,128)} %bitcast.8, bf16[1024,1024]{1,0:T(8,128)(2,1)} %q_ref.1), custom_call_target="tpu_custom_call" | custom-call | tf_op jit(solution)/shard_map/pallas_call | solution.py:86
  14.4 1.5 %collective-permute-start.1 = (f32[4,72,128]{2,1,0:T(8,128)}, f32[4,72,128]{2,1,0:T(8,128)S(1)}, u32[]{:S(2)}, u32[]{:S(2)}) collective-permute-start(f32[4,72,128]{2,1,0:T(8,128)} %get-tuple-element.21), channel_id=1, source_target_pairs={{0,4},{4,0},{1,5},{5,1},{2,6},{6,2},{3,7},{7,3},{8,12},{12,8},{9,1... | collective-permute-start | bytes 442376 | tf_op jit(solution)/shard_map/ppermute | solution.py:396
  15.9 0.1 collective-permute-start.2
  16.0 0.4 collective-permute-start.3
  16.4 0.0 copy-start
  16.4 0.1 collective-permute-start
  16.5 3.3 %shard_map.56 = (bf16[1024,512]{1,0:T(8,128)(2,1)}, bf16[1024,512]{1,0:T(8,128)(2,1)}, f32[8,128]{1,0:T(8,128)}) custom-call(s32[1]{0:T(128)} %bitcast.side_ref, f32[4,72,128]{2,1,0:T(8,128)} %get-tuple-element.20.after_ref, bf16[1024,1024]{1,0:T(8,128)(2,1)} %rest_4_.1, bf16[1024,1024]{1,0:T(8,128)(2,1)} %rest_6_.1), custom_call_target="tpu_custom_call" | custom-call | tf_op jit(solution)/shard_map/pallas_call | solution.py:130
  19.8 0.0 copy-start.2
  19.8 0.0 collective-permute-done.1.rest_1_
  19.8 0.0 collective-permute-done.2.rest_2_
  19.8 0.0 collective-permute-done.3.rest_3_
  19.8 0.0 collective-permute-done.rest_0_
  19.9 0.0 collective-permute-done.4.rest_4_
  19.9 0.0 copy-done
  19.9 0.0 copy-start.4
  19.9 0.7 copy-done.4
  20.6 0.1 shard_map.57
  20.6 0.0 all-gather.3.cloned.1.call-update
  20.6 0.5 collective-permute-start.8
  21.1 0.1 collective-permute-start.9
  21.2 21.9 %all_to_all.20.in_ref = f32[16,72,128]{2,1,0:T(8,128)S(1)} all-to-all(f32[16,72,128]{2,1,0:T(8,128)S(1)} %get-tuple-element.25), channel_id=1, replica_groups=mesh['x'=4,'y'=4,'c'=2,'z'=4] {'x','y'}, dimensions={0} | all-to-all | bytes 1179648 | tf_op jit(solution)/shard_map/all_to_all | solution.py:400
  43.1 0.0 copy-done.2
  43.1 0.8 shard_map.58
  43.9 0.0 copy-start.3
  43.9 3.5 %all-to-all-start.1 = ((bf16[16,64,128]{2,1,0:T(8,128)(2,1)}), bf16[16,64,128]{2,1,0:T(8,128)(2,1)S(1)}, u32[]{:S(2)}, u32[]{:S(2)}) async-start(bf16[16,64,128]{2,1,0:T(8,128)(2,1)} %get-tuple-element.26), calls=%async_computation.1 | async-start | bytes 524288 | tf_op jit(solution)/shard_map/all_to_all | solution.py:400
  47.5 0.9 collective-permute-start.7
  48.4 2.1 %collective-permute-start.6 = (s32[8,1024]{1,0:T(8,128)S(1)}, s32[8,1024]{1,0:T(8,128)S(1)}, u32[]{:S(2)}, u32[]{:S(2)}) collective-permute-start(s32[8,1024]{1,0:T(8,128)S(1)} %get-tuple-element.27.rest_0_), channel_id=1, source_target_pairs={{0,2},{1,3},{2,0},{3,1},{4,6},{5,7},{6,4},{7,5},{8,10},{9,11},{10,... | collective-permute-start | bytes 98312 | tf_op jit(solution)/shard_map/ppermute | solution.py:407
  50.5 0.0 collective-permute-start.5
  50.5 0.0 collective-permute-done.7.rest_3_
  50.5 0.0 copy-start.7
  50.5 2.2 %collective-permute-done.6.rest_2_ = s32[8,1024]{1,0:T(8,128)S(1)} collective-permute-done((s32[8,1024]{1,0:T(8,128)S(1)}, s32[8,1024]{1,0:T(8,128)S(1)}, u32[]{:S(2)}, u32[]{:S(2)}) %collective-permute-start.6) | collective-permute-done | bytes 32800 | tf_op jit(solution)/shard_map/ppermute | solution.py:407
  52.7 0.0 copy-start.8
  52.7 2.1 %collective-permute-done.5.rest_1_ = s32[8,1024]{1,0:T(8,128)S(1)} collective-permute-done((s32[8,1024]{1,0:T(8,128)S(1)}, s32[8,1024]{1,0:T(8,128)S(1)}, u32[]{:S(2)}, u32[]{:S(2)}) %collective-permute-start.5) | collective-permute-done | bytes 32800 | tf_op jit(solution)/shard_map/ppermute | solution.py:407
  54.8 0.0 copy-start.9
  54.8 0.0 collective-permute-done.8.rest_5_
  54.8 0.0 copy-start.5
  54.8 0.0 collective-permute-done.9.rest_7_
  54.8 0.1 all-to-all-done.1
  54.9 0.0 copy-start.6
  54.9 0.0 copy-done.3
  54.9 0.0 copy-done.7
  54.9 0.0 copy-done.8
  54.9 0.5 copy-done.9
  55.4 0.4 copy-done.5
  55.8 0.1 copy-done.6
  55.9 7.0 %shard_map.59 = (bf16[16,80,128]{2,1,0:T(8,128)(2,1)}, s32[4,8,1024]{2,1,0:T(8,128)}) custom-call(s32[1]{0:T(128)} %bitcast.side_ref, bf16[4,256,128]{2,1,0:T(8,128)(2,1)} %bitcast.12, s32[8,1024]{1,0:T(8,128)} %copy-done.3, s32[8,1024]{1,0:T(8,128)} %copy-done.9, s32[8,1024]{1,0:T(8,128)} %copy-done.8, s32[8,1024]{1,0:T(8,128)} %copy-done.7, ...), custom_call_target="tpu_custom_call" | custom-call | tf_op jit(solution)/shard_map/pallas_call | solution.py:252
  62.9 0.0 copy-start.1
  62.9 16.4 %all_to_all.21.in_ref = bf16[16,80,128]{2,1,0:T(8,128)(2,1)S(1)} all-to-all(bf16[16,80,128]{2,1,0:T(8,128)(2,1)} %get-tuple-element.31), channel_id=1, replica_groups=mesh['x'=4,'y'=4,'c'=2,'z'=4] {'x','y'}, dimensions={0} | all-to-all | bytes 655360 | tf_op jit(solution)/shard_map/all_to_all | solution.py:400
  79.3 0.4 shard_map.60
  79.7 20.0 %all_to_all.22 = bf16[64,64,128]{2,1,0:T(8,128)(2,1)S(1)} all-to-all(bf16[64,64,128]{2,1,0:T(8,128)(2,1)S(1)} %shard_map.60), channel_id=1, replica_groups=mesh['x'=4,'y'=4,'c'=2,'z'=4] {'z','x','y'}, dimensions={0} | all-to-all | bytes 2097152 | tf_op jit(solution)/shard_map/all_to_all | solution.py:400
  99.6 5.2 %collective-permute-start.10 = (bf16[16,256,128]{2,1,0:T(8,128)(2,1)S(1)}, bf16[16,256,128]{2,1,0:T(8,128)(2,1)S(1)}, u32[]{:S(2)}, u32[]{:S(2)}) collective-permute-start(bf16[16,256,128]{2,1,0:T(8,128)(2,1)S(1)} %bitcast.6), channel_id=1, source_target_pairs={{0,4},{4,0},{1,5},{5,1},{2,6},{6,2},{3,7},{7,3},{8,12},{12,8},{9,1... | collective-permute-start | bytes 3145736 | tf_op jit(solution)/shard_map/ppermute | solution.py:396
  104.8 0.0 all-gather.3.cloned.1.call-done
  104.8 0.0 copy-done.1
  104.8 4.4 %shard_map.61.near_ref = bf16[4,1024,512]{2,1,0:T(8,128)(2,1)} custom-call(s32[1]{0:T(128)} %bitcast.side_ref, s32[1]{0:T(128)} %bitcast.1.z_ref, s32[4,8,1024]{2,1,0:T(8,128)S(1)} %copy-done.1, bf16[16,256,128]{2,1,0:T(8,128)(2,1)S(1)} %bitcast.7, bf16[4,8,1024,128]{3,2,1,0:T(8,128)(2,1)} %bitcast.10), custom_call_target="tpu_custom_call" | custom-call | tf_op jit(solution)/shard_map/pallas_call | solution.py:305
  109.2 0.0 collective-permute-done.10.table_ref
  109.2 16.9 %shard_map.62 = bf16[1024,1024]{1,0:T(8,128)(2,1)} custom-call(s32[1]{0:T(128)} %bitcast.side_ref, s32[1]{0:T(128)} %bitcast.1.z_ref, bf16[4,1024,512]{2,1,0:T(8,128)(2,1)} %shard_map.61.near_ref, s32[4,8,1024]{2,1,0:T(8,128)S(1)} %copy-done.1, bf16[16,256,128]{2,1,0:T(8,128)(2,1)S(1)} %collective-permute-done.10.table_ref, bf16[4,8,1024,128]{3,2,1,0:T(8,128)(2,1)} %bitcast.11), custom_call_target="tpu_custom_call" | custom-call | tf_op jit(solution)/shard_map/pallas_call | solution.py:378
Async XLA Ops:
  6.5 98.3 %all-gather.3.cloned.1.call-start = ((), (), s32[]{:S(2)}) async-start(), calls=%async_computation.4 | async-start | bytes 8650752 | tf_op jit(solution)/shard_map/all_gather | solution.py:428
  6.5 13.3 %collective-permute-start.4 = (bf16[1024,128]{1,0:T(8,128)(2,1)}, bf16[1024,128]{1,0:T(8,128)(2,1)}, u32[]{:S(2)}, u32[]{:S(2)}) collective-permute-start(bf16[1024,128]{1,0:T(8,128)(2,1)} %param.9), channel_id=1, source_target_pairs={{0,0},{1,96},{2,64},{3,32},{32,65},{33,33},{34,1},{35,97},{64,2},{... | collective-permute-start | bytes 786440 | tf_op jit(solution)/shard_map/ppermute | solution.py:420
  14.4 5.4 %collective-permute-start.1 = (f32[4,72,128]{2,1,0:T(8,128)}, f32[4,72,128]{2,1,0:T(8,128)S(1)}, u32[]{:S(2)}, u32[]{:S(2)}) collective-permute-start(f32[4,72,128]{2,1,0:T(8,128)} %get-tuple-element.21), channel_id=1, source_target_pairs={{0,4},{4,0},{1,5},{5,1},{2,6},{6,2},{3,7},{7,3},{8,12},{12,8},{9,1... | collective-permute-start | bytes 442376 | tf_op jit(solution)/shard_map/ppermute | solution.py:396
  15.9 3.9 %collective-permute-start.2 = (f32[4,72,128]{2,1,0:T(8,128)}, f32[4,72,128]{2,1,0:T(8,128)S(1)}, u32[]{:S(2)}, u32[]{:S(2)}) collective-permute-start(f32[4,72,128]{2,1,0:T(8,128)} %get-tuple-element.22), channel_id=1, source_target_pairs={{0,4},{4,0},{1,5},{5,1},{2,6},{6,2},{3,7},{7,3},{8,12},{12,8},{9,1... | collective-permute-start | bytes 442376 | tf_op jit(solution)/shard_map/ppermute | solution.py:396
  16.0 3.8 %collective-permute-start.3 = (f32[4,72,128]{2,1,0:T(8,128)}, f32[4,72,128]{2,1,0:T(8,128)S(1)}, u32[]{:S(2)}, u32[]{:S(2)}) collective-permute-start(f32[4,72,128]{2,1,0:T(8,128)} %get-tuple-element.23), channel_id=1, source_target_pairs={{0,4},{4,0},{1,5},{5,1},{2,6},{6,2},{3,7},{7,3},{8,12},{12,8},{9,1... | collective-permute-start | bytes 442376 | tf_op jit(solution)/shard_map/ppermute | solution.py:396
  16.4 3.5 %copy-start = (f32[16,72,128]{2,1,0:T(8,128)S(1)}, f32[16,72,128]{2,1,0:T(8,128)}, u32[]{:S(2)}) copy-start(f32[16,72,128]{2,1,0:T(8,128)} %get-tuple-element.19.a_ref) | copy-start | bytes 1769476
  16.4 3.4 %collective-permute-start = (f32[4,72,128]{2,1,0:T(8,128)}, f32[4,72,128]{2,1,0:T(8,128)S(1)}, u32[]{:S(2)}, u32[]{:S(2)}) collective-permute-start(f32[4,72,128]{2,1,0:T(8,128)} %get-tuple-element.20.after_ref), channel_id=1, source_target_pairs={{0,4},{4,0},{1,5},{5,1},{2,6},{6,2},{3,7},{7,3},{8,12},{12,8},{9,1... | collective-permute-start | bytes 442376 | tf_op jit(solution)/shard_map/ppermute | solution.py:396
  19.8 23.3 %copy-start.2 = (s32[1024,8]{0,1:T(8,128)S(1)}, s32[1024,8]{0,1:T(8,128)}, u32[]{:S(2)}) copy-start(s32[1024,8]{0,1:T(8,128)} %param.8) | copy-start | bytes 98308
  19.9 0.7 copy-start.4
  20.6 34.1 %collective-permute-start.8 = (bf16[1024,512]{1,0:T(8,128)(2,1)}, bf16[1024,512]{1,0:T(8,128)(2,1)S(1)}, u32[]{:S(2)}, u32[]{:S(2)}) collective-permute-start(bf16[1024,512]{1,0:T(8,128)(2,1)} %get-tuple-element.28), channel_id=1, source_target_pairs={{0,4},{4,0},{1,5},{5,1},{2,6},{6,2},{3,7},{7,3},{8,12},{12,8},{9,1... | collective-permute-start | bytes 3145736 | tf_op jit(solution)/shard_map/ppermute | solution.py:396
  21.1 33.7 %collective-permute-start.9 = (bf16[1024,512]{1,0:T(8,128)(2,1)}, bf16[1024,512]{1,0:T(8,128)(2,1)}, u32[]{:S(2)}, u32[]{:S(2)}) collective-permute-start(bf16[1024,512]{1,0:T(8,128)(2,1)} %get-tuple-element.29), channel_id=1, source_target_pairs={{0,4},{4,0},{1,5},{5,1},{2,6},{6,2},{3,7},{7,3},{8,12},{12,8},{9,1... | collective-permute-start | bytes 3145736 | tf_op jit(solution)/shard_map/ppermute | solution.py:396
  43.9 11.0 %copy-start.3 = (s32[8,1024]{1,0:T(8,128)}, s32[8,1024]{1,0:T(8,128)S(1)}, u32[]{:S(2)}) copy-start(s32[8,1024]{1,0:T(8,128)S(1)} %get-tuple-element.27.rest_0_) | copy-start | bytes 98308
  43.9 11.0 %all-to-all-start.1 = ((bf16[16,64,128]{2,1,0:T(8,128)(2,1)}), bf16[16,64,128]{2,1,0:T(8,128)(2,1)S(1)}, u32[]{:S(2)}, u32[]{:S(2)}) async-start(bf16[16,64,128]{2,1,0:T(8,128)(2,1)} %get-tuple-element.26), calls=%async_computation.1 | async-start | bytes 524288 | tf_op jit(solution)/shard_map/all_to_all | solution.py:400
  47.5 3.0 %collective-permute-start.7 = (s32[8,1024]{1,0:T(8,128)S(1)}, s32[8,1024]{1,0:T(8,128)S(1)}, u32[]{:S(2)}, u32[]{:S(2)}) collective-permute-start(s32[8,1024]{1,0:T(8,128)S(1)} %get-tuple-element.27.rest_0_), channel_id=1, source_target_pairs={{0,3},{1,0},{2,1},{3,2},{4,7},{5,4},{6,5},{7,6},{8,11},{9,8},{10,9... | collective-permute-start | bytes 98312 | tf_op jit(solution)/shard_map/ppermute | solution.py:407
  48.4 4.3 %collective-permute-start.6 = (s32[8,1024]{1,0:T(8,128)S(1)}, s32[8,1024]{1,0:T(8,128)S(1)}, u32[]{:S(2)}, u32[]{:S(2)}) collective-permute-start(s32[8,1024]{1,0:T(8,128)S(1)} %get-tuple-element.27.rest_0_), channel_id=1, source_target_pairs={{0,2},{1,3},{2,0},{3,1},{4,6},{5,7},{6,4},{7,5},{8,10},{9,11},{10,... | collective-permute-start | bytes 98312 | tf_op jit(solution)/shard_map/ppermute | solution.py:407
  50.5 4.3 %collective-permute-start.5 = (s32[8,1024]{1,0:T(8,128)S(1)}, s32[8,1024]{1,0:T(8,128)S(1)}, u32[]{:S(2)}, u32[]{:S(2)}) collective-permute-start(s32[8,1024]{1,0:T(8,128)S(1)} %get-tuple-element.27.rest_0_), channel_id=1, source_target_pairs={{0,1},{1,2},{2,3},{3,0},{4,5},{5,6},{6,7},{7,4},{8,9},{9,10},{10,1... | collective-permute-start | bytes 98312 | tf_op jit(solution)/shard_map/ppermute | solution.py:407
  50.5 4.4 %copy-start.7 = (s32[8,1024]{1,0:T(8,128)}, s32[8,1024]{1,0:T(8,128)S(1)}, u32[]{:S(2)}) copy-start(s32[8,1024]{1,0:T(8,128)S(1)} %collective-permute-done.7.rest_3_) | copy-start | bytes 98308
  52.7 2.2 %copy-start.8 = (s32[8,1024]{1,0:T(8,128)}, s32[8,1024]{1,0:T(8,128)S(1)}, u32[]{:S(2)}) copy-start(s32[8,1024]{1,0:T(8,128)S(1)} %collective-permute-done.6.rest_2_) | copy-start | bytes 98308
  54.8 0.6 copy-start.9
  54.8 1.0 copy-start.5
  54.9 1.0 copy-start.6
  62.9 42.0 %copy-start.1 = (s32[4,8,1024]{2,1,0:T(8,128)S(1)}, s32[4,8,1024]{2,1,0:T(8,128)}, u32[]{:S(2)}) copy-start(s32[4,8,1024]{2,1,0:T(8,128)} %get-tuple-element.30.ids_ref) | copy-start | bytes 393220
  99.6 9.6 %collective-permute-start.10 = (bf16[16,256,128]{2,1,0:T(8,128)(2,1)S(1)}, bf16[16,256,128]{2,1,0:T(8,128)(2,1)S(1)}, u32[]{:S(2)}, u32[]{:S(2)}) collective-permute-start(bf16[16,256,128]{2,1,0:T(8,128)(2,1)S(1)} %bitcast.6), channel_id=1, source_target_pairs={{0,4},{4,0},{1,5},{5,1},{2,6},{6,2},{3,7},{7,3},{8,12},{12,8},{9,1... | collective-permute-start | bytes 3145736 | tf_op jit(solution)/shard_map/ppermute | solution.py:396
Sparse Core Ops, SparseCore 0:
  20.8 58.4 all-gather.2

commit v6 on v5

--- a/solution.py
+++ b/solution.py
@@ -78,6 +78,7 @@
 
 SCALARS = pl.BlockSpec(memory_space=pltpu.SMEM)
 IN_VMEM = pl.BlockSpec(memory_space=pltpu.VMEM)
+ANYWHERE = pl.BlockSpec(memory_space=pl.ANY)
 IN_HBM = pl.BlockSpec(memory_space=pltpu.HBM)
 
 
@@ -142,28 +143,31 @@
 
 
 def add_kernel(a_ref, *rest):
-    out_ref = rest[PIECES + 2]
+    ids_ref, out_ref, ids_out_ref = rest[PIECES + 2], rest[PIECES + 3], rest[PIECES + 5]
+    ids_out_ref[...] = ids_ref[...]
     size = a_ref.shape[0] // PIECES
     for k in range(PIECES):
         lines = slice(k * size, (k + 1) * size)
         out_ref[lines] = a_ref[lines] + rest[k][...]
 
 
-def add_after(a, b, passed, after):
+def add_after(a, b, passed, after, ids):
     return pl.pallas_call(
         add_kernel,
         out_shape=(
             jax.ShapeDtypeStruct(a.shape, a.dtype),
             jax.ShapeDtypeStruct(passed.shape, passed.dtype),
+            jax.ShapeDtypeStruct(ids.shape, ids.dtype),
         ),
-        in_specs=[IN_VMEM] * (PIECES + 1) + [IN_HBM, IN_HBM],
-        out_specs=(IN_VMEM, IN_HBM),
+        in_specs=[IN_VMEM] * (PIECES + 1) + [IN_HBM, IN_HBM, IN_VMEM],
+        out_specs=(IN_VMEM, IN_HBM, IN_VMEM),
         input_output_aliases={PIECES + 1: 1},
         compiler_params=params(8),
-    )(a, *b, passed, after)
-
-
-def centre_kernel(in_ref, ids_ref, out_ref, ids_out_ref):
+    )(a, *b, passed, after, ids)
+
+
+def centre_kernel(in_ref, *rest):
+    out_ref = rest[-1]
     whole = in_ref[0]
     for k in range(1, in_ref.shape[0]):
         whole += in_ref[k]
@@ -172,18 +176,16 @@
     centre = (whole[:QUARTER] / count).astype(BF16)
     for k in range(out_ref.shape[0]):
         out_ref[k] = centre
-    ids_out_ref[...] = ids_ref[...]
-
-
-def centre_of(totals, ids):
+
+
+def centre_of(totals, after):
     return pl.pallas_call(
         centre_kernel,
-        out_shape=(
-            jax.ShapeDtypeStruct((totals.shape[0], QUARTER, HDIM), BF16),
-            jax.ShapeDtypeStruct(ids.shape, ids.dtype),
-        ),
+        out_shape=jax.ShapeDtypeStruct((totals.shape[0], QUARTER, HDIM), BF16),
+        in_specs=[IN_VMEM] + [ANYWHERE] * len(after),
+        out_specs=IN_VMEM,
         compiler_params=params(8),
-    )(totals, ids)
+    )(totals, *after)
 
 
 def attention_kernel(groups, side_ref, centre_ref, *rest):
@@ -197,7 +199,7 @@
             source = source.at[:, pl.ds(pl.multiple_of(first * HDIM, HALF * HDIM), HALF * HDIM)]
         return pltpu.make_async_copy(source, held.at[k], arrived.at[k])
 
-    for k in range(4):
+    for k in range(2):
         fetch(k).start()
     copies = [
         pltpu.make_async_copy(ids_refs[d], ids_out_ref.at[d], copied.at[d]) for d in range(groups)
@@ -209,8 +211,10 @@
     line = lax.broadcasted_iota(jnp.int32, (TAIL, HDIM), 0)
     for i in range(HALF):
         if i == 0:
-            fetch(0).wait()
-            fetch(1).wait()
+            for k in range(2):
+                fetch(k).wait()
+            for k in range(2, 4):
+                fetch(k).start()
         cols = slice(i * HDIM, (i + 1) * HDIM)
         centre = centre_ref[i]
         own = lax.dot_general(centre, held[0, :, cols], NT, preferred_element_type=F32)
@@ -221,8 +225,8 @@
         own_w = jnp.exp2((own - peak) * LOG2_SCALE).astype(BF16)
         other_w = jnp.exp2((other - peak) * LOG2_SCALE).astype(BF16)
         if i == 0:
-            fetch(2).wait()
-            fetch(3).wait()
+            for k in range(2, 4):
+                fetch(k).wait()
         both = jnp.dot(
             own_w, jnp.concatenate([held[2, :, cols], ones], axis=1), preferred_element_type=F32
         ) + jnp.dot(
@@ -255,14 +259,14 @@
             jax.ShapeDtypeStruct((4 * HALF, QUARTER + TAIL, HDIM), BF16),
             jax.ShapeDtypeStruct((groups, *all_ids[0].shape), jnp.int32),
         ),
-        in_specs=[SCALARS, IN_VMEM] + [IN_HBM] * groups + [IN_HBM] * 4,
+        in_specs=[SCALARS, IN_VMEM] + [IN_HBM] * (groups + 4),
         out_specs=(IN_VMEM, IN_VMEM),
         scratch_shapes=[
             pltpu.VMEM((4, rows, HALF * HDIM), BF16),
             pltpu.SemaphoreType.DMA((4,)),
             pltpu.SemaphoreType.DMA((groups,)),
         ],
-        compiler_params=params(LARGE),
+        compiler_params=params(52),
     )(side, centre, *all_ids, keys, keys_other, values, values_other)
 
 
@@ -313,79 +317,69 @@
 
 
 def project_kernel(
-    side_ref,
-    z_ref,
-    near_ref,
-    ids_ref,
-    table_ref,
-    w_ref,
-    out_ref,
-    held,
-    near,
-    far,
-    acc,
-    arrived,
-    come,
+    side_ref, z_ref, near_ref, ids_ref, table_ref, w_ref, out_ref, held, rows_ref, arrived, come
 ):
     groups, blocks = w_ref.shape[:2]
-    depth = HALF * HDIM
+    half = HALF * HDIM
+    depth = 2 * half
+    width = out_ref.shape[1] // 2
+    own = pl.multiple_of(side_ref[0] * half, half)
+    other = pl.multiple_of(half - side_ref[0] * half, half)
 
     def fetch(i):
-        group = group_at(lax.rem(i, groups), z_ref, groups)
-        entry = lax.rem(2 * z_ref[0] + groups - group, groups)
-        side = jnp.where(i < groups, side_ref[0], 1 - side_ref[0])
-        lines = pl.ds(pl.multiple_of(side * depth, depth), depth)
-        return pltpu.make_async_copy(w_ref.at[entry, :, lines, :], held.at[i], arrived.at[i])
-
-    def weight(i):
-        return jnp.concatenate([held[i, k] for k in range(blocks)], axis=1)
+        entry = lax.rem(z_ref[0] + i, groups)
+        return pltpu.make_async_copy(w_ref.at[entry], held.at[i], arrived.at[i])
 
     def bring(i):
-        return pltpu.make_async_copy(near_ref.at[i], near.at[i], come.at[i])
+        target = rows_ref.at[:, pl.ds(i * depth + own, half)]
+        return pltpu.make_async_copy(near_ref.at[i], target, come.at[i])
 
     for i in range(groups):
+        bring(i).start()
         fetch(i).start()
-        bring(i).start()
-    for i in range(groups, 2 * groups):
-        fetch(i).start()
-    fetch(0).wait()
-    bring(0).wait()
-    acc[...] = jnp.dot(near[0], weight(0), preferred_element_type=F32)
-
-    @pl.loop(1, groups)
+
+    @pl.loop(0, groups)
     def _(i):
+        group = group_at(i, z_ref, groups)
+        for j in range(HALF):
+            row = ids_ref[i, pl.ds((1 - side_ref[0]) * HALF + j, 1), :]
+            start = pl.multiple_of(i * depth + other + j * HDIM, HDIM)
+            rows_ref[:, pl.ds(start, HDIM)] = rows_of(row, table_ref[group * HALF + j])
+
+    for i in range(groups):
+        bring(i).wait()
         fetch(i).wait()
-        bring(i).wait()
-        acc[...] += jnp.dot(near[i], weight(i), preferred_element_type=F32)
-
-    @pl.loop(groups, 2 * groups)
-    def _(i):
-        group = group_at(i - groups, z_ref, groups)
-        for j in range(HALF):
-            row = ids_ref[i - groups, pl.ds((1 - side_ref[0]) * HALF + j, 1), :]
-            far[:, j * HDIM : (j + 1) * HDIM] = rows_of(row, table_ref[group * HALF + j])
-        fetch(i).wait()
-        acc[...] += jnp.dot(far[...], weight(i), preferred_element_type=F32)
-
-    out_ref[...] = acc[...].astype(BF16)
+
+    @pl.loop(0, 2)
+    def _(b):
+        each = blocks // 2
+        weight = jnp.concatenate(
+            [
+                jnp.concatenate([held[i, b * each + k] for k in range(each)], axis=1)
+                for i in range(groups)
+            ],
+            axis=0,
+        )
+        cols = pl.ds(pl.multiple_of(b * width, width), width)
+        tall = out_ref.shape[0] // 2
+        for m in range(2):
+            lines = slice(m * tall, (m + 1) * tall)
+            product = jnp.dot(rows_ref[lines, :], weight, preferred_element_type=F32)
+            out_ref[lines, cols] = product.astype(BF16)
 
 
 def project_of(side, z, near, ids, table, weight):
     groups, lines, tokens = ids.shape
-    depth = HALF * HDIM
-    blocks, width = weight.shape[1], weight.shape[3]
-    cols = blocks * width
+    blocks, depth, width = weight.shape[1:]
     return pl.pallas_call(
         project_kernel,
-        out_shape=jax.ShapeDtypeStruct((tokens, cols), BF16),
+        out_shape=jax.ShapeDtypeStruct((tokens, blocks * width), BF16),
         in_specs=[SCALARS, SCALARS, IN_HBM, IN_VMEM, IN_VMEM, IN_HBM],
         out_specs=IN_VMEM,
         scratch_shapes=[
-            pltpu.VMEM((2 * groups, blocks, depth, width), BF16),
-            pltpu.VMEM((groups, tokens, depth), BF16),
-            pltpu.VMEM((tokens, depth), BF16),
-            pltpu.VMEM((tokens, cols), F32),
-            pltpu.SemaphoreType.DMA((2 * groups,)),
+            pltpu.VMEM(weight.shape, BF16),
+            pltpu.VMEM((tokens, groups * depth), BF16),
+            pltpu.SemaphoreType.DMA((groups,)),
             pltpu.SemaphoreType.DMA((groups,)),
         ],
         compiler_params=params(51),
@@ -423,11 +417,11 @@
     arrived = [other_core(piece) for piece in theirs]
     keys_far, values_far, token = halves_of(side, theirs[0], keys, values)
     keys_other, values_other = other_core(keys_far), other_core(values_far)
-    totals, turned_weight = add_after(mine, arrived, turned_weight, token)
-    centre, ids = centre_of(exchanged(totals, PLANE), ids)
+    totals, turned_weight, ids = add_after(mine, arrived, turned_weight, token, ids)
     weight = lax.all_gather(turned_weight, SEQ, axis=0)
     weight = weight.reshape(size, -1, *weight.shape[1:])
     all_ids = from_all_groups(ids)
+    centre = centre_of(exchanged(totals, PLANE), all_ids[1:])
     centre = exchanged(centre, PLANE).reshape(HALF, CLUSTERS, HDIM)
     parts, all_ids = attention_of(
         side, centre, all_ids, keys, keys_other, values, values_other

time: 134 us -> 128 us (0.955)
  blocking collectives: 58.2 us -> 33.7 us
  starting transfers between devices: 18 us -> 29.7 us
  waiting for transfers between devices: 4.4 us -> 15.4 us
  Pallas kernels: 37.2 us -> 34.6 us
    all_to_all x3 -> x2, blocking collectives: 58.2 us -> 33.7 us  [exchanged(): return lax.all_to_all(value, axes, split_axis=0, concat_axis=0, tiled=True)]
    all_to_all x1 -> x2, waiting for transfers between devices: 0.1 us -> 11.1 us  [exchanged(): return lax.all_to_all(value, axes, split_axis=0, concat_axis=0, tiled=True)]
    all_to_all x1 -> x2, starting transfers between devices: 3.53 us -> 14.4 us  [exchanged(): return lax.all_to_all(value, axes, split_axis=0, concat_axis=0, tiled=True)]
    pallas_call x2, Pallas kernels: 17.8 us -> 15.9 us  [the longest x1 15 us: project_of(): pl.pallas_call(project_kernel, out_shape=jax.ShapeDtypeStruct((tokens, bl...]
    pallas_call x1, Pallas kernels: 7 us -> 5.5 us  [attention_of(): pl.pallas_call(functools.partial(attention_kernel, groups), out_shape=(ja...]
  transfers between devices with their start and end apart: 13 -> 14, of which waited for: 3 -> 4; matrix products, arithmetic and copies ran while one was open for 0% -> 0% of each run, Pallas kernels for 15% -> 15%
where the time goes in v6:
time: 128 us
  Pallas kernels  34.6 us (27%)
  blocking collectives  33.7 us (26%)
  starting transfers between devices  29.7 us (23%)
  waiting for transfers between devices  15.4 us (12%)
  between operations  13.6 us (11%)
    all_to_all x2, blocking collectives, exchanged(): return lax.all_to_all(value, axes, split_axis=0, concat_axis=0, tiled=True)  33.7 us
    pallas_call x1, Pallas kernels, project_of(): pl.pallas_call(project_kernel, out_shape=jax.ShapeDtypeStruct((tokens, bl...  15 us
    all_to_all x2, starting transfers between devices, exchanged(): return lax.all_to_all(value, axes, split_axis=0, concat_axis=0, tiled=True)  14.4 us
    all_to_all x2, waiting for transfers between devices, exchanged(): return lax.all_to_all(value, axes, split_axis=0, concat_axis=0, tiled=True)  11.1 us
    ppermute x7, starting transfers between devices, other_core(): return lax.ppermute(value, 'c', [(0, 1), (1, 0)])  8.76 us
    pallas_call x1, Pallas kernels, attention_of(): pl.pallas_call(functools.partial(attention_kernel, groups), out_shape=(ja...  5.5 us
    pallas_call x1, Pallas kernels, gather_of(): pl.pallas_call(gather_kernel, out_shape=jax.ShapeDtypeStruct((groups, tok...  4.41 us
    pallas_call x1, Pallas kernels, totals_of(): pl.pallas_call(totals_kernel, out_shape=[jax.ShapeDtypeStruct((4 * HALF /...  4.31 us
  transfers between devices with their start and end apart: 14, of which 4 were waited for; matrix products, arithmetic and copies ran while one was open for 0% of the time, Pallas kernels for 15%

profile of v6, /device:TPU:1, one launch (start us, length us, event | category | flops | bytes accessed | tf_op | source)
XLA Modules:
  0.0 127.8 jit_solution(690755791541671674)
XLA Ops:
  6.5 0.0 all-gather.3.cloned.1.call-start
  6.5 3.6 %collective-permute-start.4 = (bf16[1024,128]{1,0:T(8,128)(2,1)}, bf16[1024,128]{1,0:T(8,128)(2,1)}, u32[]{:S(2)}, u32[]{:S(2)}) collective-permute-start(bf16[1024,128]{1,0:T(8,128)(2,1)} %param.9), channel_id=1, source_target_pairs={{0,0},{1,96},{2,64},{3,32},{32,65},{33,33},{34,1},{35,97},{64,2},{... | collective-permute-start | bytes 786440 | tf_op jit(solution)/shard_map/ppermute | solution.py:414
  10.1 4.3 %shard_map.55 = (f32[4,72,128]{2,1,0:T(8,128)}, f32[4,72,128]{2,1,0:T(8,128)}, f32[4,72,128]{2,1,0:T(8,128)}, f32[4,72,128]{2,1,0:T(8,128)}, f32[16,72,128]{2,1,0:T(8,128)}) custom-call(s32[1]{0:T(128)} %bitcast.side_ref, s32[8,1024]{1,0:T(8,128)} %bitcast.9, bf16[1024,1024]{1,0:T(8,128)(2,1)} %q_ref.1), custom_call_target="tpu_custom_call" | custom-call | tf_op jit(solution)/shard_map/pallas_call | solution.py:87
  14.4 1.5 %collective-permute-start.1 = (f32[4,72,128]{2,1,0:T(8,128)}, f32[4,72,128]{2,1,0:T(8,128)S(1)}, u32[]{:S(2)}, u32[]{:S(2)}) collective-permute-start(f32[4,72,128]{2,1,0:T(8,128)} %get-tuple-element.20), channel_id=1, source_target_pairs={{0,4},{4,0},{1,5},{5,1},{2,6},{6,2},{3,7},{7,3},{8,12},{12,8},{9,1... | collective-permute-start | bytes 442376 | tf_op jit(solution)/shard_map/ppermute | solution.py:390
  15.9 0.1 collective-permute-start.2
  16.0 0.4 collective-permute-start.3
  16.4 0.0 copy-start
  16.4 0.0 copy-start.1
  16.4 0.1 collective-permute-start
  16.5 3.3 %shard_map.56 = (bf16[1024,512]{1,0:T(8,128)(2,1)}, bf16[1024,512]{1,0:T(8,128)(2,1)}, f32[8,128]{1,0:T(8,128)}) custom-call(s32[1]{0:T(128)} %bitcast.side_ref, f32[4,72,128]{2,1,0:T(8,128)} %get-tuple-element.19.after_ref, bf16[1024,1024]{1,0:T(8,128)(2,1)} %rest_4_.1, bf16[1024,1024]{1,0:T(8,128)(2,1)} %rest_6_.1), custom_call_target="tpu_custom_call" | custom-call | tf_op jit(solution)/shard_map/pallas_call | solution.py:131
  19.9 0.0 collective-permute-done.1.rest_1_
  19.9 0.0 collective-permute-done.2.rest_2_
  19.9 0.0 collective-permute-done.3.rest_3_
  19.9 0.0 collective-permute-done.rest_0_
  19.9 0.0 collective-permute-done.4.rest_4_
  19.9 0.0 copy-done
  19.9 0.0 copy-done.1
  19.9 0.0 copy-start.2
  20.0 0.7 copy-done.2
  20.6 0.9 shard_map.57
  21.5 0.0 all-gather.3.cloned.1.call-update
  21.5 0.5 collective-permute-start.8
  22.0 0.1 collective-permute-start.9
  22.1 9.2 %all-to-all-start = ((f32[16,72,128]{2,1,0:T(8,128)}), f32[16,72,128]{2,1,0:T(8,128)S(1)}, u32[]{:S(2)}, u32[]{:S(2)}) async-start(f32[16,72,128]{2,1,0:T(8,128)} %get-tuple-element.24), calls=%async_computation | async-start | bytes 1179648 | tf_op jit(solution)/shard_map/all_to_all | solution.py:394
  31.3 1.7 %collective-permute-start.7 = (s32[8,1024]{1,0:T(8,128)S(1)}, s32[8,1024]{1,0:T(8,128)S(1)}, u32[]{:S(2)}, u32[]{:S(2)}) collective-permute-start(s32[8,1024]{1,0:T(8,128)S(1)} %get-tuple-element.25.rest_0_), channel_id=1, source_target_pairs={{0,3},{1,0},{2,1},{3,2},{4,7},{5,4},{6,5},{7,6},{8,11},{9,8},{10,9... | collective-permute-start | bytes 98312 | tf_op jit(solution)/shard_map/ppermute | solution.py:401
  33.0 1.3 %collective-permute-start.6 = (s32[8,1024]{1,0:T(8,128)S(1)}, s32[8,1024]{1,0:T(8,128)S(1)}, u32[]{:S(2)}, u32[]{:S(2)}) collective-permute-start(s32[8,1024]{1,0:T(8,128)S(1)} %get-tuple-element.25.rest_0_), channel_id=1, source_target_pairs={{0,2},{1,3},{2,0},{3,1},{4,6},{5,7},{6,4},{7,5},{8,10},{9,11},{10,... | collective-permute-start | bytes 98312 | tf_op jit(solution)/shard_map/ppermute | solution.py:401
  34.3 0.0 collective-permute-start.5
  34.3 0.0 collective-permute-done.7.rest_2_.rest_3_
  34.3 3.0 %collective-permute-done.6.rest_1_.rest_2_ = s32[8,1024]{1,0:T(8,128)S(1)} collective-permute-done((s32[8,1024]{1,0:T(8,128)S(1)}, s32[8,1024]{1,0:T(8,128)S(1)}, u32[]{:S(2)}, u32[]{:S(2)}) %collective-permute-start.6) | collective-permute-done | bytes 32800 | tf_op jit(solution)/shard_map/ppermute | solution.py:401
  37.3 1.3 %collective-permute-done.5.rest_0_.rest_1_ = s32[8,1024]{1,0:T(8,128)S(1)} collective-permute-done((s32[8,1024]{1,0:T(8,128)S(1)}, s32[8,1024]{1,0:T(8,128)S(1)}, u32[]{:S(2)}, u32[]{:S(2)}) %collective-permute-start.5) | collective-permute-done | bytes 32800 | tf_op jit(solution)/shard_map/ppermute | solution.py:401
  38.6 3.7 %all-to-all-done.in_ref = f32[16,72,128]{2,1,0:T(8,128)S(1)} async-done(((f32[16,72,128]{2,1,0:T(8,128)}), f32[16,72,128]{2,1,0:T(8,128)S(1)}, u32[]{:S(2)}, u32[]{:S(2)}) %all-to-all-start) | async-done | bytes 589856 | tf_op jit(solution)/shard_map/all_to_all | solution.py:394
  42.3 0.8 shard_map.58
  43.2 5.2 %all-to-all-start.1 = ((bf16[16,64,128]{2,1,0:T(8,128)(2,1)}), bf16[16,64,128]{2,1,0:T(8,128)(2,1)S(1)}, u32[]{:S(2)}, u32[]{:S(2)}) async-start(bf16[16,64,128]{2,1,0:T(8,128)(2,1)} %shard_map.58), calls=%async_computation.1 | async-start | bytes 524288 | tf_op jit(solution)/shard_map/all_to_all | solution.py:394
  48.4 0.0 collective-permute-done.8.rest_5_
  48.4 0.0 collective-permute-done.9.rest_7_
  48.4 0.0 copy-start.3
  48.4 7.4 %all-to-all-done.1 = bf16[16,64,128]{2,1,0:T(8,128)(2,1)S(1)} async-done(((bf16[16,64,128]{2,1,0:T(8,128)(2,1)}), bf16[16,64,128]{2,1,0:T(8,128)(2,1)S(1)}, u32[]{:S(2)}, u32[]{:S(2)}) %all-to-all-start.1) | async-done | bytes 262176 | tf_op jit(solution)/shard_map/all_to_all | solution.py:394
  55.8 0.0 copy-done.3
  55.8 5.5 %shard_map.59 = (bf16[16,80,128]{2,1,0:T(8,128)(2,1)S(1)}, s32[4,8,1024]{2,1,0:T(8,128)S(1)}) custom-call(s32[1]{0:T(128)} %bitcast.side_ref, bf16[4,256,128]{2,1,0:T(8,128)(2,1)S(1)} %bitcast.8, s32[8,1024]{1,0:T(8,128)S(1)} %get-tuple-element.25.rest_0_, s32[8,1024]{1,0:T(8,128)S(1)} %collective-permute-done.5.rest_0_.rest_1_, ...), custom_call_target="tpu_custom_call" | custom-call | tf_op jit(solution)/shard_map/pallas_call | solution.py:256
  61.3 13.3 %all_to_all.20.in_ref = bf16[16,80,128]{2,1,0:T(8,128)(2,1)S(1)} all-to-all(bf16[16,80,128]{2,1,0:T(8,128)(2,1)S(1)} %get-tuple-element.29), channel_id=1, replica_groups=mesh['x'=4,'y'=4,'c'=2,'z'=4] {'x','y'}, dimensions={0} | all-to-all | bytes 655360 | tf_op jit(solution)/shard_map/all_to_all | solution.py:394
  74.6 0.4 shard_map.60
  75.0 20.4 %all_to_all.21 = bf16[64,64,128]{2,1,0:T(8,128)(2,1)S(1)} all-to-all(bf16[64,64,128]{2,1,0:T(8,128)(2,1)S(1)} %shard_map.60), channel_id=1, replica_groups=mesh['x'=4,'y'=4,'c'=2,'z'=4] {'z','x','y'}, dimensions={0} | all-to-all | bytes 2097152 | tf_op jit(solution)/shard_map/all_to_all | solution.py:394
  95.4 6.1 %collective-permute-start.10 = (bf16[16,256,128]{2,1,0:T(8,128)(2,1)S(1)}, bf16[16,256,128]{2,1,0:T(8,128)(2,1)S(1)}, u32[]{:S(2)}, u32[]{:S(2)}) collective-permute-start(bf16[16,256,128]{2,1,0:T(8,128)(2,1)S(1)} %bitcast.6), channel_id=1, source_target_pairs={{0,4},{4,0},{1,5},{5,1},{2,6},{6,2},{3,7},{7,3},{8,12},{12,8},{9,1... | collective-permute-start | bytes 3145736 | tf_op jit(solution)/shard_map/ppermute | solution.py:390
  101.4 0.0 all-gather.3.cloned.1.call-done
  101.4 4.4 %shard_map.61.near_ref = bf16[4,1024,512]{2,1,0:T(8,128)(2,1)} custom-call(s32[1]{0:T(128)} %bitcast.side_ref, s32[1]{0:T(128)} %bitcast.1.z_ref, s32[4,8,1024]{2,1,0:T(8,128)S(1)} %get-tuple-element.28.ids_ref, bf16[16,256,128]{2,1,0:T(8,128)(2,1)S(1)} %bitcast.7, bf16[4,8,1024,128]{3,2,1,0:T(8,128)(2,1)} %bitcast.11), custom_call_target="tpu_custom_call" | custom-call | tf_op jit(solution)/shard_map/pallas_call | solution.py:309
  105.9 0.0 collective-permute-done.10.table_ref
  105.9 15.0 %shard_map.62 = bf16[1024,1024]{1,0:T(8,128)(2,1)} custom-call(s32[1]{0:T(128)} %bitcast.side_ref, s32[1]{0:T(128)} %bitcast.1.z_ref, bf16[4,1024,512]{2,1,0:T(8,128)(2,1)} %shard_map.61.near_ref, s32[4,8,1024]{2,1,0:T(8,128)S(1)} %get-tuple-element.28.ids_ref, bf16[16,256,128]{2,1,0:T(8,128)(2,1)S(1)} %collective-permute-done.10.table_ref, ...), custom_call_target="tpu_custom_call" | custom-call | tf_op jit(solution)/shard_map/pallas_call | solution.py:374
Async XLA Ops:
  6.5 94.9 %all-gather.3.cloned.1.call-start = ((), (), s32[]{:S(2)}) async-start(), calls=%async_computation.4 | async-start | bytes 8650752 | tf_op jit(solution)/shard_map/all_gather | solution.py:421
  6.5 13.4 %collective-permute-start.4 = (bf16[1024,128]{1,0:T(8,128)(2,1)}, bf16[1024,128]{1,0:T(8,128)(2,1)}, u32[]{:S(2)}, u32[]{:S(2)}) collective-permute-start(bf16[1024,128]{1,0:T(8,128)(2,1)} %param.9), channel_id=1, source_target_pairs={{0,0},{1,96},{2,64},{3,32},{32,65},{33,33},{34,1},{35,97},{64,2},{... | collective-permute-start | bytes 786440 | tf_op jit(solution)/shard_map/ppermute | solution.py:414
  14.4 5.4 %collective-permute-start.1 = (f32[4,72,128]{2,1,0:T(8,128)}, f32[4,72,128]{2,1,0:T(8,128)S(1)}, u32[]{:S(2)}, u32[]{:S(2)}) collective-permute-start(f32[4,72,128]{2,1,0:T(8,128)} %get-tuple-element.20), channel_id=1, source_target_pairs={{0,4},{4,0},{1,5},{5,1},{2,6},{6,2},{3,7},{7,3},{8,12},{12,8},{9,1... | collective-permute-start | bytes 442376 | tf_op jit(solution)/shard_map/ppermute | solution.py:390
  15.9 4.0 %collective-permute-start.2 = (f32[4,72,128]{2,1,0:T(8,128)}, f32[4,72,128]{2,1,0:T(8,128)S(1)}, u32[]{:S(2)}, u32[]{:S(2)}) collective-permute-start(f32[4,72,128]{2,1,0:T(8,128)} %get-tuple-element.21), channel_id=1, source_target_pairs={{0,4},{4,0},{1,5},{5,1},{2,6},{6,2},{3,7},{7,3},{8,12},{12,8},{9,1... | collective-permute-start | bytes 442376 | tf_op jit(solution)/shard_map/ppermute | solution.py:390
  16.0 3.9 %collective-permute-start.3 = (f32[4,72,128]{2,1,0:T(8,128)}, f32[4,72,128]{2,1,0:T(8,128)S(1)}, u32[]{:S(2)}, u32[]{:S(2)}) collective-permute-start(f32[4,72,128]{2,1,0:T(8,128)} %get-tuple-element.22), channel_id=1, source_target_pairs={{0,4},{4,0},{1,5},{5,1},{2,6},{6,2},{3,7},{7,3},{8,12},{12,8},{9,1... | collective-permute-start | bytes 442376 | tf_op jit(solution)/shard_map/ppermute | solution.py:390
  16.4 3.5 %copy-start = (f32[16,72,128]{2,1,0:T(8,128)S(1)}, f32[16,72,128]{2,1,0:T(8,128)}, u32[]{:S(2)}) copy-start(f32[16,72,128]{2,1,0:T(8,128)} %get-tuple-element.18.a_ref) | copy-start | bytes 1769476
  16.4 3.5 %copy-start.1 = (s32[1024,8]{0,1:T(8,128)S(1)}, s32[1024,8]{0,1:T(8,128)}, u32[]{:S(2)}) copy-start(s32[1024,8]{0,1:T(8,128)} %param.8) | copy-start | bytes 98308
  16.4 3.5 %collective-permute-start = (f32[4,72,128]{2,1,0:T(8,128)}, f32[4,72,128]{2,1,0:T(8,128)S(1)}, u32[]{:S(2)}, u32[]{:S(2)}) collective-permute-start(f32[4,72,128]{2,1,0:T(8,128)} %get-tuple-element.19.after_ref), channel_id=1, source_target_pairs={{0,4},{4,0},{1,5},{5,1},{2,6},{6,2},{3,7},{7,3},{8,12},{12,8},{9,1... | collective-permute-start | bytes 442376 | tf_op jit(solution)/shard_map/ppermute | solution.py:390
  19.9 0.7 copy-start.2
  21.5 26.8 %collective-permute-start.8 = (bf16[1024,512]{1,0:T(8,128)(2,1)}, bf16[1024,512]{1,0:T(8,128)(2,1)S(1)}, u32[]{:S(2)}, u32[]{:S(2)}) collective-permute-start(bf16[1024,512]{1,0:T(8,128)(2,1)} %get-tuple-element.26), channel_id=1, source_target_pairs={{0,4},{4,0},{1,5},{5,1},{2,6},{6,2},{3,7},{7,3},{8,12},{12,8},{9,1... | collective-permute-start | bytes 3145736 | tf_op jit(solution)/shard_map/ppermute | solution.py:390
  22.0 26.4 %collective-permute-start.9 = (bf16[1024,512]{1,0:T(8,128)(2,1)}, bf16[1024,512]{1,0:T(8,128)(2,1)S(1)}, u32[]{:S(2)}, u32[]{:S(2)}) collective-permute-start(bf16[1024,512]{1,0:T(8,128)(2,1)} %get-tuple-element.27), channel_id=1, source_target_pairs={{0,4},{4,0},{1,5},{5,1},{2,6},{6,2},{3,7},{7,3},{8,12},{12,8},{9,1... | collective-permute-start | bytes 3145736 | tf_op jit(solution)/shard_map/ppermute | solution.py:390
  22.1 20.2 %all-to-all-start = ((f32[16,72,128]{2,1,0:T(8,128)}), f32[16,72,128]{2,1,0:T(8,128)S(1)}, u32[]{:S(2)}, u32[]{:S(2)}) async-start(f32[16,72,128]{2,1,0:T(8,128)} %get-tuple-element.24), calls=%async_computation | async-start | bytes 1179648 | tf_op jit(solution)/shard_map/all_to_all | solution.py:394
  31.3 3.0 %collective-permute-start.7 = (s32[8,1024]{1,0:T(8,128)S(1)}, s32[8,1024]{1,0:T(8,128)S(1)}, u32[]{:S(2)}, u32[]{:S(2)}) collective-permute-start(s32[8,1024]{1,0:T(8,128)S(1)} %get-tuple-element.25.rest_0_), channel_id=1, source_target_pairs={{0,3},{1,0},{2,1},{3,2},{4,7},{5,4},{6,5},{7,6},{8,11},{9,8},{10,9... | collective-permute-start | bytes 98312 | tf_op jit(solution)/shard_map/ppermute | solution.py:401
  33.0 4.3 %collective-permute-start.6 = (s32[8,1024]{1,0:T(8,128)S(1)}, s32[8,1024]{1,0:T(8,128)S(1)}, u32[]{:S(2)}, u32[]{:S(2)}) collective-permute-start(s32[8,1024]{1,0:T(8,128)S(1)} %get-tuple-element.25.rest_0_), channel_id=1, source_target_pairs={{0,2},{1,3},{2,0},{3,1},{4,6},{5,7},{6,4},{7,5},{8,10},{9,11},{10,... | collective-permute-start | bytes 98312 | tf_op jit(solution)/shard_map/ppermute | solution.py:401
  34.3 4.3 %collective-permute-start.5 = (s32[8,1024]{1,0:T(8,128)S(1)}, s32[8,1024]{1,0:T(8,128)S(1)}, u32[]{:S(2)}, u32[]{:S(2)}) collective-permute-start(s32[8,1024]{1,0:T(8,128)S(1)} %get-tuple-element.25.rest_0_), channel_id=1, source_target_pairs={{0,1},{1,2},{2,3},{3,0},{4,5},{5,6},{6,7},{7,4},{8,9},{9,10},{10,1... | collective-permute-start | bytes 98312 | tf_op jit(solution)/shard_map/ppermute | solution.py:401
  43.2 12.6 %all-to-all-start.1 = ((bf16[16,64,128]{2,1,0:T(8,128)(2,1)}), bf16[16,64,128]{2,1,0:T(8,128)(2,1)S(1)}, u32[]{:S(2)}, u32[]{:S(2)}) async-start(bf16[16,64,128]{2,1,0:T(8,128)(2,1)} %shard_map.58), calls=%async_computation.1 | async-start | bytes 524288 | tf_op jit(solution)/shard_map/all_to_all | solution.py:394
  48.4 7.4 %copy-start.3 = (bf16[1024,512]{1,0:T(8,128)(2,1)}, bf16[1024,512]{1,0:T(8,128)(2,1)S(1)}, u32[]{:S(2)}) copy-start(bf16[1024,512]{1,0:T(8,128)(2,1)S(1)} %collective-permute-done.9.rest_7_) | copy-start | bytes 3145732
  95.4 10.5 %collective-permute-start.10 = (bf16[16,256,128]{2,1,0:T(8,128)(2,1)S(1)}, bf16[16,256,128]{2,1,0:T(8,128)(2,1)S(1)}, u32[]{:S(2)}, u32[]{:S(2)}) collective-permute-start(bf16[16,256,128]{2,1,0:T(8,128)(2,1)S(1)} %bitcast.6), channel_id=1, source_target_pairs={{0,4},{4,0},{1,5},{5,1},{2,6},{6,2},{3,7},{7,3},{8,12},{12,8},{9,1... | collective-permute-start | bytes 3145736 | tf_op jit(solution)/shard_map/ppermute | solution.py:390
Sparse Core Ops, SparseCore 0:
  21.6 60.6 all-gather.2

commit v7 on v6

--- a/solution.py
+++ b/solution.py
@@ -105,7 +105,7 @@
     side_ref, after_ref, k_ref, v_ref, k_out_ref, v_out_ref, token_ref, held, come, gone
 ):
     del after_ref
-    token_ref[...] = jnp.zeros(token_ref.shape, token_ref.dtype)
+    token_ref[0] = side_ref[0]
     start = pl.multiple_of((1 - side_ref[0]) * HALF * HDIM, HALF * HDIM)
 
     def fetch(k, source):
@@ -130,9 +130,9 @@
     half = jax.ShapeDtypeStruct((keys.shape[0], HALF * HDIM), BF16)
     return pl.pallas_call(
         halves_kernel,
-        out_shape=(half, half, jax.ShapeDtypeStruct((8, HDIM), F32)),
+        out_shape=(half, half, jax.ShapeDtypeStruct((1,), jnp.int32)),
         in_specs=[SCALARS, IN_HBM, IN_HBM, IN_HBM],
-        out_specs=(IN_HBM, IN_HBM, IN_VMEM),
+        out_specs=(IN_HBM, IN_HBM, SCALARS),
         scratch_shapes=[
             pltpu.VMEM((2, *half.shape), BF16),
             pltpu.SemaphoreType.DMA((2,)),
@@ -143,7 +143,7 @@
 
 
 def add_kernel(a_ref, *rest):
-    ids_ref, out_ref, ids_out_ref = rest[PIECES + 2], rest[PIECES + 3], rest[PIECES + 5]
+    ids_ref, out_ref, ids_out_ref = rest[PIECES + 1], rest[PIECES + 3], rest[PIECES + 5]
     ids_out_ref[...] = ids_ref[...]
     size = a_ref.shape[0] // PIECES
     for k in range(PIECES):
@@ -151,7 +151,7 @@
         out_ref[lines] = a_ref[lines] + rest[k][...]
 
 
-def add_after(a, b, passed, after, ids):
+def add_after(a, b, passed, ids, after):
     return pl.pallas_call(
         add_kernel,
         out_shape=(
@@ -159,15 +159,15 @@
             jax.ShapeDtypeStruct(passed.shape, passed.dtype),
             jax.ShapeDtypeStruct(ids.shape, ids.dtype),
         ),
-        in_specs=[IN_VMEM] * (PIECES + 1) + [IN_HBM, IN_HBM, IN_VMEM],
+        in_specs=[IN_VMEM] * (PIECES + 1) + [IN_HBM, IN_VMEM, SCALARS],
         out_specs=(IN_VMEM, IN_HBM, IN_VMEM),
         input_output_aliases={PIECES + 1: 1},
         compiler_params=params(8),
-    )(a, *b, passed, after, ids)
+    )(a, *b, passed, ids, after)
 
 
 def centre_kernel(in_ref, *rest):
-    out_ref = rest[-1]
+    out_ref = rest[-2]
     whole = in_ref[0]
     for k in range(1, in_ref.shape[0]):
         whole += in_ref[k]
@@ -178,14 +178,18 @@
         out_ref[k] = centre
 
 
-def centre_of(totals, after):
+def centre_of(totals, after, passed):
     return pl.pallas_call(
         centre_kernel,
-        out_shape=jax.ShapeDtypeStruct((totals.shape[0], QUARTER, HDIM), BF16),
-        in_specs=[IN_VMEM] + [ANYWHERE] * len(after),
-        out_specs=IN_VMEM,
+        out_shape=(
+            jax.ShapeDtypeStruct((totals.shape[0], QUARTER, HDIM), BF16),
+            jax.ShapeDtypeStruct(passed.shape, passed.dtype),
+        ),
+        in_specs=[IN_VMEM] + [ANYWHERE] * len(after) + [IN_HBM],
+        out_specs=(IN_VMEM, IN_HBM),
+        input_output_aliases={1 + len(after): 1},
         compiler_params=params(8),
-    )(totals, *after)
+    )(totals, *after, passed)
 
 
 def attention_kernel(groups, side_ref, centre_ref, *rest):
@@ -415,13 +419,13 @@
 
     *theirs, mine = totals_of(side, ids, queries)
     arrived = [other_core(piece) for piece in theirs]
-    keys_far, values_far, token = halves_of(side, theirs[0], keys, values)
+    keys_far, values_far, token = halves_of(side, mine, keys, values)
     keys_other, values_other = other_core(keys_far), other_core(values_far)
-    totals, turned_weight, ids = add_after(mine, arrived, turned_weight, token, ids)
+    totals, turned_weight, ids = add_after(mine, arrived, turned_weight, ids, token)
+    all_ids = from_all_groups(ids)
+    centre, turned_weight = centre_of(exchanged(totals, PLANE), all_ids[1:], turned_weight)
     weight = lax.all_gather(turned_weight, SEQ, axis=0)
     weight = weight.reshape(size, -1, *weight.shape[1:])
-    all_ids = from_all_groups(ids)
-    centre = centre_of(exchanged(totals, PLANE), all_ids[1:])
     centre = exchanged(centre, PLANE).reshape(HALF, CLUSTERS, HDIM)
     parts, all_ids = attention_of(
         side, centre, all_ids, keys, keys_other, values, values_other

time: 128 us -> 135 us (1.055)
  blocking collectives: 33.7 us -> 43.8 us
  starting transfers between devices: 29.7 us -> 26.2 us
    all_to_all x2, blocking collectives: 33.7 us -> 43.8 us  [exchanged(): return lax.all_to_all(value, axes, split_axis=0, concat_axis=0, tiled=True)]
    ppermute x7, starting transfers between devices: 8.76 us -> 6.83 us  [other_core(): return lax.ppermute(value, 'c', [(0, 1), (1, 0)])]
    all_to_all x2, starting transfers between devices: 14.4 us -> 12.7 us  [exchanged(): return lax.all_to_all(value, axes, split_axis=0, concat_axis=0, tiled=True)]
  transfers between devices with their start and end apart: 14 -> 14, of which waited for: 4 -> 5; matrix products, arithmetic and copies ran while one was open for 0% -> 0% of each run, Pallas kernels for 15% -> 13%
where the time goes in v7:
time: 135 us; the launch traced here: 134 us
  blocking collectives  43.8 us (32%)
  Pallas kernels  35.1 us (26%)
  starting transfers between devices  26.2 us (19%)
  waiting for transfers between devices  15.6 us (12%)
  between operations  13.5 us (10%)
    all_to_all x2, blocking collectives, exchanged(): return lax.all_to_all(value, axes, split_axis=0, concat_axis=0, tiled=True)  43.8 us
    pallas_call x1, Pallas kernels, project_of(): pl.pallas_call(project_kernel, out_shape=jax.ShapeDtypeStruct((tokens, bl...  15 us
    all_to_all x2, starting transfers between devices, exchanged(): return lax.all_to_all(value, axes, split_axis=0, concat_axis=0, tiled=True)  12.7 us
    all_to_all x2, waiting for transfers between devices, exchanged(): return lax.all_to_all(value, axes, split_axis=0, concat_axis=0, tiled=True)  10.9 us
    ppermute x7, starting transfers between devices, other_core(): return lax.ppermute(value, 'c', [(0, 1), (1, 0)])  6.83 us
    pallas_call x1, Pallas kernels, attention_of(): pl.pallas_call(functools.partial(attention_kernel, groups), out_shape=(ja...  5.42 us
    pallas_call x1, Pallas kernels, gather_of(): pl.pallas_call(gather_kernel, out_shape=jax.ShapeDtypeStruct((groups, tok...  4.41 us
    pallas_call x1, Pallas kernels, totals_of(): pl.pallas_call(totals_kernel, out_shape=[jax.ShapeDtypeStruct((4 * HALF /...  4.29 us
  transfers between devices with their start and end apart: 14, of which 5 were waited for; matrix products, arithmetic and copies ran while one was open for 0% of the time, Pallas kernels for 13%

profile of v7, /device:TPU:1, one launch (start us, length us, event | category | flops | bytes accessed | tf_op | source)
XLA Modules:
  0.0 134.2 jit_solution(13722774848760422511)
XLA Ops:
  6.5 3.6 %collective-permute-start.4 = (bf16[1024,128]{1,0:T(8,128)(2,1)}, bf16[1024,128]{1,0:T(8,128)(2,1)}, u32[]{:S(2)}, u32[]{:S(2)}) collective-permute-start(bf16[1024,128]{1,0:T(8,128)(2,1)} %param.9), channel_id=1, source_target_pairs={{0,0},{1,96},{2,64},{3,32},{32,65},{33,33},{34,1},{35,97},{64,2},{... | collective-permute-start | bytes 786440 | tf_op jit(solution)/shard_map/ppermute | solution.py:418
  10.1 4.3 %shard_map.55 = (f32[4,72,128]{2,1,0:T(8,128)}, f32[4,72,128]{2,1,0:T(8,128)}, f32[4,72,128]{2,1,0:T(8,128)}, f32[4,72,128]{2,1,0:T(8,128)}, f32[16,72,128]{2,1,0:T(8,128)}) custom-call(s32[1]{0:T(128)} %bitcast.side_ref, s32[8,1024]{1,0:T(8,128)} %bitcast.9, bf16[1024,1024]{1,0:T(8,128)(2,1)} %q_ref.1), custom_call_target="tpu_custom_call" | custom-call | tf_op jit(solution)/shard_map/pallas_call | solution.py:87
  14.4 1.5 %collective-permute-start = (f32[4,72,128]{2,1,0:T(8,128)}, f32[4,72,128]{2,1,0:T(8,128)S(1)}, u32[]{:S(2)}, u32[]{:S(2)}) collective-permute-start(f32[4,72,128]{2,1,0:T(8,128)} %get-tuple-element.21), channel_id=1, source_target_pairs={{0,4},{4,0},{1,5},{5,1},{2,6},{6,2},{3,7},{7,3},{8,12},{12,8},{9,1... | collective-permute-start | bytes 442376 | tf_op jit(solution)/shard_map/ppermute | solution.py:394
  15.9 0.1 collective-permute-start.1
  16.0 0.4 collective-permute-start.2
  16.4 0.1 collective-permute-start.3
  16.5 0.0 copy-start
  16.5 0.0 copy-start.1
  16.5 3.3 %shard_map.56 = (bf16[1024,512]{1,0:T(8,128)(2,1)}, bf16[1024,512]{1,0:T(8,128)(2,1)}, s32[1]{0:T(128)}) custom-call(s32[1]{0:T(128)} %bitcast.side_ref, f32[16,72,128]{2,1,0:T(8,128)} %get-tuple-element.20.after_ref.a_ref, bf16[1024,1024]{1,0:T(8,128)(2,1)} %rest_4_.1, bf16[1024,1024]{1,0:T(8,128)(2,1)} %rest_6_.1), custom_call_target="tpu_custom_call" | custom-call | tf_op jit(solution)/shard_map/pallas_call | solution.py:131
  19.8 0.0 collective-permute-done.rest_0_
  19.8 0.0 collective-permute-done.1.rest_1_
  19.8 0.0 collective-permute-done.2.rest_2_
  19.8 0.0 collective-permute-done.3.rest_3_
  19.8 0.0 collective-permute-done.4.rest_4_
  19.8 0.0 copy-done
  19.9 0.0 copy-done.1
  19.9 1.5 %shard_map.57 = (f32[16,72,128]{2,1,0:T(8,128)}, bf16[1024,128]{1,0:T(8,128)(2,1)}, s32[8,1024]{1,0:T(8,128)S(1)}) custom-call(f32[16,72,128]{2,1,0:T(8,128)S(1)} %copy-done, f32[4,72,128]{2,1,0:T(8,128)S(1)} %collective-permute-done.rest_0_, f32[4,72,128]{2,1,0:T(8,128)S(1)} %collective-permute-done.1.rest_1_, ...), custom_call_target="tpu_custom_call", output_to_operand_aliasing={{1}: (5, {})} | custom-call | tf_op jit(solution)/shard_map/pallas_call | solution.py:155
  21.4 9.2 %all-to-all-start = ((f32[16,72,128]{2,1,0:T(8,128)}), f32[16,72,128]{2,1,0:T(8,128)S(1)}, u32[]{:S(2)}, u32[]{:S(2)}) async-start(f32[16,72,128]{2,1,0:T(8,128)} %get-tuple-element.26), calls=%async_computation | async-start | bytes 1179648 | tf_op jit(solution)/shard_map/all_to_all | solution.py:398
  30.6 0.0 all-gather.3.cloned.1.call-start
  30.7 1.2 collective-permute-start.7
  31.9 1.8 %collective-permute-start.6 = (s32[8,1024]{1,0:T(8,128)S(1)}, s32[8,1024]{1,0:T(8,128)S(1)}, u32[]{:S(2)}, u32[]{:S(2)}) collective-permute-start(s32[8,1024]{1,0:T(8,128)S(1)} %get-tuple-element.27.rest_0_), channel_id=1, source_target_pairs={{0,2},{1,3},{2,0},{3,1},{4,6},{5,7},{6,4},{7,5},{8,10},{9,11},{10,... | collective-permute-start | bytes 98312 | tf_op jit(solution)/shard_map/ppermute | solution.py:405
  33.7 0.0 collective-permute-start.5
  33.7 0.0 collective-permute-done.7.rest_2_.rest_3_
  33.7 2.7 %collective-permute-done.6.rest_1_.rest_2_ = s32[8,1024]{1,0:T(8,128)S(1)} collective-permute-done((s32[8,1024]{1,0:T(8,128)S(1)}, s32[8,1024]{1,0:T(8,128)S(1)}, u32[]{:S(2)}, u32[]{:S(2)}) %collective-permute-start.6) | collective-permute-done | bytes 32800 | tf_op jit(solution)/shard_map/ppermute | solution.py:405
  36.4 1.5 %collective-permute-done.5.rest_0_.rest_1_ = s32[8,1024]{1,0:T(8,128)S(1)} collective-permute-done((s32[8,1024]{1,0:T(8,128)S(1)}, s32[8,1024]{1,0:T(8,128)S(1)}, u32[]{:S(2)}, u32[]{:S(2)}) %collective-permute-start.5) | collective-permute-done | bytes 32800 | tf_op jit(solution)/shard_map/ppermute | solution.py:405
  37.9 3.6 %all-to-all-done.in_ref = f32[16,72,128]{2,1,0:T(8,128)S(1)} async-done(((f32[16,72,128]{2,1,0:T(8,128)}), f32[16,72,128]{2,1,0:T(8,128)S(1)}, u32[]{:S(2)}, u32[]{:S(2)}) %all-to-all-start) | async-done | bytes 589856 | tf_op jit(solution)/shard_map/all_to_all | solution.py:398
  41.5 0.8 shard_map.58
  42.3 0.0 all-gather.3.cloned.1.call-update
  42.3 2.3 %collective-permute-start.8 = (bf16[1024,512]{1,0:T(8,128)(2,1)}, bf16[1024,512]{1,0:T(8,128)(2,1)S(1)}, u32[]{:S(2)}, u32[]{:S(2)}) collective-permute-start(bf16[1024,512]{1,0:T(8,128)(2,1)} %get-tuple-element.30), channel_id=1, source_target_pairs={{0,4},{4,0},{1,5},{5,1},{2,6},{6,2},{3,7},{7,3},{8,12},{12,8},{9,1... | collective-permute-start | bytes 3145736 | tf_op jit(solution)/shard_map/ppermute | solution.py:394
  44.7 0.1 collective-permute-start.9
  44.8 3.5 %all-to-all-start.1 = ((bf16[16,64,128]{2,1,0:T(8,128)(2,1)}), bf16[16,64,128]{2,1,0:T(8,128)(2,1)S(1)}, u32[]{:S(2)}, u32[]{:S(2)}) async-start(bf16[16,64,128]{2,1,0:T(8,128)(2,1)} %get-tuple-element.29), calls=%async_computation.1 | async-start | bytes 524288 | tf_op jit(solution)/shard_map/all_to_all | solution.py:398
  48.3 0.0 collective-permute-done.8.rest_5_
  48.3 0.4 collective-permute-done.9.rest_7_
  48.7 0.0 copy-start.2
  48.7 7.3 %all-to-all-done.1 = bf16[16,64,128]{2,1,0:T(8,128)(2,1)S(1)} async-done(((bf16[16,64,128]{2,1,0:T(8,128)(2,1)}), bf16[16,64,128]{2,1,0:T(8,128)(2,1)S(1)}, u32[]{:S(2)}, u32[]{:S(2)}) %all-to-all-start.1) | async-done | bytes 262176 | tf_op jit(solution)/shard_map/all_to_all | solution.py:398
  56.0 0.0 copy-done.2
  56.0 5.4 %shard_map.59 = (bf16[16,80,128]{2,1,0:T(8,128)(2,1)S(1)}, s32[4,8,1024]{2,1,0:T(8,128)S(1)}) custom-call(s32[1]{0:T(128)} %bitcast.side_ref, bf16[4,256,128]{2,1,0:T(8,128)(2,1)S(1)} %bitcast.8, s32[8,1024]{1,0:T(8,128)S(1)} %get-tuple-element.27.rest_0_, s32[8,1024]{1,0:T(8,128)S(1)} %collective-permute-done.5.rest_0_.rest_1_, ...), custom_call_target="tpu_custom_call" | custom-call | tf_op jit(solution)/shard_map/pallas_call | solution.py:260
  61.5 11.2 %all_to_all.20.in_ref = bf16[16,80,128]{2,1,0:T(8,128)(2,1)S(1)} all-to-all(bf16[16,80,128]{2,1,0:T(8,128)(2,1)S(1)} %get-tuple-element.33), channel_id=1, replica_groups=mesh['x'=4,'y'=4,'c'=2,'z'=4] {'x','y'}, dimensions={0} | all-to-all | bytes 655360 | tf_op jit(solution)/shard_map/all_to_all | solution.py:398
  72.7 0.4 shard_map.60
  73.0 32.6 %all_to_all.21 = bf16[64,64,128]{2,1,0:T(8,128)(2,1)S(1)} all-to-all(bf16[64,64,128]{2,1,0:T(8,128)(2,1)S(1)} %shard_map.60), channel_id=1, replica_groups=mesh['x'=4,'y'=4,'c'=2,'z'=4] {'z','x','y'}, dimensions={0} | all-to-all | bytes 2097152 | tf_op jit(solution)/shard_map/all_to_all | solution.py:398
  105.6 2.3 %collective-permute-start.10 = (bf16[16,256,128]{2,1,0:T(8,128)(2,1)S(1)}, bf16[16,256,128]{2,1,0:T(8,128)(2,1)S(1)}, u32[]{:S(2)}, u32[]{:S(2)}) collective-permute-start(bf16[16,256,128]{2,1,0:T(8,128)(2,1)S(1)} %bitcast.6), channel_id=1, source_target_pairs={{0,4},{4,0},{1,5},{5,1},{2,6},{6,2},{3,7},{7,3},{8,12},{12,8},{9,1... | collective-permute-start | bytes 3145736 | tf_op jit(solution)/shard_map/ppermute | solution.py:394
  107.9 0.0 all-gather.3.cloned.1.call-done
  107.9 4.4 %shard_map.61.near_ref = bf16[4,1024,512]{2,1,0:T(8,128)(2,1)} custom-call(s32[1]{0:T(128)} %bitcast.side_ref, s32[1]{0:T(128)} %bitcast.1.z_ref, s32[4,8,1024]{2,1,0:T(8,128)S(1)} %get-tuple-element.32.ids_ref, bf16[16,256,128]{2,1,0:T(8,128)(2,1)S(1)} %bitcast.7, bf16[4,8,1024,128]{3,2,1,0:T(8,128)(2,1)} %bitcast.11), custom_call_target="tpu_custom_call" | custom-call | tf_op jit(solution)/shard_map/pallas_call | solution.py:313
  112.3 0.0 collective-permute-done.10.table_ref
  112.3 15.0 %shard_map.62 = bf16[1024,1024]{1,0:T(8,128)(2,1)} custom-call(s32[1]{0:T(128)} %bitcast.side_ref, s32[1]{0:T(128)} %bitcast.1.z_ref, bf16[4,1024,512]{2,1,0:T(8,128)(2,1)} %shard_map.61.near_ref, s32[4,8,1024]{2,1,0:T(8,128)S(1)} %get-tuple-element.32.ids_ref, bf16[16,256,128]{2,1,0:T(8,128)(2,1)S(1)} %collective-permute-done.10.table_ref, ...), custom_call_target="tpu_custom_call" | custom-call | tf_op jit(solution)/shard_map/pallas_call | solution.py:378
Async XLA Ops:
  6.5 13.3 %collective-permute-start.4 = (bf16[1024,128]{1,0:T(8,128)(2,1)}, bf16[1024,128]{1,0:T(8,128)(2,1)}, u32[]{:S(2)}, u32[]{:S(2)}) collective-permute-start(bf16[1024,128]{1,0:T(8,128)(2,1)} %param.9), channel_id=1, source_target_pairs={{0,0},{1,96},{2,64},{3,32},{32,65},{33,33},{34,1},{35,97},{64,2},{... | collective-permute-start | bytes 786440 | tf_op jit(solution)/shard_map/ppermute | solution.py:418
  14.4 5.4 %collective-permute-start = (f32[4,72,128]{2,1,0:T(8,128)}, f32[4,72,128]{2,1,0:T(8,128)S(1)}, u32[]{:S(2)}, u32[]{:S(2)}) collective-permute-start(f32[4,72,128]{2,1,0:T(8,128)} %get-tuple-element.21), channel_id=1, source_target_pairs={{0,4},{4,0},{1,5},{5,1},{2,6},{6,2},{3,7},{7,3},{8,12},{12,8},{9,1... | collective-permute-start | bytes 442376 | tf_op jit(solution)/shard_map/ppermute | solution.py:394
  15.9 3.9 %collective-permute-start.1 = (f32[4,72,128]{2,1,0:T(8,128)}, f32[4,72,128]{2,1,0:T(8,128)S(1)}, u32[]{:S(2)}, u32[]{:S(2)}) collective-permute-start(f32[4,72,128]{2,1,0:T(8,128)} %get-tuple-element.22), channel_id=1, source_target_pairs={{0,4},{4,0},{1,5},{5,1},{2,6},{6,2},{3,7},{7,3},{8,12},{12,8},{9,1... | collective-permute-start | bytes 442376 | tf_op jit(solution)/shard_map/ppermute | solution.py:394
  16.0 3.8 %collective-permute-start.2 = (f32[4,72,128]{2,1,0:T(8,128)}, f32[4,72,128]{2,1,0:T(8,128)S(1)}, u32[]{:S(2)}, u32[]{:S(2)}) collective-permute-start(f32[4,72,128]{2,1,0:T(8,128)} %get-tuple-element.23), channel_id=1, source_target_pairs={{0,4},{4,0},{1,5},{5,1},{2,6},{6,2},{3,7},{7,3},{8,12},{12,8},{9,1... | collective-permute-start | bytes 442376 | tf_op jit(solution)/shard_map/ppermute | solution.py:394
  16.4 3.4 %collective-permute-start.3 = (f32[4,72,128]{2,1,0:T(8,128)}, f32[4,72,128]{2,1,0:T(8,128)S(1)}, u32[]{:S(2)}, u32[]{:S(2)}) collective-permute-start(f32[4,72,128]{2,1,0:T(8,128)} %get-tuple-element.24), channel_id=1, source_target_pairs={{0,4},{4,0},{1,5},{5,1},{2,6},{6,2},{3,7},{7,3},{8,12},{12,8},{9,1... | collective-permute-start | bytes 442376 | tf_op jit(solution)/shard_map/ppermute | solution.py:394
  16.5 3.3 %copy-start = (f32[16,72,128]{2,1,0:T(8,128)S(1)}, f32[16,72,128]{2,1,0:T(8,128)}, u32[]{:S(2)}) copy-start(f32[16,72,128]{2,1,0:T(8,128)} %get-tuple-element.20.after_ref.a_ref) | copy-start | bytes 1769476
  16.5 3.3 %copy-start.1 = (s32[1024,8]{0,1:T(8,128)S(1)}, s32[1024,8]{0,1:T(8,128)}, u32[]{:S(2)}) copy-start(s32[1024,8]{0,1:T(8,128)} %param.8) | copy-start | bytes 98308
  21.4 20.1 %all-to-all-start = ((f32[16,72,128]{2,1,0:T(8,128)}), f32[16,72,128]{2,1,0:T(8,128)S(1)}, u32[]{:S(2)}, u32[]{:S(2)}) async-start(f32[16,72,128]{2,1,0:T(8,128)} %get-tuple-element.26), calls=%async_computation | async-start | bytes 1179648 | tf_op jit(solution)/shard_map/all_to_all | solution.py:398
  30.6 77.3 %all-gather.3.cloned.1.call-start = ((), (), s32[]{:S(2)}) async-start(), calls=%async_computation.4 | async-start | bytes 8650752 | tf_op jit(solution)/shard_map/all_gather | solution.py:427
  30.7 3.0 %collective-permute-start.7 = (s32[8,1024]{1,0:T(8,128)S(1)}, s32[8,1024]{1,0:T(8,128)S(1)}, u32[]{:S(2)}, u32[]{:S(2)}) collective-permute-start(s32[8,1024]{1,0:T(8,128)S(1)} %get-tuple-element.27.rest_0_), channel_id=1, source_target_pairs={{0,3},{1,0},{2,1},{3,2},{4,7},{5,4},{6,5},{7,6},{8,11},{9,8},{10,9... | collective-permute-start | bytes 98312 | tf_op jit(solution)/shard_map/ppermute | solution.py:405
  31.9 4.6 %collective-permute-start.6 = (s32[8,1024]{1,0:T(8,128)S(1)}, s32[8,1024]{1,0:T(8,128)S(1)}, u32[]{:S(2)}, u32[]{:S(2)}) collective-permute-start(s32[8,1024]{1,0:T(8,128)S(1)} %get-tuple-element.27.rest_0_), channel_id=1, source_target_pairs={{0,2},{1,3},{2,0},{3,1},{4,6},{5,7},{6,4},{7,5},{8,10},{9,11},{10,... | collective-permute-start | bytes 98312 | tf_op jit(solution)/shard_map/ppermute | solution.py:405
  33.7 4.3 %collective-permute-start.5 = (s32[8,1024]{1,0:T(8,128)S(1)}, s32[8,1024]{1,0:T(8,128)S(1)}, u32[]{:S(2)}, u32[]{:S(2)}) collective-permute-start(s32[8,1024]{1,0:T(8,128)S(1)} %get-tuple-element.27.rest_0_), channel_id=1, source_target_pairs={{0,1},{1,2},{2,3},{3,0},{4,5},{5,6},{6,7},{7,4},{8,9},{9,10},{10,1... | collective-permute-start | bytes 98312 | tf_op jit(solution)/shard_map/ppermute | solution.py:405
  42.3 6.0 %collective-permute-start.8 = (bf16[1024,512]{1,0:T(8,128)(2,1)}, bf16[1024,512]{1,0:T(8,128)(2,1)S(1)}, u32[]{:S(2)}, u32[]{:S(2)}) collective-permute-start(bf16[1024,512]{1,0:T(8,128)(2,1)} %get-tuple-element.30), channel_id=1, source_target_pairs={{0,4},{4,0},{1,5},{5,1},{2,6},{6,2},{3,7},{7,3},{8,12},{12,8},{9,1... | collective-permute-start | bytes 3145736 | tf_op jit(solution)/shard_map/ppermute | solution.py:394
  44.7 4.0 %collective-permute-start.9 = (bf16[1024,512]{1,0:T(8,128)(2,1)}, bf16[1024,512]{1,0:T(8,128)(2,1)S(1)}, u32[]{:S(2)}, u32[]{:S(2)}) collective-permute-start(bf16[1024,512]{1,0:T(8,128)(2,1)} %get-tuple-element.31), channel_id=1, source_target_pairs={{0,4},{4,0},{1,5},{5,1},{2,6},{6,2},{3,7},{7,3},{8,12},{12,8},{9,1... | collective-permute-start | bytes 3145736 | tf_op jit(solution)/shard_map/ppermute | solution.py:394
  44.8 11.2 %all-to-all-start.1 = ((bf16[16,64,128]{2,1,0:T(8,128)(2,1)}), bf16[16,64,128]{2,1,0:T(8,128)(2,1)S(1)}, u32[]{:S(2)}, u32[]{:S(2)}) async-start(bf16[16,64,128]{2,1,0:T(8,128)(2,1)} %get-tuple-element.29), calls=%async_computation.1 | async-start | bytes 524288 | tf_op jit(solution)/shard_map/all_to_all | solution.py:398
  48.7 7.3 %copy-start.2 = (bf16[1024,512]{1,0:T(8,128)(2,1)}, bf16[1024,512]{1,0:T(8,128)(2,1)S(1)}, u32[]{:S(2)}) copy-start(bf16[1024,512]{1,0:T(8,128)(2,1)S(1)} %collective-permute-done.9.rest_7_) | copy-start | bytes 3145732
  105.6 6.7 %collective-permute-start.10 = (bf16[16,256,128]{2,1,0:T(8,128)(2,1)S(1)}, bf16[16,256,128]{2,1,0:T(8,128)(2,1)S(1)}, u32[]{:S(2)}, u32[]{:S(2)}) collective-permute-start(bf16[16,256,128]{2,1,0:T(8,128)(2,1)S(1)} %bitcast.6), channel_id=1, source_target_pairs={{0,4},{4,0},{1,5},{5,1},{2,6},{6,2},{3,7},{7,3},{8,12},{12,8},{9,1... | collective-permute-start | bytes 3145736 | tf_op jit(solution)/shard_map/ppermute | solution.py:394
Sparse Core Ops, SparseCore 0:
  42.5 61.5 all-gather.2

commit v8 on v6

--- a/solution.py
+++ b/solution.py
@@ -105,7 +105,7 @@
     side_ref, after_ref, k_ref, v_ref, k_out_ref, v_out_ref, token_ref, held, come, gone
 ):
     del after_ref
-    token_ref[...] = jnp.zeros(token_ref.shape, token_ref.dtype)
+    token_ref[0] = side_ref[0]
     start = pl.multiple_of((1 - side_ref[0]) * HALF * HDIM, HALF * HDIM)
 
     def fetch(k, source):
@@ -130,9 +130,9 @@
     half = jax.ShapeDtypeStruct((keys.shape[0], HALF * HDIM), BF16)
     return pl.pallas_call(
         halves_kernel,
-        out_shape=(half, half, jax.ShapeDtypeStruct((8, HDIM), F32)),
+        out_shape=(half, half, jax.ShapeDtypeStruct((1,), jnp.int32)),
         in_specs=[SCALARS, IN_HBM, IN_HBM, IN_HBM],
-        out_specs=(IN_HBM, IN_HBM, IN_VMEM),
+        out_specs=(IN_HBM, IN_HBM, SCALARS),
         scratch_shapes=[
             pltpu.VMEM((2, *half.shape), BF16),
             pltpu.SemaphoreType.DMA((2,)),
@@ -143,7 +143,7 @@
 
 
 def add_kernel(a_ref, *rest):
-    ids_ref, out_ref, ids_out_ref = rest[PIECES + 2], rest[PIECES + 3], rest[PIECES + 5]
+    ids_ref, out_ref, ids_out_ref = rest[PIECES + 1], rest[PIECES + 3], rest[PIECES + 5]
     ids_out_ref[...] = ids_ref[...]
     size = a_ref.shape[0] // PIECES
     for k in range(PIECES):
@@ -151,7 +151,7 @@
         out_ref[lines] = a_ref[lines] + rest[k][...]
 
 
-def add_after(a, b, passed, after, ids):
+def add_after(a, b, passed, ids, after):
     return pl.pallas_call(
         add_kernel,
         out_shape=(
@@ -159,11 +159,11 @@
             jax.ShapeDtypeStruct(passed.shape, passed.dtype),
             jax.ShapeDtypeStruct(ids.shape, ids.dtype),
         ),
-        in_specs=[IN_VMEM] * (PIECES + 1) + [IN_HBM, IN_HBM, IN_VMEM],
+        in_specs=[IN_VMEM] * (PIECES + 1) + [IN_HBM, IN_VMEM, SCALARS],
         out_specs=(IN_VMEM, IN_HBM, IN_VMEM),
         input_output_aliases={PIECES + 1: 1},
         compiler_params=params(8),
-    )(a, *b, passed, after, ids)
+    )(a, *b, passed, ids, after)
 
 
 def centre_kernel(in_ref, *rest):
@@ -288,8 +288,8 @@
         out_ref[k] = whole
 
 
-def rows_of(ids_row, table):
-    return lax.dot_general(member_of(ids_row), table, TN, preferred_element_type=F32).astype(BF16)
+def columns_of(ids_row, table):
+    return lax.dot_general(table, member_of(ids_row), TN, preferred_element_type=F32).astype(BF16)
 
 
 def group_at(i, z_ref, groups):
@@ -301,23 +301,35 @@
     group = group_at(pl.program_id(0), z_ref, pl.num_programs(0))
     for j in range(HALF):
         row = ids_ref[pl.program_id(0), pl.ds(side_ref[0] * HALF + j, 1), :]
-        out_ref[:, j * HDIM : (j + 1) * HDIM] = rows_of(row, table_ref[group * HALF + j])
+        out_ref[j * HDIM : (j + 1) * HDIM, :] = columns_of(row, table_ref[group * HALF + j])
 
 
 def gather_of(side, z, ids, table, after):
     groups, lines, tokens = ids.shape
     return pl.pallas_call(
         gather_kernel,
-        out_shape=jax.ShapeDtypeStruct((groups, tokens, HALF * HDIM), BF16),
+        out_shape=jax.ShapeDtypeStruct((groups, HALF * HDIM, tokens), BF16),
         grid=(groups,),
         in_specs=[SCALARS, SCALARS, IN_VMEM, IN_VMEM, IN_HBM],
-        out_specs=pl.BlockSpec((None, tokens, HALF * HDIM), lambda i: (i, 0, 0)),
+        out_specs=pl.BlockSpec((None, HALF * HDIM, tokens), lambda i: (i, 0, 0)),
         compiler_params=params(51),
     )(side, z, ids, table, after)
 
 
 def project_kernel(
-    side_ref, z_ref, near_ref, ids_ref, table_ref, w_ref, out_ref, held, rows_ref, arrived, come
+    side_ref,
+    z_ref,
+    near_ref,
+    ids_ref,
+    table_ref,
+    w_ref,
+    out_ref,
+    held,
+    columns_ref,
+    done_ref,
+    arrived,
+    come,
+    gone,
 ):
     groups, blocks = w_ref.shape[:2]
     half = HALF * HDIM
@@ -331,7 +343,7 @@
         return pltpu.make_async_copy(w_ref.at[entry], held.at[i], arrived.at[i])
 
     def bring(i):
-        target = rows_ref.at[:, pl.ds(i * depth + own, half)]
+        target = columns_ref.at[pl.ds(i * depth + own, half), :]
         return pltpu.make_async_copy(near_ref.at[i], target, come.at[i])
 
     for i in range(groups):
@@ -344,7 +356,11 @@
         for j in range(HALF):
             row = ids_ref[i, pl.ds((1 - side_ref[0]) * HALF + j, 1), :]
             start = pl.multiple_of(i * depth + other + j * HDIM, HDIM)
-            rows_ref[:, pl.ds(start, HDIM)] = rows_of(row, table_ref[group * HALF + j])
+            columns_ref[pl.ds(start, HDIM), :] = columns_of(row, table_ref[group * HALF + j])
+
+    def put(b):
+        cols = pl.ds(pl.multiple_of(b * width, width), width)
+        return pltpu.make_async_copy(done_ref.at[b], out_ref.at[:, cols], gone.at[b])
 
     for i in range(groups):
         bring(i).wait()
@@ -360,12 +376,12 @@
             ],
             axis=0,
         )
-        cols = pl.ds(pl.multiple_of(b * width, width), width)
-        tall = out_ref.shape[0] // 2
-        for m in range(2):
-            lines = slice(m * tall, (m + 1) * tall)
-            product = jnp.dot(rows_ref[lines, :], weight, preferred_element_type=F32)
-            out_ref[lines, cols] = product.astype(BF16)
+        product = lax.dot_general(columns_ref[...], weight, TN, preferred_element_type=F32)
+        done_ref[b] = product.astype(BF16)
+        put(b).start()
+
+    for b in range(2):
+        put(b).wait()
 
 
 def project_of(side, z, near, ids, table, weight):
@@ -375,12 +391,14 @@
         project_kernel,
         out_shape=jax.ShapeDtypeStruct((tokens, blocks * width), BF16),
         in_specs=[SCALARS, SCALARS, IN_HBM, IN_VMEM, IN_VMEM, IN_HBM],
-        out_specs=IN_VMEM,
+        out_specs=IN_HBM,
         scratch_shapes=[
             pltpu.VMEM(weight.shape, BF16),
-            pltpu.VMEM((tokens, groups * depth), BF16),
+            pltpu.VMEM((groups * depth, tokens), BF16),
+            pltpu.VMEM((2, tokens, blocks * width // 2), BF16),
             pltpu.SemaphoreType.DMA((groups,)),
             pltpu.SemaphoreType.DMA((groups,)),
+            pltpu.SemaphoreType.DMA((2,)),
         ],
         compiler_params=params(51),
     )(side, z, near, ids, table, weight)
@@ -415,9 +433,9 @@
 
     *theirs, mine = totals_of(side, ids, queries)
     arrived = [other_core(piece) for piece in theirs]
-    keys_far, values_far, token = halves_of(side, theirs[0], keys, values)
+    keys_far, values_far, token = halves_of(side, mine, keys, values)
     keys_other, values_other = other_core(keys_far), other_core(values_far)
-    totals, turned_weight, ids = add_after(mine, arrived, turned_weight, token, ids)
+    totals, turned_weight, ids = add_after(mine, arrived, turned_weight, ids, token)
     weight = lax.all_gather(turned_weight, SEQ, axis=0)
     weight = weight.reshape(size, -1, *weight.shape[1:])
     all_ids = from_all_groups(ids)

time: 128 us -> 128 us (level)
  transfers between devices with their start and end apart: 14 -> 14, of which waited for: 4 -> 4; matrix products, arithmetic and copies ran while one was open for 0% -> 0% of each run, Pallas kernels for 15% -> 14%
where the time goes in v8:
time: 128 us; the launch traced here: 127 us
  Pallas kernels  34.1 us (27%)
  blocking collectives  33.9 us (26%)
  starting transfers between devices  29.8 us (23%)
  waiting for transfers between devices  15.4 us (12%)
  between operations  13.5 us (11%)
    all_to_all x2, blocking collectives, exchanged(): return lax.all_to_all(value, axes, split_axis=0, concat_axis=0, tiled=True)  33.9 us
    pallas_call x1, Pallas kernels, project_of(): pl.pallas_call(project_kernel, out_shape=jax.ShapeDtypeStruct((tokens, bl...  14.8 us
    all_to_all x2, starting transfers between devices, exchanged(): return lax.all_to_all(value, axes, split_axis=0, concat_axis=0, tiled=True)  14.4 us
    all_to_all x2, waiting for transfers between devices, exchanged(): return lax.all_to_all(value, axes, split_axis=0, concat_axis=0, tiled=True)  11.1 us
    ppermute x7, starting transfers between devices, other_core(): return lax.ppermute(value, 'c', [(0, 1), (1, 0)])  8.87 us
    pallas_call x1, Pallas kernels, attention_of(): pl.pallas_call(functools.partial(attention_kernel, groups), out_shape=(ja...  5.39 us
    pallas_call x1, Pallas kernels, totals_of(): pl.pallas_call(totals_kernel, out_shape=[jax.ShapeDtypeStruct((4 * HALF /...  4.27 us
    ppermute x3, waiting for transfers between devices, from_all_groups(): lax.ppermute(value, 'z', [(i, (i + d) % size) for i in range(size)])  4.27 us
  transfers between devices with their start and end apart: 14, of which 4 were waited for; matrix products, arithmetic and copies ran while one was open for 0% of the time, Pallas kernels for 14%

profile of v8, /device:TPU:1, one launch (start us, length us, event | category | flops | bytes accessed | tf_op | source)
XLA Modules:
  0.0 126.8 jit_solution(14098936873035171213)
XLA Ops:
  6.5 0.0 all-gather.3.cloned.1.call-start
  6.5 3.6 %collective-permute-start.4 = (bf16[1024,128]{1,0:T(8,128)(2,1)}, bf16[1024,128]{1,0:T(8,128)(2,1)}, u32[]{:S(2)}, u32[]{:S(2)}) collective-permute-start(bf16[1024,128]{1,0:T(8,128)(2,1)} %param.9), channel_id=1, source_target_pairs={{0,0},{1,96},{2,64},{3,32},{32,65},{33,33},{34,1},{35,97},{64,2},{... | collective-permute-start | bytes 786440 | tf_op jit(solution)/shard_map/ppermute | solution.py:432
  10.1 4.3 %shard_map.55 = (f32[4,72,128]{2,1,0:T(8,128)}, f32[4,72,128]{2,1,0:T(8,128)}, f32[4,72,128]{2,1,0:T(8,128)}, f32[4,72,128]{2,1,0:T(8,128)}, f32[16,72,128]{2,1,0:T(8,128)}) custom-call(s32[1]{0:T(128)} %bitcast.side_ref, s32[8,1024]{1,0:T(8,128)} %bitcast.9, bf16[1024,1024]{1,0:T(8,128)(2,1)} %q_ref.1), custom_call_target="tpu_custom_call" | custom-call | tf_op jit(solution)/shard_map/pallas_call | solution.py:87
  14.4 1.5 %collective-permute-start = (f32[4,72,128]{2,1,0:T(8,128)}, f32[4,72,128]{2,1,0:T(8,128)S(1)}, u32[]{:S(2)}, u32[]{:S(2)}) collective-permute-start(f32[4,72,128]{2,1,0:T(8,128)} %get-tuple-element.19), channel_id=1, source_target_pairs={{0,4},{4,0},{1,5},{5,1},{2,6},{6,2},{3,7},{7,3},{8,12},{12,8},{9,1... | collective-permute-start | bytes 442376 | tf_op jit(solution)/shard_map/ppermute | solution.py:408
  15.9 0.1 collective-permute-start.1
  16.0 0.4 collective-permute-start.2
  16.4 0.1 collective-permute-start.3
  16.5 0.0 copy-start
  16.5 0.0 copy-start.1
  16.5 3.2 %shard_map.56 = (bf16[1024,512]{1,0:T(8,128)(2,1)}, bf16[1024,512]{1,0:T(8,128)(2,1)}, s32[1]{0:T(128)}) custom-call(s32[1]{0:T(128)} %bitcast.side_ref, f32[16,72,128]{2,1,0:T(8,128)} %get-tuple-element.18.after_ref.a_ref, bf16[1024,1024]{1,0:T(8,128)(2,1)} %rest_4_.1, bf16[1024,1024]{1,0:T(8,128)(2,1)} %rest_6_.1), custom_call_target="tpu_custom_call" | custom-call | tf_op jit(solution)/shard_map/pallas_call | solution.py:131
  19.7 0.0 collective-permute-done.rest_0_
  19.8 0.0 collective-permute-done.1.rest_1_
  19.8 0.0 collective-permute-done.2.rest_2_
  19.8 0.0 collective-permute-done.3.rest_3_
  19.8 0.0 collective-permute-done.4.rest_4_
  19.8 0.0 copy-done
  19.8 0.0 copy-done.1
  19.8 1.5 %shard_map.57 = (f32[16,72,128]{2,1,0:T(8,128)}, bf16[1024,128]{1,0:T(8,128)(2,1)}, s32[8,1024]{1,0:T(8,128)S(1)}) custom-call(f32[16,72,128]{2,1,0:T(8,128)S(1)} %copy-done, f32[4,72,128]{2,1,0:T(8,128)S(1)} %collective-permute-done.rest_0_, f32[4,72,128]{2,1,0:T(8,128)S(1)} %collective-permute-done.1.rest_1_, ...), custom_call_target="tpu_custom_call", output_to_operand_aliasing={{1}: (5, {})} | custom-call | tf_op jit(solution)/shard_map/pallas_call | solution.py:155
  21.3 0.0 all-gather.3.cloned.1.call-update
  21.4 0.5 collective-permute-start.8
  21.8 0.1 collective-permute-start.9
  21.9 9.2 %all-to-all-start = ((f32[16,72,128]{2,1,0:T(8,128)}), f32[16,72,128]{2,1,0:T(8,128)S(1)}, u32[]{:S(2)}, u32[]{:S(2)}) async-start(f32[16,72,128]{2,1,0:T(8,128)} %get-tuple-element.24), calls=%async_computation | async-start | bytes 1179648 | tf_op jit(solution)/shard_map/all_to_all | solution.py:412
  31.2 1.8 %collective-permute-start.7 = (s32[8,1024]{1,0:T(8,128)S(1)}, s32[8,1024]{1,0:T(8,128)S(1)}, u32[]{:S(2)}, u32[]{:S(2)}) collective-permute-start(s32[8,1024]{1,0:T(8,128)S(1)} %get-tuple-element.25.rest_0_), channel_id=1, source_target_pairs={{0,3},{1,0},{2,1},{3,2},{4,7},{5,4},{6,5},{7,6},{8,11},{9,8},{10,9... | collective-permute-start | bytes 98312 | tf_op jit(solution)/shard_map/ppermute | solution.py:419
  33.0 1.2 collective-permute-start.6
  34.2 0.0 collective-permute-start.5
  34.2 0.0 collective-permute-done.7.rest_2_.rest_3_
  34.2 3.1 %collective-permute-done.6.rest_1_.rest_2_ = s32[8,1024]{1,0:T(8,128)S(1)} collective-permute-done((s32[8,1024]{1,0:T(8,128)S(1)}, s32[8,1024]{1,0:T(8,128)S(1)}, u32[]{:S(2)}, u32[]{:S(2)}) %collective-permute-start.6) | collective-permute-done | bytes 32800 | tf_op jit(solution)/shard_map/ppermute | solution.py:419
  37.2 1.2 collective-permute-done.5.rest_0_.rest_1_
  38.4 3.7 %all-to-all-done.in_ref = f32[16,72,128]{2,1,0:T(8,128)S(1)} async-done(((f32[16,72,128]{2,1,0:T(8,128)}), f32[16,72,128]{2,1,0:T(8,128)S(1)}, u32[]{:S(2)}, u32[]{:S(2)}) %all-to-all-start) | async-done | bytes 589856 | tf_op jit(solution)/shard_map/all_to_all | solution.py:412
  42.1 0.8 shard_map.58
  43.0 5.2 %all-to-all-start.1 = ((bf16[16,64,128]{2,1,0:T(8,128)(2,1)}), bf16[16,64,128]{2,1,0:T(8,128)(2,1)S(1)}, u32[]{:S(2)}, u32[]{:S(2)}) async-start(bf16[16,64,128]{2,1,0:T(8,128)(2,1)} %shard_map.58), calls=%async_computation.1 | async-start | bytes 524288 | tf_op jit(solution)/shard_map/all_to_all | solution.py:412
  48.1 0.0 collective-permute-done.8.rest_5_
  48.2 0.0 collective-permute-done.9.rest_7_
  48.2 0.0 copy-start.2
  48.2 7.4 %all-to-all-done.1 = bf16[16,64,128]{2,1,0:T(8,128)(2,1)S(1)} async-done(((bf16[16,64,128]{2,1,0:T(8,128)(2,1)}), bf16[16,64,128]{2,1,0:T(8,128)(2,1)S(1)}, u32[]{:S(2)}, u32[]{:S(2)}) %all-to-all-start.1) | async-done | bytes 262176 | tf_op jit(solution)/shard_map/all_to_all | solution.py:412
  55.6 0.0 copy-done.2
  55.6 5.4 %shard_map.59 = (bf16[16,80,128]{2,1,0:T(8,128)(2,1)S(1)}, s32[4,8,1024]{2,1,0:T(8,128)S(1)}) custom-call(s32[1]{0:T(128)} %bitcast.side_ref, bf16[4,256,128]{2,1,0:T(8,128)(2,1)S(1)} %bitcast.8, s32[8,1024]{1,0:T(8,128)S(1)} %get-tuple-element.25.rest_0_, s32[8,1024]{1,0:T(8,128)S(1)} %collective-permute-done.5.rest_0_.rest_1_, ...), custom_call_target="tpu_custom_call" | custom-call | tf_op jit(solution)/shard_map/pallas_call | solution.py:256
  61.0 13.4 %all_to_all.20.in_ref = bf16[16,80,128]{2,1,0:T(8,128)(2,1)S(1)} all-to-all(bf16[16,80,128]{2,1,0:T(8,128)(2,1)S(1)} %get-tuple-element.29), channel_id=1, replica_groups=mesh['x'=4,'y'=4,'c'=2,'z'=4] {'x','y'}, dimensions={0} | all-to-all | bytes 655360 | tf_op jit(solution)/shard_map/all_to_all | solution.py:412
  74.4 0.4 shard_map.60
  74.8 20.4 %all_to_all.21 = bf16[64,64,128]{2,1,0:T(8,128)(2,1)S(1)} all-to-all(bf16[64,64,128]{2,1,0:T(8,128)(2,1)S(1)} %shard_map.60), channel_id=1, replica_groups=mesh['x'=4,'y'=4,'c'=2,'z'=4] {'z','x','y'}, dimensions={0} | all-to-all | bytes 2097152 | tf_op jit(solution)/shard_map/all_to_all | solution.py:412
  95.2 6.2 %collective-permute-start.10 = (bf16[16,256,128]{2,1,0:T(8,128)(2,1)S(1)}, bf16[16,256,128]{2,1,0:T(8,128)(2,1)S(1)}, u32[]{:S(2)}, u32[]{:S(2)}) collective-permute-start(bf16[16,256,128]{2,1,0:T(8,128)(2,1)S(1)} %bitcast.6), channel_id=1, source_target_pairs={{0,4},{4,0},{1,5},{5,1},{2,6},{6,2},{3,7},{7,3},{8,12},{12,8},{9,1... | collective-permute-start | bytes 3145736 | tf_op jit(solution)/shard_map/ppermute | solution.py:408
  101.4 0.0 all-gather.3.cloned.1.call-done
  101.4 3.8 %shard_map.61.near_ref = bf16[4,512,1024]{2,1,0:T(8,128)(2,1)} custom-call(s32[1]{0:T(128)} %bitcast.side_ref, s32[1]{0:T(128)} %bitcast.1.z_ref, s32[4,8,1024]{2,1,0:T(8,128)S(1)} %get-tuple-element.28.ids_ref, bf16[16,256,128]{2,1,0:T(8,128)(2,1)S(1)} %bitcast.7, bf16[4,8,1024,128]{3,2,1,0:T(8,128)(2,1)} %bitcast.11), custom_call_target="tpu_custom_call" | custom-call | tf_op jit(solution)/shard_map/pallas_call | solution.py:309
  105.2 0.0 collective-permute-done.10.table_ref
  105.2 14.8 %shard_map.62 = bf16[1024,1024]{1,0:T(8,128)(2,1)} custom-call(s32[1]{0:T(128)} %bitcast.side_ref, s32[1]{0:T(128)} %bitcast.1.z_ref, bf16[4,512,1024]{2,1,0:T(8,128)(2,1)} %shard_map.61.near_ref, s32[4,8,1024]{2,1,0:T(8,128)S(1)} %get-tuple-element.28.ids_ref, bf16[16,256,128]{2,1,0:T(8,128)(2,1)S(1)} %collective-permute-done.10.table_ref, ...), custom_call_target="tpu_custom_call" | custom-call | tf_op jit(solution)/shard_map/pallas_call | solution.py:390
Async XLA Ops:
  6.5 94.9 %all-gather.3.cloned.1.call-start = ((), (), s32[]{:S(2)}) async-start(), calls=%async_computation.4 | async-start | bytes 8650752 | tf_op jit(solution)/shard_map/all_gather | solution.py:439
  6.5 13.2 %collective-permute-start.4 = (bf16[1024,128]{1,0:T(8,128)(2,1)}, bf16[1024,128]{1,0:T(8,128)(2,1)}, u32[]{:S(2)}, u32[]{:S(2)}) collective-permute-start(bf16[1024,128]{1,0:T(8,128)(2,1)} %param.9), channel_id=1, source_target_pairs={{0,0},{1,96},{2,64},{3,32},{32,65},{33,33},{34,1},{35,97},{64,2},{... | collective-permute-start | bytes 786440 | tf_op jit(solution)/shard_map/ppermute | solution.py:432
  14.4 5.4 %collective-permute-start = (f32[4,72,128]{2,1,0:T(8,128)}, f32[4,72,128]{2,1,0:T(8,128)S(1)}, u32[]{:S(2)}, u32[]{:S(2)}) collective-permute-start(f32[4,72,128]{2,1,0:T(8,128)} %get-tuple-element.19), channel_id=1, source_target_pairs={{0,4},{4,0},{1,5},{5,1},{2,6},{6,2},{3,7},{7,3},{8,12},{12,8},{9,1... | collective-permute-start | bytes 442376 | tf_op jit(solution)/shard_map/ppermute | solution.py:408
  15.9 3.9 %collective-permute-start.1 = (f32[4,72,128]{2,1,0:T(8,128)}, f32[4,72,128]{2,1,0:T(8,128)S(1)}, u32[]{:S(2)}, u32[]{:S(2)}) collective-permute-start(f32[4,72,128]{2,1,0:T(8,128)} %get-tuple-element.20), channel_id=1, source_target_pairs={{0,4},{4,0},{1,5},{5,1},{2,6},{6,2},{3,7},{7,3},{8,12},{12,8},{9,1... | collective-permute-start | bytes 442376 | tf_op jit(solution)/shard_map/ppermute | solution.py:408
  16.0 3.8 %collective-permute-start.2 = (f32[4,72,128]{2,1,0:T(8,128)}, f32[4,72,128]{2,1,0:T(8,128)S(1)}, u32[]{:S(2)}, u32[]{:S(2)}) collective-permute-start(f32[4,72,128]{2,1,0:T(8,128)} %get-tuple-element.21), channel_id=1, source_target_pairs={{0,4},{4,0},{1,5},{5,1},{2,6},{6,2},{3,7},{7,3},{8,12},{12,8},{9,1... | collective-permute-start | bytes 442376 | tf_op jit(solution)/shard_map/ppermute | solution.py:408
  16.4 3.4 %collective-permute-start.3 = (f32[4,72,128]{2,1,0:T(8,128)}, f32[4,72,128]{2,1,0:T(8,128)S(1)}, u32[]{:S(2)}, u32[]{:S(2)}) collective-permute-start(f32[4,72,128]{2,1,0:T(8,128)} %get-tuple-element.22), channel_id=1, source_target_pairs={{0,4},{4,0},{1,5},{5,1},{2,6},{6,2},{3,7},{7,3},{8,12},{12,8},{9,1... | collective-permute-start | bytes 442376 | tf_op jit(solution)/shard_map/ppermute | solution.py:408
  16.5 3.3 %copy-start = (f32[16,72,128]{2,1,0:T(8,128)S(1)}, f32[16,72,128]{2,1,0:T(8,128)}, u32[]{:S(2)}) copy-start(f32[16,72,128]{2,1,0:T(8,128)} %get-tuple-element.18.after_ref.a_ref) | copy-start | bytes 1769476
  16.5 3.3 %copy-start.1 = (s32[1024,8]{0,1:T(8,128)S(1)}, s32[1024,8]{0,1:T(8,128)}, u32[]{:S(2)}) copy-start(s32[1024,8]{0,1:T(8,128)} %param.8) | copy-start | bytes 98308
  21.4 26.8 %collective-permute-start.8 = (bf16[1024,512]{1,0:T(8,128)(2,1)}, bf16[1024,512]{1,0:T(8,128)(2,1)S(1)}, u32[]{:S(2)}, u32[]{:S(2)}) collective-permute-start(bf16[1024,512]{1,0:T(8,128)(2,1)} %get-tuple-element.26), channel_id=1, source_target_pairs={{0,4},{4,0},{1,5},{5,1},{2,6},{6,2},{3,7},{7,3},{8,12},{12,8},{9,1... | collective-permute-start | bytes 3145736 | tf_op jit(solution)/shard_map/ppermute | solution.py:408
  21.8 26.3 %collective-permute-start.9 = (bf16[1024,512]{1,0:T(8,128)(2,1)}, bf16[1024,512]{1,0:T(8,128)(2,1)S(1)}, u32[]{:S(2)}, u32[]{:S(2)}) collective-permute-start(bf16[1024,512]{1,0:T(8,128)(2,1)} %get-tuple-element.27), channel_id=1, source_target_pairs={{0,4},{4,0},{1,5},{5,1},{2,6},{6,2},{3,7},{7,3},{8,12},{12,8},{9,1... | collective-permute-start | bytes 3145736 | tf_op jit(solution)/shard_map/ppermute | solution.py:408
  21.9 20.2 %all-to-all-start = ((f32[16,72,128]{2,1,0:T(8,128)}), f32[16,72,128]{2,1,0:T(8,128)S(1)}, u32[]{:S(2)}, u32[]{:S(2)}) async-start(f32[16,72,128]{2,1,0:T(8,128)} %get-tuple-element.24), calls=%async_computation | async-start | bytes 1179648 | tf_op jit(solution)/shard_map/all_to_all | solution.py:412
  31.2 3.0 %collective-permute-start.7 = (s32[8,1024]{1,0:T(8,128)S(1)}, s32[8,1024]{1,0:T(8,128)S(1)}, u32[]{:S(2)}, u32[]{:S(2)}) collective-permute-start(s32[8,1024]{1,0:T(8,128)S(1)} %get-tuple-element.25.rest_0_), channel_id=1, source_target_pairs={{0,3},{1,0},{2,1},{3,2},{4,7},{5,4},{6,5},{7,6},{8,11},{9,8},{10,9... | collective-permute-start | bytes 98312 | tf_op jit(solution)/shard_map/ppermute | solution.py:419
  33.0 4.3 %collective-permute-start.6 = (s32[8,1024]{1,0:T(8,128)S(1)}, s32[8,1024]{1,0:T(8,128)S(1)}, u32[]{:S(2)}, u32[]{:S(2)}) collective-permute-start(s32[8,1024]{1,0:T(8,128)S(1)} %get-tuple-element.25.rest_0_), channel_id=1, source_target_pairs={{0,2},{1,3},{2,0},{3,1},{4,6},{5,7},{6,4},{7,5},{8,10},{9,11},{10,... | collective-permute-start | bytes 98312 | tf_op jit(solution)/shard_map/ppermute | solution.py:419
  34.2 4.3 %collective-permute-start.5 = (s32[8,1024]{1,0:T(8,128)S(1)}, s32[8,1024]{1,0:T(8,128)S(1)}, u32[]{:S(2)}, u32[]{:S(2)}) collective-permute-start(s32[8,1024]{1,0:T(8,128)S(1)} %get-tuple-element.25.rest_0_), channel_id=1, source_target_pairs={{0,1},{1,2},{2,3},{3,0},{4,5},{5,6},{6,7},{7,4},{8,9},{9,10},{10,1... | collective-permute-start | bytes 98312 | tf_op jit(solution)/shard_map/ppermute | solution.py:419
  43.0 12.6 %all-to-all-start.1 = ((bf16[16,64,128]{2,1,0:T(8,128)(2,1)}), bf16[16,64,128]{2,1,0:T(8,128)(2,1)S(1)}, u32[]{:S(2)}, u32[]{:S(2)}) async-start(bf16[16,64,128]{2,1,0:T(8,128)(2,1)} %shard_map.58), calls=%async_computation.1 | async-start | bytes 524288 | tf_op jit(solution)/shard_map/all_to_all | solution.py:412
  48.2 7.4 %copy-start.2 = (bf16[1024,512]{1,0:T(8,128)(2,1)}, bf16[1024,512]{1,0:T(8,128)(2,1)S(1)}, u32[]{:S(2)}) copy-start(bf16[1024,512]{1,0:T(8,128)(2,1)S(1)} %collective-permute-done.9.rest_7_) | copy-start | bytes 3145732
  95.2 9.9 %collective-permute-start.10 = (bf16[16,256,128]{2,1,0:T(8,128)(2,1)S(1)}, bf16[16,256,128]{2,1,0:T(8,128)(2,1)S(1)}, u32[]{:S(2)}, u32[]{:S(2)}) collective-permute-start(bf16[16,256,128]{2,1,0:T(8,128)(2,1)S(1)} %bitcast.6), channel_id=1, source_target_pairs={{0,4},{4,0},{1,5},{5,1},{2,6},{6,2},{3,7},{7,3},{8,12},{12,8},{9,1... | collective-permute-start | bytes 3145736 | tf_op jit(solution)/shard_map/ppermute | solution.py:408
Sparse Core Ops, SparseCore 0:
  21.5 60.7 all-gather.2

commit v9 on v8

--- a/solution.py
+++ b/solution.py
@@ -338,9 +338,12 @@
     own = pl.multiple_of(side_ref[0] * half, half)
     other = pl.multiple_of(half - side_ref[0] * half, half)
 
-    def fetch(i):
+    each = blocks // 2
+
+    def fetch(i, b):
         entry = lax.rem(z_ref[0] + i, groups)
-        return pltpu.make_async_copy(w_ref.at[entry], held.at[i], arrived.at[i])
+        part = pl.ds(b * each, each)
+        return pltpu.make_async_copy(w_ref.at[entry, part], held.at[i, part], arrived.at[i, b])
 
     def bring(i):
         target = columns_ref.at[pl.ds(i * depth + own, half), :]
@@ -348,7 +351,9 @@
 
     for i in range(groups):
         bring(i).start()
-        fetch(i).start()
+        fetch(i, 0).start()
+    for i in range(groups):
+        fetch(i, 1).start()
 
     @pl.loop(0, groups)
     def _(i):
@@ -364,11 +369,11 @@
 
     for i in range(groups):
         bring(i).wait()
-        fetch(i).wait()
 
     @pl.loop(0, 2)
     def _(b):
-        each = blocks // 2
+        for i in range(groups):
+            fetch(i, b).wait()
         weight = jnp.concatenate(
             [
                 jnp.concatenate([held[i, b * each + k] for k in range(each)], axis=1)
@@ -396,7 +401,7 @@
             pltpu.VMEM(weight.shape, BF16),
             pltpu.VMEM((groups * depth, tokens), BF16),
             pltpu.VMEM((2, tokens, blocks * width // 2), BF16),
-            pltpu.SemaphoreType.DMA((groups,)),
+            pltpu.SemaphoreType.DMA((groups, 2)),
             pltpu.SemaphoreType.DMA((groups,)),
             pltpu.SemaphoreType.DMA((2,)),
         ],

time: 128 us -> 127 us (level)
  no operation moved by 1% of the time
where the time goes in v9:
time: 127 us; the launch traced here: 126 us
  blocking collectives  33.9 us (27%)
  Pallas kernels  33.8 us (27%)
  starting transfers between devices  29.8 us (23%)
  waiting for transfers between devices  15.4 us (12%)
  between operations  13.5 us (11%)
    all_to_all x2, blocking collectives, exchanged(): return lax.all_to_all(value, axes, split_axis=0, concat_axis=0, tiled=True)  33.9 us
    pallas_call x1, Pallas kernels, project_of(): pl.pallas_call(project_kernel, out_shape=jax.ShapeDtypeStruct((tokens, bl...  14.4 us
    all_to_all x2, starting transfers between devices, exchanged(): return lax.all_to_all(value, axes, split_axis=0, concat_axis=0, tiled=True)  14.4 us
    all_to_all x2, waiting for transfers between devices, exchanged(): return lax.all_to_all(value, axes, split_axis=0, concat_axis=0, tiled=True)  11.1 us
    ppermute x7, starting transfers between devices, other_core(): return lax.ppermute(value, 'c', [(0, 1), (1, 0)])  8.87 us
    pallas_call x1, Pallas kernels, attention_of(): pl.pallas_call(functools.partial(attention_kernel, groups), out_shape=(ja...  5.39 us
    pallas_call x1, Pallas kernels, totals_of(): pl.pallas_call(totals_kernel, out_shape=[jax.ShapeDtypeStruct((4 * HALF /...  4.27 us
    ppermute x3, waiting for transfers between devices, from_all_groups(): lax.ppermute(value, 'z', [(i, (i + d) % size) for i in range(size)])  4.27 us
  transfers between devices with their start and end apart: 14, of which 4 were waited for; matrix products, arithmetic and copies ran while one was open for 0% of the time, Pallas kernels for 14%

profile of v9, /device:TPU:1, one launch (start us, length us, event | category | flops | bytes accessed | tf_op | source)
XLA Modules:
  0.0 126.5 jit_solution(9300640034720952808)
XLA Ops:
  6.5 0.0 all-gather.3.cloned.1.call-start
  6.5 3.6 %collective-permute-start.4 = (bf16[1024,128]{1,0:T(8,128)(2,1)}, bf16[1024,128]{1,0:T(8,128)(2,1)}, u32[]{:S(2)}, u32[]{:S(2)}) collective-permute-start(bf16[1024,128]{1,0:T(8,128)(2,1)} %param.9), channel_id=1, source_target_pairs={{0,0},{1,96},{2,64},{3,32},{32,65},{33,33},{34,1},{35,97},{64,2},{... | collective-permute-start | bytes 786440 | tf_op jit(solution)/shard_map/ppermute | solution.py:437
  10.1 4.3 %shard_map.55 = (f32[4,72,128]{2,1,0:T(8,128)}, f32[4,72,128]{2,1,0:T(8,128)}, f32[4,72,128]{2,1,0:T(8,128)}, f32[4,72,128]{2,1,0:T(8,128)}, f32[16,72,128]{2,1,0:T(8,128)}) custom-call(s32[1]{0:T(128)} %bitcast.side_ref, s32[8,1024]{1,0:T(8,128)} %bitcast.9, bf16[1024,1024]{1,0:T(8,128)(2,1)} %q_ref.1), custom_call_target="tpu_custom_call" | custom-call | tf_op jit(solution)/shard_map/pallas_call | solution.py:87
  14.4 1.5 %collective-permute-start = (f32[4,72,128]{2,1,0:T(8,128)}, f32[4,72,128]{2,1,0:T(8,128)S(1)}, u32[]{:S(2)}, u32[]{:S(2)}) collective-permute-start(f32[4,72,128]{2,1,0:T(8,128)} %get-tuple-element.19), channel_id=1, source_target_pairs={{0,4},{4,0},{1,5},{5,1},{2,6},{6,2},{3,7},{7,3},{8,12},{12,8},{9,1... | collective-permute-start | bytes 442376 | tf_op jit(solution)/shard_map/ppermute | solution.py:413
  15.9 0.1 collective-permute-start.1
  16.0 0.4 collective-permute-start.2
  16.4 0.1 collective-permute-start.3
  16.5 0.0 copy-start
  16.5 0.0 copy-start.1
  16.5 3.2 %shard_map.56 = (bf16[1024,512]{1,0:T(8,128)(2,1)}, bf16[1024,512]{1,0:T(8,128)(2,1)}, s32[1]{0:T(128)}) custom-call(s32[1]{0:T(128)} %bitcast.side_ref, f32[16,72,128]{2,1,0:T(8,128)} %get-tuple-element.18.after_ref.a_ref, bf16[1024,1024]{1,0:T(8,128)(2,1)} %rest_4_.1, bf16[1024,1024]{1,0:T(8,128)(2,1)} %rest_6_.1), custom_call_target="tpu_custom_call" | custom-call | tf_op jit(solution)/shard_map/pallas_call | solution.py:131
  19.7 0.0 collective-permute-done.rest_0_
  19.8 0.0 collective-permute-done.1.rest_1_
  19.8 0.0 collective-permute-done.2.rest_2_
  19.8 0.0 collective-permute-done.3.rest_3_
  19.8 0.0 collective-permute-done.4.rest_4_
  19.8 0.0 copy-done
  19.8 0.0 copy-done.1
  19.8 1.5 %shard_map.57 = (f32[16,72,128]{2,1,0:T(8,128)}, bf16[1024,128]{1,0:T(8,128)(2,1)}, s32[8,1024]{1,0:T(8,128)S(1)}) custom-call(f32[16,72,128]{2,1,0:T(8,128)S(1)} %copy-done, f32[4,72,128]{2,1,0:T(8,128)S(1)} %collective-permute-done.rest_0_, f32[4,72,128]{2,1,0:T(8,128)S(1)} %collective-permute-done.1.rest_1_, ...), custom_call_target="tpu_custom_call", output_to_operand_aliasing={{1}: (5, {})} | custom-call | tf_op jit(solution)/shard_map/pallas_call | solution.py:155
  21.3 0.0 all-gather.3.cloned.1.call-update
  21.4 0.5 collective-permute-start.8
  21.8 0.1 collective-permute-start.9
  21.9 9.2 %all-to-all-start = ((f32[16,72,128]{2,1,0:T(8,128)}), f32[16,72,128]{2,1,0:T(8,128)S(1)}, u32[]{:S(2)}, u32[]{:S(2)}) async-start(f32[16,72,128]{2,1,0:T(8,128)} %get-tuple-element.24), calls=%async_computation | async-start | bytes 1179648 | tf_op jit(solution)/shard_map/all_to_all | solution.py:417
  31.2 1.8 %collective-permute-start.7 = (s32[8,1024]{1,0:T(8,128)S(1)}, s32[8,1024]{1,0:T(8,128)S(1)}, u32[]{:S(2)}, u32[]{:S(2)}) collective-permute-start(s32[8,1024]{1,0:T(8,128)S(1)} %get-tuple-element.25.rest_0_), channel_id=1, source_target_pairs={{0,3},{1,0},{2,1},{3,2},{4,7},{5,4},{6,5},{7,6},{8,11},{9,8},{10,9... | collective-permute-start | bytes 98312 | tf_op jit(solution)/shard_map/ppermute | solution.py:424
  33.0 1.2 collective-permute-start.6
  34.2 0.0 collective-permute-start.5
  34.2 0.0 collective-permute-done.7.rest_2_.rest_3_
  34.2 3.1 %collective-permute-done.6.rest_1_.rest_2_ = s32[8,1024]{1,0:T(8,128)S(1)} collective-permute-done((s32[8,1024]{1,0:T(8,128)S(1)}, s32[8,1024]{1,0:T(8,128)S(1)}, u32[]{:S(2)}, u32[]{:S(2)}) %collective-permute-start.6) | collective-permute-done | bytes 32800 | tf_op jit(solution)/shard_map/ppermute | solution.py:424
  37.2 1.2 collective-permute-done.5.rest_0_.rest_1_
  38.4 3.7 %all-to-all-done.in_ref = f32[16,72,128]{2,1,0:T(8,128)S(1)} async-done(((f32[16,72,128]{2,1,0:T(8,128)}), f32[16,72,128]{2,1,0:T(8,128)S(1)}, u32[]{:S(2)}, u32[]{:S(2)}) %all-to-all-start) | async-done | bytes 589856 | tf_op jit(solution)/shard_map/all_to_all | solution.py:417
  42.1 0.8 shard_map.58
  43.0 5.2 %all-to-all-start.1 = ((bf16[16,64,128]{2,1,0:T(8,128)(2,1)}), bf16[16,64,128]{2,1,0:T(8,128)(2,1)S(1)}, u32[]{:S(2)}, u32[]{:S(2)}) async-start(bf16[16,64,128]{2,1,0:T(8,128)(2,1)} %shard_map.58), calls=%async_computation.1 | async-start | bytes 524288 | tf_op jit(solution)/shard_map/all_to_all | solution.py:417
  48.1 0.0 collective-permute-done.8.rest_5_
  48.2 0.0 collective-permute-done.9.rest_7_
  48.2 0.0 copy-start.2
  48.2 7.4 %all-to-all-done.1 = bf16[16,64,128]{2,1,0:T(8,128)(2,1)S(1)} async-done(((bf16[16,64,128]{2,1,0:T(8,128)(2,1)}), bf16[16,64,128]{2,1,0:T(8,128)(2,1)S(1)}, u32[]{:S(2)}, u32[]{:S(2)}) %all-to-all-start.1) | async-done | bytes 262176 | tf_op jit(solution)/shard_map/all_to_all | solution.py:417
  55.6 0.0 copy-done.2
  55.6 5.4 %shard_map.59 = (bf16[16,80,128]{2,1,0:T(8,128)(2,1)S(1)}, s32[4,8,1024]{2,1,0:T(8,128)S(1)}) custom-call(s32[1]{0:T(128)} %bitcast.side_ref, bf16[4,256,128]{2,1,0:T(8,128)(2,1)S(1)} %bitcast.8, s32[8,1024]{1,0:T(8,128)S(1)} %get-tuple-element.25.rest_0_, s32[8,1024]{1,0:T(8,128)S(1)} %collective-permute-done.5.rest_0_.rest_1_, ...), custom_call_target="tpu_custom_call" | custom-call | tf_op jit(solution)/shard_map/pallas_call | solution.py:256
  61.0 13.4 %all_to_all.20.in_ref = bf16[16,80,128]{2,1,0:T(8,128)(2,1)S(1)} all-to-all(bf16[16,80,128]{2,1,0:T(8,128)(2,1)S(1)} %get-tuple-element.29), channel_id=1, replica_groups=mesh['x'=4,'y'=4,'c'=2,'z'=4] {'x','y'}, dimensions={0} | all-to-all | bytes 655360 | tf_op jit(solution)/shard_map/all_to_all | solution.py:417
  74.4 0.4 shard_map.60
  74.8 20.4 %all_to_all.21 = bf16[64,64,128]{2,1,0:T(8,128)(2,1)S(1)} all-to-all(bf16[64,64,128]{2,1,0:T(8,128)(2,1)S(1)} %shard_map.60), channel_id=1, replica_groups=mesh['x'=4,'y'=4,'c'=2,'z'=4] {'z','x','y'}, dimensions={0} | all-to-all | bytes 2097152 | tf_op jit(solution)/shard_map/all_to_all | solution.py:417
  95.2 6.2 %collective-permute-start.10 = (bf16[16,256,128]{2,1,0:T(8,128)(2,1)S(1)}, bf16[16,256,128]{2,1,0:T(8,128)(2,1)S(1)}, u32[]{:S(2)}, u32[]{:S(2)}) collective-permute-start(bf16[16,256,128]{2,1,0:T(8,128)(2,1)S(1)} %bitcast.6), channel_id=1, source_target_pairs={{0,4},{4,0},{1,5},{5,1},{2,6},{6,2},{3,7},{7,3},{8,12},{12,8},{9,1... | collective-permute-start | bytes 3145736 | tf_op jit(solution)/shard_map/ppermute | solution.py:413
  101.4 0.0 all-gather.3.cloned.1.call-done
  101.4 3.8 %shard_map.61.near_ref = bf16[4,512,1024]{2,1,0:T(8,128)(2,1)} custom-call(s32[1]{0:T(128)} %bitcast.side_ref, s32[1]{0:T(128)} %bitcast.1.z_ref, s32[4,8,1024]{2,1,0:T(8,128)S(1)} %get-tuple-element.28.ids_ref, bf16[16,256,128]{2,1,0:T(8,128)(2,1)S(1)} %bitcast.7, bf16[4,8,1024,128]{3,2,1,0:T(8,128)(2,1)} %bitcast.11), custom_call_target="tpu_custom_call" | custom-call | tf_op jit(solution)/shard_map/pallas_call | solution.py:309
  105.2 0.0 collective-permute-done.10.table_ref
  105.2 14.4 %shard_map.62 = bf16[1024,1024]{1,0:T(8,128)(2,1)} custom-call(s32[1]{0:T(128)} %bitcast.side_ref, s32[1]{0:T(128)} %bitcast.1.z_ref, bf16[4,512,1024]{2,1,0:T(8,128)(2,1)} %shard_map.61.near_ref, s32[4,8,1024]{2,1,0:T(8,128)S(1)} %get-tuple-element.28.ids_ref, bf16[16,256,128]{2,1,0:T(8,128)(2,1)S(1)} %collective-permute-done.10.table_ref, ...), custom_call_target="tpu_custom_call" | custom-call | tf_op jit(solution)/shard_map/pallas_call | solution.py:395
Async XLA Ops:
  6.5 94.9 %all-gather.3.cloned.1.call-start = ((), (), s32[]{:S(2)}) async-start(), calls=%async_computation.4 | async-start | bytes 8650752 | tf_op jit(solution)/shard_map/all_gather | solution.py:444
  6.5 13.2 %collective-permute-start.4 = (bf16[1024,128]{1,0:T(8,128)(2,1)}, bf16[1024,128]{1,0:T(8,128)(2,1)}, u32[]{:S(2)}, u32[]{:S(2)}) collective-permute-start(bf16[1024,128]{1,0:T(8,128)(2,1)} %param.9), channel_id=1, source_target_pairs={{0,0},{1,96},{2,64},{3,32},{32,65},{33,33},{34,1},{35,97},{64,2},{... | collective-permute-start | bytes 786440 | tf_op jit(solution)/shard_map/ppermute | solution.py:437
  14.4 5.4 %collective-permute-start = (f32[4,72,128]{2,1,0:T(8,128)}, f32[4,72,128]{2,1,0:T(8,128)S(1)}, u32[]{:S(2)}, u32[]{:S(2)}) collective-permute-start(f32[4,72,128]{2,1,0:T(8,128)} %get-tuple-element.19), channel_id=1, source_target_pairs={{0,4},{4,0},{1,5},{5,1},{2,6},{6,2},{3,7},{7,3},{8,12},{12,8},{9,1... | collective-permute-start | bytes 442376 | tf_op jit(solution)/shard_map/ppermute | solution.py:413
  15.9 3.9 %collective-permute-start.1 = (f32[4,72,128]{2,1,0:T(8,128)}, f32[4,72,128]{2,1,0:T(8,128)S(1)}, u32[]{:S(2)}, u32[]{:S(2)}) collective-permute-start(f32[4,72,128]{2,1,0:T(8,128)} %get-tuple-element.20), channel_id=1, source_target_pairs={{0,4},{4,0},{1,5},{5,1},{2,6},{6,2},{3,7},{7,3},{8,12},{12,8},{9,1... | collective-permute-start | bytes 442376 | tf_op jit(solution)/shard_map/ppermute | solution.py:413
  16.0 3.8 %collective-permute-start.2 = (f32[4,72,128]{2,1,0:T(8,128)}, f32[4,72,128]{2,1,0:T(8,128)S(1)}, u32[]{:S(2)}, u32[]{:S(2)}) collective-permute-start(f32[4,72,128]{2,1,0:T(8,128)} %get-tuple-element.21), channel_id=1, source_target_pairs={{0,4},{4,0},{1,5},{5,1},{2,6},{6,2},{3,7},{7,3},{8,12},{12,8},{9,1... | collective-permute-start | bytes 442376 | tf_op jit(solution)/shard_map/ppermute | solution.py:413
  16.4 3.4 %collective-permute-start.3 = (f32[4,72,128]{2,1,0:T(8,128)}, f32[4,72,128]{2,1,0:T(8,128)S(1)}, u32[]{:S(2)}, u32[]{:S(2)}) collective-permute-start(f32[4,72,128]{2,1,0:T(8,128)} %get-tuple-element.22), channel_id=1, source_target_pairs={{0,4},{4,0},{1,5},{5,1},{2,6},{6,2},{3,7},{7,3},{8,12},{12,8},{9,1... | collective-permute-start | bytes 442376 | tf_op jit(solution)/shard_map/ppermute | solution.py:413
  16.5 3.3 %copy-start = (f32[16,72,128]{2,1,0:T(8,128)S(1)}, f32[16,72,128]{2,1,0:T(8,128)}, u32[]{:S(2)}) copy-start(f32[16,72,128]{2,1,0:T(8,128)} %get-tuple-element.18.after_ref.a_ref) | copy-start | bytes 1769476
  16.5 3.3 %copy-start.1 = (s32[1024,8]{0,1:T(8,128)S(1)}, s32[1024,8]{0,1:T(8,128)}, u32[]{:S(2)}) copy-start(s32[1024,8]{0,1:T(8,128)} %param.8) | copy-start | bytes 98308
  21.4 26.8 %collective-permute-start.8 = (bf16[1024,512]{1,0:T(8,128)(2,1)}, bf16[1024,512]{1,0:T(8,128)(2,1)S(1)}, u32[]{:S(2)}, u32[]{:S(2)}) collective-permute-start(bf16[1024,512]{1,0:T(8,128)(2,1)} %get-tuple-element.26), channel_id=1, source_target_pairs={{0,4},{4,0},{1,5},{5,1},{2,6},{6,2},{3,7},{7,3},{8,12},{12,8},{9,1... | collective-permute-start | bytes 3145736 | tf_op jit(solution)/shard_map/ppermute | solution.py:413
  21.8 26.3 %collective-permute-start.9 = (bf16[1024,512]{1,0:T(8,128)(2,1)}, bf16[1024,512]{1,0:T(8,128)(2,1)S(1)}, u32[]{:S(2)}, u32[]{:S(2)}) collective-permute-start(bf16[1024,512]{1,0:T(8,128)(2,1)} %get-tuple-element.27), channel_id=1, source_target_pairs={{0,4},{4,0},{1,5},{5,1},{2,6},{6,2},{3,7},{7,3},{8,12},{12,8},{9,1... | collective-permute-start | bytes 3145736 | tf_op jit(solution)/shard_map/ppermute | solution.py:413
  21.9 20.2 %all-to-all-start = ((f32[16,72,128]{2,1,0:T(8,128)}), f32[16,72,128]{2,1,0:T(8,128)S(1)}, u32[]{:S(2)}, u32[]{:S(2)}) async-start(f32[16,72,128]{2,1,0:T(8,128)} %get-tuple-element.24), calls=%async_computation | async-start | bytes 1179648 | tf_op jit(solution)/shard_map/all_to_all | solution.py:417
  31.2 3.0 %collective-permute-start.7 = (s32[8,1024]{1,0:T(8,128)S(1)}, s32[8,1024]{1,0:T(8,128)S(1)}, u32[]{:S(2)}, u32[]{:S(2)}) collective-permute-start(s32[8,1024]{1,0:T(8,128)S(1)} %get-tuple-element.25.rest_0_), channel_id=1, source_target_pairs={{0,3},{1,0},{2,1},{3,2},{4,7},{5,4},{6,5},{7,6},{8,11},{9,8},{10,9... | collective-permute-start | bytes 98312 | tf_op jit(solution)/shard_map/ppermute | solution.py:424
  33.0 4.3 %collective-permute-start.6 = (s32[8,1024]{1,0:T(8,128)S(1)}, s32[8,1024]{1,0:T(8,128)S(1)}, u32[]{:S(2)}, u32[]{:S(2)}) collective-permute-start(s32[8,1024]{1,0:T(8,128)S(1)} %get-tuple-element.25.rest_0_), channel_id=1, source_target_pairs={{0,2},{1,3},{2,0},{3,1},{4,6},{5,7},{6,4},{7,5},{8,10},{9,11},{10,... | collective-permute-start | bytes 98312 | tf_op jit(solution)/shard_map/ppermute | solution.py:424
  34.2 4.3 %collective-permute-start.5 = (s32[8,1024]{1,0:T(8,128)S(1)}, s32[8,1024]{1,0:T(8,128)S(1)}, u32[]{:S(2)}, u32[]{:S(2)}) collective-permute-start(s32[8,1024]{1,0:T(8,128)S(1)} %get-tuple-element.25.rest_0_), channel_id=1, source_target_pairs={{0,1},{1,2},{2,3},{3,0},{4,5},{5,6},{6,7},{7,4},{8,9},{9,10},{10,1... | collective-permute-start | bytes 98312 | tf_op jit(solution)/shard_map/ppermute | solution.py:424
  43.0 12.6 %all-to-all-start.1 = ((bf16[16,64,128]{2,1,0:T(8,128)(2,1)}), bf16[16,64,128]{2,1,0:T(8,128)(2,1)S(1)}, u32[]{:S(2)}, u32[]{:S(2)}) async-start(bf16[16,64,128]{2,1,0:T(8,128)(2,1)} %shard_map.58), calls=%async_computation.1 | async-start | bytes 524288 | tf_op jit(solution)/shard_map/all_to_all | solution.py:417
  48.2 7.4 %copy-start.2 = (bf16[1024,512]{1,0:T(8,128)(2,1)}, bf16[1024,512]{1,0:T(8,128)(2,1)S(1)}, u32[]{:S(2)}) copy-start(bf16[1024,512]{1,0:T(8,128)(2,1)S(1)} %collective-permute-done.9.rest_7_) | copy-start | bytes 3145732
  95.2 9.9 %collective-permute-start.10 = (bf16[16,256,128]{2,1,0:T(8,128)(2,1)S(1)}, bf16[16,256,128]{2,1,0:T(8,128)(2,1)S(1)}, u32[]{:S(2)}, u32[]{:S(2)}) collective-permute-start(bf16[16,256,128]{2,1,0:T(8,128)(2,1)S(1)} %bitcast.6), channel_id=1, source_target_pairs={{0,4},{4,0},{1,5},{5,1},{2,6},{6,2},{3,7},{7,3},{8,12},{12,8},{9,1... | collective-permute-start | bytes 3145736 | tf_op jit(solution)/shard_map/ppermute | solution.py:413
Sparse Core Ops, SparseCore 0:
  21.5 60.7 all-gather.2

commit v10 on v9

--- a/solution.py
+++ b/solution.py
@@ -193,14 +193,18 @@
     out_ref, ids_out_ref, held, arrived, copied = rest[groups + 4 :]
     first = side_ref[0] * HALF
 
-    def fetch(k):
-        source = sources[k]
-        if k % 2 == 0:
-            source = source.at[:, pl.ds(pl.multiple_of(first * HDIM, HALF * HDIM), HALF * HDIM)]
-        return pltpu.make_async_copy(source, held.at[k], arrived.at[k])
+    pair = 2 * HDIM
+
+    def fetch(k, p):
+        start = p * pair if k % 2 else pl.multiple_of(first * HDIM + p * pair, pair)
+        return pltpu.make_async_copy(
+            sources[k].at[:, pl.ds(start, pair)],
+            held.at[k, :, pl.ds(p * pair, pair)],
+            arrived.at[k, p],
+        )
 
     for k in range(2):
-        fetch(k).start()
+        fetch(k, 0).start()
     copies = [
         pltpu.make_async_copy(ids_refs[d], ids_out_ref.at[d], copied.at[d]) for d in range(groups)
     ]
@@ -210,11 +214,14 @@
     diagonal = eye(QUARTER, HDIM)
     line = lax.broadcasted_iota(jnp.int32, (TAIL, HDIM), 0)
     for i in range(HALF):
+        if i % 2 == 0:
+            for k in range(2):
+                fetch(k, i // 2).wait()
         if i == 0:
-            for k in range(2):
-                fetch(k).wait()
-            for k in range(2, 4):
-                fetch(k).start()
+            for k in (2, 3):
+                fetch(k, 0).start()
+            for k in range(4):
+                fetch(k, 1).start()
         cols = slice(i * HDIM, (i + 1) * HDIM)
         centre = centre_ref[i]
         own = lax.dot_general(centre, held[0, :, cols], NT, preferred_element_type=F32)
@@ -224,9 +231,9 @@
         )
         own_w = jnp.exp2((own - peak) * LOG2_SCALE).astype(BF16)
         other_w = jnp.exp2((other - peak) * LOG2_SCALE).astype(BF16)
-        if i == 0:
-            for k in range(2, 4):
-                fetch(k).wait()
+        if i % 2 == 0:
+            for k in (2, 3):
+                fetch(k, i // 2).wait()
         both = jnp.dot(
             own_w, jnp.concatenate([held[2, :, cols], ones], axis=1), preferred_element_type=F32
         ) + jnp.dot(
@@ -263,7 +270,7 @@
         out_specs=(IN_VMEM, IN_VMEM),
         scratch_shapes=[
             pltpu.VMEM((4, rows, HALF * HDIM), BF16),
-            pltpu.SemaphoreType.DMA((4,)),
+            pltpu.SemaphoreType.DMA((4, 2)),
             pltpu.SemaphoreType.DMA((groups,)),
         ],
         compiler_params=params(52),

time: 127 us -> 128 us (level)
  transfers between devices with their start and end apart: 14 -> 14, of which waited for: 4 -> 4; matrix products, arithmetic and copies ran while one was open for 0% -> 0% of each run, Pallas kernels for 14% -> 15%
where the time goes in v10:
time: 128 us; the launch traced here: 127 us
  Pallas kernels  34.7 us (27%)
  blocking collectives  33.8 us (26%)
  starting transfers between devices  29.8 us (23%)
  waiting for transfers between devices  15.4 us (12%)
  between operations  13.5 us (11%)
    all_to_all x2, blocking collectives, exchanged(): return lax.all_to_all(value, axes, split_axis=0, concat_axis=0, tiled=True)  33.8 us
    pallas_call x1, Pallas kernels, project_of(): pl.pallas_call(project_kernel, out_shape=jax.ShapeDtypeStruct((tokens, bl...  14.4 us
    all_to_all x2, starting transfers between devices, exchanged(): return lax.all_to_all(value, axes, split_axis=0, concat_axis=0, tiled=True)  14.4 us
    all_to_all x2, waiting for transfers between devices, exchanged(): return lax.all_to_all(value, axes, split_axis=0, concat_axis=0, tiled=True)  11.1 us
    ppermute x7, starting transfers between devices, other_core(): return lax.ppermute(value, 'c', [(0, 1), (1, 0)])  8.8 us
    pallas_call x1, Pallas kernels, attention_of(): pl.pallas_call(functools.partial(attention_kernel, groups), out_shape=(ja...  6.23 us
    pallas_call x1, Pallas kernels, totals_of(): pl.pallas_call(totals_kernel, out_shape=[jax.ShapeDtypeStruct((4 * HALF /...  4.27 us
    ppermute x3, waiting for transfers between devices, from_all_groups(): lax.ppermute(value, 'z', [(i, (i + d) % size) for i in range(size)])  4.27 us
  transfers between devices with their start and end apart: 14, of which 4 were waited for; matrix products, arithmetic and copies ran while one was open for 0% of the time, Pallas kernels for 15%

profile of v10, /device:TPU:1, one launch (start us, length us, event | category | flops | bytes accessed | tf_op | source)
XLA Modules:
  0.0 127.1 jit_solution(3924256765545773994)
XLA Ops:
  6.5 0.0 all-gather.3.cloned.1.call-start
  6.5 3.6 %collective-permute-start.4 = (bf16[1024,128]{1,0:T(8,128)(2,1)}, bf16[1024,128]{1,0:T(8,128)(2,1)}, u32[]{:S(2)}, u32[]{:S(2)}) collective-permute-start(bf16[1024,128]{1,0:T(8,128)(2,1)} %param.9), channel_id=1, source_target_pairs={{0,0},{1,96},{2,64},{3,32},{32,65},{33,33},{34,1},{35,97},{64,2},{... | collective-permute-start | bytes 786440 | tf_op jit(solution)/shard_map/ppermute | solution.py:444
  10.1 4.3 %shard_map.55 = (f32[4,72,128]{2,1,0:T(8,128)}, f32[4,72,128]{2,1,0:T(8,128)}, f32[4,72,128]{2,1,0:T(8,128)}, f32[4,72,128]{2,1,0:T(8,128)}, f32[16,72,128]{2,1,0:T(8,128)}) custom-call(s32[1]{0:T(128)} %bitcast.side_ref, s32[8,1024]{1,0:T(8,128)} %bitcast.9, bf16[1024,1024]{1,0:T(8,128)(2,1)} %q_ref.1), custom_call_target="tpu_custom_call" | custom-call | tf_op jit(solution)/shard_map/pallas_call | solution.py:87
  14.4 1.5 %collective-permute-start = (f32[4,72,128]{2,1,0:T(8,128)}, f32[4,72,128]{2,1,0:T(8,128)S(1)}, u32[]{:S(2)}, u32[]{:S(2)}) collective-permute-start(f32[4,72,128]{2,1,0:T(8,128)} %get-tuple-element.19), channel_id=1, source_target_pairs={{0,4},{4,0},{1,5},{5,1},{2,6},{6,2},{3,7},{7,3},{8,12},{12,8},{9,1... | collective-permute-start | bytes 442376 | tf_op jit(solution)/shard_map/ppermute | solution.py:420
  15.9 0.1 collective-permute-start.1
  16.0 0.4 collective-permute-start.2
  16.4 0.1 collective-permute-start.3
  16.5 0.0 copy-start
  16.5 0.0 copy-start.1
  16.5 3.2 %shard_map.56 = (bf16[1024,512]{1,0:T(8,128)(2,1)}, bf16[1024,512]{1,0:T(8,128)(2,1)}, s32[1]{0:T(128)}) custom-call(s32[1]{0:T(128)} %bitcast.side_ref, f32[16,72,128]{2,1,0:T(8,128)} %get-tuple-element.18.after_ref.a_ref, bf16[1024,1024]{1,0:T(8,128)(2,1)} %rest_4_.1, bf16[1024,1024]{1,0:T(8,128)(2,1)} %rest_6_.1), custom_call_target="tpu_custom_call" | custom-call | tf_op jit(solution)/shard_map/pallas_call | solution.py:131
  19.7 0.0 collective-permute-done.rest_0_
  19.8 0.0 collective-permute-done.1.rest_1_
  19.8 0.0 collective-permute-done.2.rest_2_
  19.8 0.0 collective-permute-done.3.rest_3_
  19.8 0.0 collective-permute-done.4.rest_4_
  19.8 0.0 copy-done
  19.8 0.0 copy-done.1
  19.8 1.5 %shard_map.57 = (f32[16,72,128]{2,1,0:T(8,128)}, bf16[1024,128]{1,0:T(8,128)(2,1)}, s32[8,1024]{1,0:T(8,128)S(1)}) custom-call(f32[16,72,128]{2,1,0:T(8,128)S(1)} %copy-done, f32[4,72,128]{2,1,0:T(8,128)S(1)} %collective-permute-done.rest_0_, f32[4,72,128]{2,1,0:T(8,128)S(1)} %collective-permute-done.1.rest_1_, ...), custom_call_target="tpu_custom_call", output_to_operand_aliasing={{1}: (5, {})} | custom-call | tf_op jit(solution)/shard_map/pallas_call | solution.py:155
  21.3 0.0 all-gather.3.cloned.1.call-update
  21.4 0.5 collective-permute-start.8
  21.8 0.1 collective-permute-start.9
  21.9 9.2 %all-to-all-start = ((f32[16,72,128]{2,1,0:T(8,128)}), f32[16,72,128]{2,1,0:T(8,128)S(1)}, u32[]{:S(2)}, u32[]{:S(2)}) async-start(f32[16,72,128]{2,1,0:T(8,128)} %get-tuple-element.24), calls=%async_computation | async-start | bytes 1179648 | tf_op jit(solution)/shard_map/all_to_all | solution.py:424
  31.2 1.8 %collective-permute-start.7 = (s32[8,1024]{1,0:T(8,128)S(1)}, s32[8,1024]{1,0:T(8,128)S(1)}, u32[]{:S(2)}, u32[]{:S(2)}) collective-permute-start(s32[8,1024]{1,0:T(8,128)S(1)} %get-tuple-element.25.rest_0_), channel_id=1, source_target_pairs={{0,3},{1,0},{2,1},{3,2},{4,7},{5,4},{6,5},{7,6},{8,11},{9,8},{10,9... | collective-permute-start | bytes 98312 | tf_op jit(solution)/shard_map/ppermute | solution.py:431
  33.0 1.2 collective-permute-start.6
  34.2 0.0 collective-permute-start.5
  34.2 0.0 collective-permute-done.7.rest_2_.rest_3_
  34.2 3.1 %collective-permute-done.6.rest_1_.rest_2_ = s32[8,1024]{1,0:T(8,128)S(1)} collective-permute-done((s32[8,1024]{1,0:T(8,128)S(1)}, s32[8,1024]{1,0:T(8,128)S(1)}, u32[]{:S(2)}, u32[]{:S(2)}) %collective-permute-start.6) | collective-permute-done | bytes 32800 | tf_op jit(solution)/shard_map/ppermute | solution.py:431
  37.2 1.2 collective-permute-done.5.rest_0_.rest_1_
  38.4 3.7 %all-to-all-done.in_ref = f32[16,72,128]{2,1,0:T(8,128)S(1)} async-done(((f32[16,72,128]{2,1,0:T(8,128)}), f32[16,72,128]{2,1,0:T(8,128)S(1)}, u32[]{:S(2)}, u32[]{:S(2)}) %all-to-all-start) | async-done | bytes 589856 | tf_op jit(solution)/shard_map/all_to_all | solution.py:424
  42.1 0.8 shard_map.58
  43.0 5.2 %all-to-all-start.1 = ((bf16[16,64,128]{2,1,0:T(8,128)(2,1)}), bf16[16,64,128]{2,1,0:T(8,128)(2,1)S(1)}, u32[]{:S(2)}, u32[]{:S(2)}) async-start(bf16[16,64,128]{2,1,0:T(8,128)(2,1)} %shard_map.58), calls=%async_computation.1 | async-start | bytes 524288 | tf_op jit(solution)/shard_map/all_to_all | solution.py:424
  48.1 0.0 collective-permute-done.8.rest_5_
  48.2 0.0 collective-permute-done.9.rest_7_
  48.2 0.0 copy-start.2
  48.2 7.4 %all-to-all-done.1 = bf16[16,64,128]{2,1,0:T(8,128)(2,1)S(1)} async-done(((bf16[16,64,128]{2,1,0:T(8,128)(2,1)}), bf16[16,64,128]{2,1,0:T(8,128)(2,1)S(1)}, u32[]{:S(2)}, u32[]{:S(2)}) %all-to-all-start.1) | async-done | bytes 262176 | tf_op jit(solution)/shard_map/all_to_all | solution.py:424
  55.6 0.0 copy-done.2
  55.6 6.2 %shard_map.59 = (bf16[16,80,128]{2,1,0:T(8,128)(2,1)S(1)}, s32[4,8,1024]{2,1,0:T(8,128)S(1)}) custom-call(s32[1]{0:T(128)} %bitcast.side_ref, bf16[4,256,128]{2,1,0:T(8,128)(2,1)S(1)} %bitcast.8, s32[8,1024]{1,0:T(8,128)S(1)} %get-tuple-element.25.rest_0_, s32[8,1024]{1,0:T(8,128)S(1)} %collective-permute-done.5.rest_0_.rest_1_, ...), custom_call_target="tpu_custom_call" | custom-call | tf_op jit(solution)/shard_map/pallas_call | solution.py:263
  61.8 13.4 %all_to_all.20.in_ref = bf16[16,80,128]{2,1,0:T(8,128)(2,1)S(1)} all-to-all(bf16[16,80,128]{2,1,0:T(8,128)(2,1)S(1)} %get-tuple-element.29), channel_id=1, replica_groups=mesh['x'=4,'y'=4,'c'=2,'z'=4] {'x','y'}, dimensions={0} | all-to-all | bytes 655360 | tf_op jit(solution)/shard_map/all_to_all | solution.py:424
  75.2 0.4 shard_map.60
  75.6 20.4 %all_to_all.21 = bf16[64,64,128]{2,1,0:T(8,128)(2,1)S(1)} all-to-all(bf16[64,64,128]{2,1,0:T(8,128)(2,1)S(1)} %shard_map.60), channel_id=1, replica_groups=mesh['x'=4,'y'=4,'c'=2,'z'=4] {'z','x','y'}, dimensions={0} | all-to-all | bytes 2097152 | tf_op jit(solution)/shard_map/all_to_all | solution.py:424
  95.9 6.1 %collective-permute-start.10 = (bf16[16,256,128]{2,1,0:T(8,128)(2,1)S(1)}, bf16[16,256,128]{2,1,0:T(8,128)(2,1)S(1)}, u32[]{:S(2)}, u32[]{:S(2)}) collective-permute-start(bf16[16,256,128]{2,1,0:T(8,128)(2,1)S(1)} %bitcast.6), channel_id=1, source_target_pairs={{0,4},{4,0},{1,5},{5,1},{2,6},{6,2},{3,7},{7,3},{8,12},{12,8},{9,1... | collective-permute-start | bytes 3145736 | tf_op jit(solution)/shard_map/ppermute | solution.py:420
  102.0 0.0 all-gather.3.cloned.1.call-done
  102.0 3.8 %shard_map.61.near_ref = bf16[4,512,1024]{2,1,0:T(8,128)(2,1)} custom-call(s32[1]{0:T(128)} %bitcast.side_ref, s32[1]{0:T(128)} %bitcast.1.z_ref, s32[4,8,1024]{2,1,0:T(8,128)S(1)} %get-tuple-element.28.ids_ref, bf16[16,256,128]{2,1,0:T(8,128)(2,1)S(1)} %bitcast.7, bf16[4,8,1024,128]{3,2,1,0:T(8,128)(2,1)} %bitcast.11), custom_call_target="tpu_custom_call" | custom-call | tf_op jit(solution)/shard_map/pallas_call | solution.py:316
  105.8 0.0 collective-permute-done.10.table_ref
  105.8 14.4 %shard_map.62 = bf16[1024,1024]{1,0:T(8,128)(2,1)} custom-call(s32[1]{0:T(128)} %bitcast.side_ref, s32[1]{0:T(128)} %bitcast.1.z_ref, bf16[4,512,1024]{2,1,0:T(8,128)(2,1)} %shard_map.61.near_ref, s32[4,8,1024]{2,1,0:T(8,128)S(1)} %get-tuple-element.28.ids_ref, bf16[16,256,128]{2,1,0:T(8,128)(2,1)S(1)} %collective-permute-done.10.table_ref, ...), custom_call_target="tpu_custom_call" | custom-call | tf_op jit(solution)/shard_map/pallas_call | solution.py:402
Async XLA Ops:
  6.5 95.5 %all-gather.3.cloned.1.call-start = ((), (), s32[]{:S(2)}) async-start(), calls=%async_computation.4 | async-start | bytes 8650752 | tf_op jit(solution)/shard_map/all_gather | solution.py:451
  6.5 13.2 %collective-permute-start.4 = (bf16[1024,128]{1,0:T(8,128)(2,1)}, bf16[1024,128]{1,0:T(8,128)(2,1)}, u32[]{:S(2)}, u32[]{:S(2)}) collective-permute-start(bf16[1024,128]{1,0:T(8,128)(2,1)} %param.9), channel_id=1, source_target_pairs={{0,0},{1,96},{2,64},{3,32},{32,65},{33,33},{34,1},{35,97},{64,2},{... | collective-permute-start | bytes 786440 | tf_op jit(solution)/shard_map/ppermute | solution.py:444
  14.4 5.4 %collective-permute-start = (f32[4,72,128]{2,1,0:T(8,128)}, f32[4,72,128]{2,1,0:T(8,128)S(1)}, u32[]{:S(2)}, u32[]{:S(2)}) collective-permute-start(f32[4,72,128]{2,1,0:T(8,128)} %get-tuple-element.19), channel_id=1, source_target_pairs={{0,4},{4,0},{1,5},{5,1},{2,6},{6,2},{3,7},{7,3},{8,12},{12,8},{9,1... | collective-permute-start | bytes 442376 | tf_op jit(solution)/shard_map/ppermute | solution.py:420
  15.9 3.9 %collective-permute-start.1 = (f32[4,72,128]{2,1,0:T(8,128)}, f32[4,72,128]{2,1,0:T(8,128)S(1)}, u32[]{:S(2)}, u32[]{:S(2)}) collective-permute-start(f32[4,72,128]{2,1,0:T(8,128)} %get-tuple-element.20), channel_id=1, source_target_pairs={{0,4},{4,0},{1,5},{5,1},{2,6},{6,2},{3,7},{7,3},{8,12},{12,8},{9,1... | collective-permute-start | bytes 442376 | tf_op jit(solution)/shard_map/ppermute | solution.py:420
  16.0 3.8 %collective-permute-start.2 = (f32[4,72,128]{2,1,0:T(8,128)}, f32[4,72,128]{2,1,0:T(8,128)S(1)}, u32[]{:S(2)}, u32[]{:S(2)}) collective-permute-start(f32[4,72,128]{2,1,0:T(8,128)} %get-tuple-element.21), channel_id=1, source_target_pairs={{0,4},{4,0},{1,5},{5,1},{2,6},{6,2},{3,7},{7,3},{8,12},{12,8},{9,1... | collective-permute-start | bytes 442376 | tf_op jit(solution)/shard_map/ppermute | solution.py:420
  16.4 3.4 %collective-permute-start.3 = (f32[4,72,128]{2,1,0:T(8,128)}, f32[4,72,128]{2,1,0:T(8,128)S(1)}, u32[]{:S(2)}, u32[]{:S(2)}) collective-permute-start(f32[4,72,128]{2,1,0:T(8,128)} %get-tuple-element.22), channel_id=1, source_target_pairs={{0,4},{4,0},{1,5},{5,1},{2,6},{6,2},{3,7},{7,3},{8,12},{12,8},{9,1... | collective-permute-start | bytes 442376 | tf_op jit(solution)/shard_map/ppermute | solution.py:420
  16.5 3.3 %copy-start = (f32[16,72,128]{2,1,0:T(8,128)S(1)}, f32[16,72,128]{2,1,0:T(8,128)}, u32[]{:S(2)}) copy-start(f32[16,72,128]{2,1,0:T(8,128)} %get-tuple-element.18.after_ref.a_ref) | copy-start | bytes 1769476
  16.5 3.3 %copy-start.1 = (s32[1024,8]{0,1:T(8,128)S(1)}, s32[1024,8]{0,1:T(8,128)}, u32[]{:S(2)}) copy-start(s32[1024,8]{0,1:T(8,128)} %param.8) | copy-start | bytes 98308
  21.4 26.8 %collective-permute-start.8 = (bf16[1024,512]{1,0:T(8,128)(2,1)}, bf16[1024,512]{1,0:T(8,128)(2,1)S(1)}, u32[]{:S(2)}, u32[]{:S(2)}) collective-permute-start(bf16[1024,512]{1,0:T(8,128)(2,1)} %get-tuple-element.26), channel_id=1, source_target_pairs={{0,4},{4,0},{1,5},{5,1},{2,6},{6,2},{3,7},{7,3},{8,12},{12,8},{9,1... | collective-permute-start | bytes 3145736 | tf_op jit(solution)/shard_map/ppermute | solution.py:420
  21.8 26.3 %collective-permute-start.9 = (bf16[1024,512]{1,0:T(8,128)(2,1)}, bf16[1024,512]{1,0:T(8,128)(2,1)S(1)}, u32[]{:S(2)}, u32[]{:S(2)}) collective-permute-start(bf16[1024,512]{1,0:T(8,128)(2,1)} %get-tuple-element.27), channel_id=1, source_target_pairs={{0,4},{4,0},{1,5},{5,1},{2,6},{6,2},{3,7},{7,3},{8,12},{12,8},{9,1... | collective-permute-start | bytes 3145736 | tf_op jit(solution)/shard_map/ppermute | solution.py:420
  21.9 20.2 %all-to-all-start = ((f32[16,72,128]{2,1,0:T(8,128)}), f32[16,72,128]{2,1,0:T(8,128)S(1)}, u32[]{:S(2)}, u32[]{:S(2)}) async-start(f32[16,72,128]{2,1,0:T(8,128)} %get-tuple-element.24), calls=%async_computation | async-start | bytes 1179648 | tf_op jit(solution)/shard_map/all_to_all | solution.py:424
  31.2 3.0 %collective-permute-start.7 = (s32[8,1024]{1,0:T(8,128)S(1)}, s32[8,1024]{1,0:T(8,128)S(1)}, u32[]{:S(2)}, u32[]{:S(2)}) collective-permute-start(s32[8,1024]{1,0:T(8,128)S(1)} %get-tuple-element.25.rest_0_), channel_id=1, source_target_pairs={{0,3},{1,0},{2,1},{3,2},{4,7},{5,4},{6,5},{7,6},{8,11},{9,8},{10,9... | collective-permute-start | bytes 98312 | tf_op jit(solution)/shard_map/ppermute | solution.py:431
  33.0 4.3 %collective-permute-start.6 = (s32[8,1024]{1,0:T(8,128)S(1)}, s32[8,1024]{1,0:T(8,128)S(1)}, u32[]{:S(2)}, u32[]{:S(2)}) collective-permute-start(s32[8,1024]{1,0:T(8,128)S(1)} %get-tuple-element.25.rest_0_), channel_id=1, source_target_pairs={{0,2},{1,3},{2,0},{3,1},{4,6},{5,7},{6,4},{7,5},{8,10},{9,11},{10,... | collective-permute-start | bytes 98312 | tf_op jit(solution)/shard_map/ppermute | solution.py:431
  34.2 4.3 %collective-permute-start.5 = (s32[8,1024]{1,0:T(8,128)S(1)}, s32[8,1024]{1,0:T(8,128)S(1)}, u32[]{:S(2)}, u32[]{:S(2)}) collective-permute-start(s32[8,1024]{1,0:T(8,128)S(1)} %get-tuple-element.25.rest_0_), channel_id=1, source_target_pairs={{0,1},{1,2},{2,3},{3,0},{4,5},{5,6},{6,7},{7,4},{8,9},{9,10},{10,1... | collective-permute-start | bytes 98312 | tf_op jit(solution)/shard_map/ppermute | solution.py:431
  43.0 12.6 %all-to-all-start.1 = ((bf16[16,64,128]{2,1,0:T(8,128)(2,1)}), bf16[16,64,128]{2,1,0:T(8,128)(2,1)S(1)}, u32[]{:S(2)}, u32[]{:S(2)}) async-start(bf16[16,64,128]{2,1,0:T(8,128)(2,1)} %shard_map.58), calls=%async_computation.1 | async-start | bytes 524288 | tf_op jit(solution)/shard_map/all_to_all | solution.py:424
  48.2 7.4 %copy-start.2 = (bf16[1024,512]{1,0:T(8,128)(2,1)}, bf16[1024,512]{1,0:T(8,128)(2,1)S(1)}, u32[]{:S(2)}) copy-start(bf16[1024,512]{1,0:T(8,128)(2,1)S(1)} %collective-permute-done.9.rest_7_) | copy-start | bytes 3145732
  95.9 9.9 %collective-permute-start.10 = (bf16[16,256,128]{2,1,0:T(8,128)(2,1)S(1)}, bf16[16,256,128]{2,1,0:T(8,128)(2,1)S(1)}, u32[]{:S(2)}, u32[]{:S(2)}) collective-permute-start(bf16[16,256,128]{2,1,0:T(8,128)(2,1)S(1)} %bitcast.6), channel_id=1, source_target_pairs={{0,4},{4,0},{1,5},{5,1},{2,6},{6,2},{3,7},{7,3},{8,12},{12,8},{9,1... | collective-permute-start | bytes 3145736 | tf_op jit(solution)/shard_map/ppermute | solution.py:420
Sparse Core Ops, SparseCore 0:
  21.5 60.7 all-gather.2

commit v11 on v9

--- a/solution.py
+++ b/solution.py
@@ -189,18 +189,18 @@
 
 
 def attention_kernel(groups, side_ref, centre_ref, *rest):
-    ids_refs, sources = rest[:groups], rest[groups : groups + 4]
+    ids_refs, others_ref = rest[:groups], rest[groups + 1]
+    sources = (rest[groups], rest[groups + 2], rest[groups + 3])
     out_ref, ids_out_ref, held, arrived, copied = rest[groups + 4 :]
     first = side_ref[0] * HALF
 
     def fetch(k):
         source = sources[k]
-        if k % 2 == 0:
+        if k < 2:
             source = source.at[:, pl.ds(pl.multiple_of(first * HDIM, HALF * HDIM), HALF * HDIM)]
         return pltpu.make_async_copy(source, held.at[k], arrived.at[k])
 
-    for k in range(2):
-        fetch(k).start()
+    fetch(0).start()
     copies = [
         pltpu.make_async_copy(ids_refs[d], ids_out_ref.at[d], copied.at[d]) for d in range(groups)
     ]
@@ -211,26 +211,25 @@
     line = lax.broadcasted_iota(jnp.int32, (TAIL, HDIM), 0)
     for i in range(HALF):
         if i == 0:
-            for k in range(2):
-                fetch(k).wait()
-            for k in range(2, 4):
-                fetch(k).start()
+            fetch(0).wait()
+            fetch(1).start()
+            fetch(2).start()
         cols = slice(i * HDIM, (i + 1) * HDIM)
         centre = centre_ref[i]
         own = lax.dot_general(centre, held[0, :, cols], NT, preferred_element_type=F32)
-        other = lax.dot_general(centre, held[1, :, cols], NT, preferred_element_type=F32)
+        other = lax.dot_general(centre, others_ref[:, cols], NT, preferred_element_type=F32)
         peak = jnp.maximum(
             jnp.max(own, axis=1, keepdims=True), jnp.max(other, axis=1, keepdims=True)
         )
         own_w = jnp.exp2((own - peak) * LOG2_SCALE).astype(BF16)
         other_w = jnp.exp2((other - peak) * LOG2_SCALE).astype(BF16)
         if i == 0:
-            for k in range(2, 4):
-                fetch(k).wait()
+            fetch(1).wait()
+            fetch(2).wait()
         both = jnp.dot(
-            own_w, jnp.concatenate([held[2, :, cols], ones], axis=1), preferred_element_type=F32
+            own_w, jnp.concatenate([held[1, :, cols], ones], axis=1), preferred_element_type=F32
         ) + jnp.dot(
-            other_w, jnp.concatenate([held[3, :, cols], ones], axis=1), preferred_element_type=F32
+            other_w, jnp.concatenate([held[2, :, cols], ones], axis=1), preferred_element_type=F32
         )
         mass = both[:, HDIM:]
         part = (both[:, :HDIM] / mass).astype(BF16)
@@ -259,11 +258,11 @@
             jax.ShapeDtypeStruct((4 * HALF, QUARTER + TAIL, HDIM), BF16),
             jax.ShapeDtypeStruct((groups, *all_ids[0].shape), jnp.int32),
         ),
-        in_specs=[SCALARS, IN_VMEM] + [IN_HBM] * (groups + 4),
+        in_specs=[SCALARS, IN_VMEM] + [IN_HBM] * (groups + 1) + [IN_VMEM, IN_HBM, IN_HBM],
         out_specs=(IN_VMEM, IN_VMEM),
         scratch_shapes=[
-            pltpu.VMEM((4, rows, HALF * HDIM), BF16),
-            pltpu.SemaphoreType.DMA((4,)),
+            pltpu.VMEM((3, rows, HALF * HDIM), BF16),
+            pltpu.SemaphoreType.DMA((3,)),
             pltpu.SemaphoreType.DMA((groups,)),
         ],
         compiler_params=params(52),

time: 127 us -> 127 us (level)
  no operation moved by 1% of the time
where the time goes in v11:
time: 127 us; the launch traced here: 126 us
  blocking collectives  33.9 us (27%)
  Pallas kernels  33.8 us (27%)
  starting transfers between devices  29.8 us (23%)
  waiting for transfers between devices  15.4 us (12%)
  between operations  13.5 us (11%)
    all_to_all x2, blocking collectives, exchanged(): return lax.all_to_all(value, axes, split_axis=0, concat_axis=0, tiled=True)  33.9 us
    pallas_call x1, Pallas kernels, project_of(): pl.pallas_call(project_kernel, out_shape=jax.ShapeDtypeStruct((tokens, bl...  14.4 us
    all_to_all x2, starting transfers between devices, exchanged(): return lax.all_to_all(value, axes, split_axis=0, concat_axis=0, tiled=True)  14.4 us
    all_to_all x2, waiting for transfers between devices, exchanged(): return lax.all_to_all(value, axes, split_axis=0, concat_axis=0, tiled=True)  11.1 us
    ppermute x7, starting transfers between devices, other_core(): return lax.ppermute(value, 'c', [(0, 1), (1, 0)])  8.87 us
    pallas_call x1, Pallas kernels, attention_of(): pl.pallas_call(functools.partial(attention_kernel, groups), out_shape=(ja...  5.38 us
    pallas_call x1, Pallas kernels, totals_of(): pl.pallas_call(totals_kernel, out_shape=[jax.ShapeDtypeStruct((4 * HALF /...  4.27 us
    ppermute x3, waiting for transfers between devices, from_all_groups(): lax.ppermute(value, 'z', [(i, (i + d) % size) for i in range(size)])  4.27 us
  transfers between devices with their start and end apart: 14, of which 4 were waited for; matrix products, arithmetic and copies ran while one was open for 0% of the time, Pallas kernels for 14%

profile of v11, /device:TPU:1, one launch (start us, length us, event | category | flops | bytes accessed | tf_op | source)
XLA Modules:
  0.0 126.5 jit_solution(15897386706323439604)
XLA Ops:
  6.5 0.0 all-gather.3.cloned.1.call-start
  6.5 3.6 %collective-permute-start.4 = (bf16[1024,128]{1,0:T(8,128)(2,1)}, bf16[1024,128]{1,0:T(8,128)(2,1)}, u32[]{:S(2)}, u32[]{:S(2)}) collective-permute-start(bf16[1024,128]{1,0:T(8,128)(2,1)} %param.9), channel_id=1, source_target_pairs={{0,0},{1,96},{2,64},{3,32},{32,65},{33,33},{34,1},{35,97},{64,2},{... | collective-permute-start | bytes 786440 | tf_op jit(solution)/shard_map/ppermute | solution.py:436
  10.1 4.3 %shard_map.55 = (f32[4,72,128]{2,1,0:T(8,128)}, f32[4,72,128]{2,1,0:T(8,128)}, f32[4,72,128]{2,1,0:T(8,128)}, f32[4,72,128]{2,1,0:T(8,128)}, f32[16,72,128]{2,1,0:T(8,128)}) custom-call(s32[1]{0:T(128)} %bitcast.side_ref, s32[8,1024]{1,0:T(8,128)} %bitcast.9, bf16[1024,1024]{1,0:T(8,128)(2,1)} %q_ref.1), custom_call_target="tpu_custom_call" | custom-call | tf_op jit(solution)/shard_map/pallas_call | solution.py:87
  14.4 1.5 %collective-permute-start = (f32[4,72,128]{2,1,0:T(8,128)}, f32[4,72,128]{2,1,0:T(8,128)S(1)}, u32[]{:S(2)}, u32[]{:S(2)}) collective-permute-start(f32[4,72,128]{2,1,0:T(8,128)} %get-tuple-element.19), channel_id=1, source_target_pairs={{0,4},{4,0},{1,5},{5,1},{2,6},{6,2},{3,7},{7,3},{8,12},{12,8},{9,1... | collective-permute-start | bytes 442376 | tf_op jit(solution)/shard_map/ppermute | solution.py:412
  15.9 0.1 collective-permute-start.1
  16.0 0.4 collective-permute-start.2
  16.4 0.1 collective-permute-start.3
  16.5 0.0 copy-start
  16.5 0.0 copy-start.1
  16.5 3.2 %shard_map.56 = (bf16[1024,512]{1,0:T(8,128)(2,1)}, bf16[1024,512]{1,0:T(8,128)(2,1)}, s32[1]{0:T(128)}) custom-call(s32[1]{0:T(128)} %bitcast.side_ref, f32[16,72,128]{2,1,0:T(8,128)} %get-tuple-element.18.after_ref.a_ref, bf16[1024,1024]{1,0:T(8,128)(2,1)} %rest_4_.1, bf16[1024,1024]{1,0:T(8,128)(2,1)} %rest_6_.1), custom_call_target="tpu_custom_call" | custom-call | tf_op jit(solution)/shard_map/pallas_call | solution.py:131
  19.7 0.0 collective-permute-done.rest_0_
  19.8 0.0 collective-permute-done.1.rest_1_
  19.8 0.0 collective-permute-done.2.rest_2_
  19.8 0.0 collective-permute-done.3.rest_3_
  19.8 0.0 collective-permute-done.4.rest_4_
  19.8 0.0 copy-done
  19.8 0.0 copy-done.1
  19.8 1.5 %shard_map.57 = (f32[16,72,128]{2,1,0:T(8,128)}, bf16[1024,128]{1,0:T(8,128)(2,1)}, s32[8,1024]{1,0:T(8,128)S(1)}) custom-call(f32[16,72,128]{2,1,0:T(8,128)S(1)} %copy-done, f32[4,72,128]{2,1,0:T(8,128)S(1)} %collective-permute-done.rest_0_, f32[4,72,128]{2,1,0:T(8,128)S(1)} %collective-permute-done.1.rest_1_, ...), custom_call_target="tpu_custom_call", output_to_operand_aliasing={{1}: (5, {})} | custom-call | tf_op jit(solution)/shard_map/pallas_call | solution.py:155
  21.3 0.0 all-gather.3.cloned.1.call-update
  21.4 0.5 collective-permute-start.8
  21.8 0.1 collective-permute-start.9
  21.9 9.2 %all-to-all-start = ((f32[16,72,128]{2,1,0:T(8,128)}), f32[16,72,128]{2,1,0:T(8,128)S(1)}, u32[]{:S(2)}, u32[]{:S(2)}) async-start(f32[16,72,128]{2,1,0:T(8,128)} %get-tuple-element.24), calls=%async_computation | async-start | bytes 1179648 | tf_op jit(solution)/shard_map/all_to_all | solution.py:416
  31.2 1.8 %collective-permute-start.7 = (s32[8,1024]{1,0:T(8,128)S(1)}, s32[8,1024]{1,0:T(8,128)S(1)}, u32[]{:S(2)}, u32[]{:S(2)}) collective-permute-start(s32[8,1024]{1,0:T(8,128)S(1)} %get-tuple-element.25.rest_0_), channel_id=1, source_target_pairs={{0,3},{1,0},{2,1},{3,2},{4,7},{5,4},{6,5},{7,6},{8,11},{9,8},{10,9... | collective-permute-start | bytes 98312 | tf_op jit(solution)/shard_map/ppermute | solution.py:423
  33.0 1.2 collective-permute-start.6
  34.2 0.0 collective-permute-start.5
  34.2 0.0 collective-permute-done.7.rest_2_.rest_3_
  34.2 3.1 %collective-permute-done.6.rest_1_.rest_2_ = s32[8,1024]{1,0:T(8,128)S(1)} collective-permute-done((s32[8,1024]{1,0:T(8,128)S(1)}, s32[8,1024]{1,0:T(8,128)S(1)}, u32[]{:S(2)}, u32[]{:S(2)}) %collective-permute-start.6) | collective-permute-done | bytes 32800 | tf_op jit(solution)/shard_map/ppermute | solution.py:423
  37.2 1.2 collective-permute-done.5.rest_0_.rest_1_
  38.4 3.7 %all-to-all-done.in_ref = f32[16,72,128]{2,1,0:T(8,128)S(1)} async-done(((f32[16,72,128]{2,1,0:T(8,128)}), f32[16,72,128]{2,1,0:T(8,128)S(1)}, u32[]{:S(2)}, u32[]{:S(2)}) %all-to-all-start) | async-done | bytes 589856 | tf_op jit(solution)/shard_map/all_to_all | solution.py:416
  42.1 0.8 shard_map.58
  43.0 5.2 %all-to-all-start.1 = ((bf16[16,64,128]{2,1,0:T(8,128)(2,1)}), bf16[16,64,128]{2,1,0:T(8,128)(2,1)S(1)}, u32[]{:S(2)}, u32[]{:S(2)}) async-start(bf16[16,64,128]{2,1,0:T(8,128)(2,1)} %shard_map.58), calls=%async_computation.1 | async-start | bytes 524288 | tf_op jit(solution)/shard_map/all_to_all | solution.py:416
  48.1 0.0 collective-permute-done.8.rest_5_
  48.2 0.0 collective-permute-done.9.rest_7_
  48.2 0.0 copy-start.2
  48.2 7.4 %all-to-all-done.1 = bf16[16,64,128]{2,1,0:T(8,128)(2,1)S(1)} async-done(((bf16[16,64,128]{2,1,0:T(8,128)(2,1)}), bf16[16,64,128]{2,1,0:T(8,128)(2,1)S(1)}, u32[]{:S(2)}, u32[]{:S(2)}) %all-to-all-start.1) | async-done | bytes 262176 | tf_op jit(solution)/shard_map/all_to_all | solution.py:416
  55.6 0.0 copy-done.2
  55.6 5.4 %shard_map.59 = (bf16[16,80,128]{2,1,0:T(8,128)(2,1)S(1)}, s32[4,8,1024]{2,1,0:T(8,128)S(1)}) custom-call(s32[1]{0:T(128)} %bitcast.side_ref, bf16[4,256,128]{2,1,0:T(8,128)(2,1)S(1)} %bitcast.8, s32[8,1024]{1,0:T(8,128)S(1)} %get-tuple-element.25.rest_0_, s32[8,1024]{1,0:T(8,128)S(1)} %collective-permute-done.5.rest_0_.rest_1_, ...), custom_call_target="tpu_custom_call" | custom-call | tf_op jit(solution)/shard_map/pallas_call | solution.py:255
  61.0 13.5 %all_to_all.20.in_ref = bf16[16,80,128]{2,1,0:T(8,128)(2,1)S(1)} all-to-all(bf16[16,80,128]{2,1,0:T(8,128)(2,1)S(1)} %get-tuple-element.29), channel_id=1, replica_groups=mesh['x'=4,'y'=4,'c'=2,'z'=4] {'x','y'}, dimensions={0} | all-to-all | bytes 655360 | tf_op jit(solution)/shard_map/all_to_all | solution.py:416
  74.4 0.4 shard_map.60
  74.8 20.4 %all_to_all.21 = bf16[64,64,128]{2,1,0:T(8,128)(2,1)S(1)} all-to-all(bf16[64,64,128]{2,1,0:T(8,128)(2,1)S(1)} %shard_map.60), channel_id=1, replica_groups=mesh['x'=4,'y'=4,'c'=2,'z'=4] {'z','x','y'}, dimensions={0} | all-to-all | bytes 2097152 | tf_op jit(solution)/shard_map/all_to_all | solution.py:416
  95.2 6.2 %collective-permute-start.10 = (bf16[16,256,128]{2,1,0:T(8,128)(2,1)S(1)}, bf16[16,256,128]{2,1,0:T(8,128)(2,1)S(1)}, u32[]{:S(2)}, u32[]{:S(2)}) collective-permute-start(bf16[16,256,128]{2,1,0:T(8,128)(2,1)S(1)} %bitcast.6), channel_id=1, source_target_pairs={{0,4},{4,0},{1,5},{5,1},{2,6},{6,2},{3,7},{7,3},{8,12},{12,8},{9,1... | collective-permute-start | bytes 3145736 | tf_op jit(solution)/shard_map/ppermute | solution.py:412
  101.4 0.0 all-gather.3.cloned.1.call-done
  101.4 3.8 %shard_map.61.near_ref = bf16[4,512,1024]{2,1,0:T(8,128)(2,1)} custom-call(s32[1]{0:T(128)} %bitcast.side_ref, s32[1]{0:T(128)} %bitcast.1.z_ref, s32[4,8,1024]{2,1,0:T(8,128)S(1)} %get-tuple-element.28.ids_ref, bf16[16,256,128]{2,1,0:T(8,128)(2,1)S(1)} %bitcast.7, bf16[4,8,1024,128]{3,2,1,0:T(8,128)(2,1)} %bitcast.11), custom_call_target="tpu_custom_call" | custom-call | tf_op jit(solution)/shard_map/pallas_call | solution.py:308
  105.2 0.0 collective-permute-done.10.table_ref
  105.2 14.4 %shard_map.62 = bf16[1024,1024]{1,0:T(8,128)(2,1)} custom-call(s32[1]{0:T(128)} %bitcast.side_ref, s32[1]{0:T(128)} %bitcast.1.z_ref, bf16[4,512,1024]{2,1,0:T(8,128)(2,1)} %shard_map.61.near_ref, s32[4,8,1024]{2,1,0:T(8,128)S(1)} %get-tuple-element.28.ids_ref, bf16[16,256,128]{2,1,0:T(8,128)(2,1)S(1)} %collective-permute-done.10.table_ref, ...), custom_call_target="tpu_custom_call" | custom-call | tf_op jit(solution)/shard_map/pallas_call | solution.py:394
Async XLA Ops:
  6.5 94.9 %all-gather.3.cloned.1.call-start = ((), (), s32[]{:S(2)}) async-start(), calls=%async_computation.4 | async-start | bytes 8650752 | tf_op jit(solution)/shard_map/all_gather | solution.py:443
  6.5 13.2 %collective-permute-start.4 = (bf16[1024,128]{1,0:T(8,128)(2,1)}, bf16[1024,128]{1,0:T(8,128)(2,1)}, u32[]{:S(2)}, u32[]{:S(2)}) collective-permute-start(bf16[1024,128]{1,0:T(8,128)(2,1)} %param.9), channel_id=1, source_target_pairs={{0,0},{1,96},{2,64},{3,32},{32,65},{33,33},{34,1},{35,97},{64,2},{... | collective-permute-start | bytes 786440 | tf_op jit(solution)/shard_map/ppermute | solution.py:436
  14.4 5.4 %collective-permute-start = (f32[4,72,128]{2,1,0:T(8,128)}, f32[4,72,128]{2,1,0:T(8,128)S(1)}, u32[]{:S(2)}, u32[]{:S(2)}) collective-permute-start(f32[4,72,128]{2,1,0:T(8,128)} %get-tuple-element.19), channel_id=1, source_target_pairs={{0,4},{4,0},{1,5},{5,1},{2,6},{6,2},{3,7},{7,3},{8,12},{12,8},{9,1... | collective-permute-start | bytes 442376 | tf_op jit(solution)/shard_map/ppermute | solution.py:412
  15.9 3.9 %collective-permute-start.1 = (f32[4,72,128]{2,1,0:T(8,128)}, f32[4,72,128]{2,1,0:T(8,128)S(1)}, u32[]{:S(2)}, u32[]{:S(2)}) collective-permute-start(f32[4,72,128]{2,1,0:T(8,128)} %get-tuple-element.20), channel_id=1, source_target_pairs={{0,4},{4,0},{1,5},{5,1},{2,6},{6,2},{3,7},{7,3},{8,12},{12,8},{9,1... | collective-permute-start | bytes 442376 | tf_op jit(solution)/shard_map/ppermute | solution.py:412
  16.0 3.8 %collective-permute-start.2 = (f32[4,72,128]{2,1,0:T(8,128)}, f32[4,72,128]{2,1,0:T(8,128)S(1)}, u32[]{:S(2)}, u32[]{:S(2)}) collective-permute-start(f32[4,72,128]{2,1,0:T(8,128)} %get-tuple-element.21), channel_id=1, source_target_pairs={{0,4},{4,0},{1,5},{5,1},{2,6},{6,2},{3,7},{7,3},{8,12},{12,8},{9,1... | collective-permute-start | bytes 442376 | tf_op jit(solution)/shard_map/ppermute | solution.py:412
  16.4 3.4 %collective-permute-start.3 = (f32[4,72,128]{2,1,0:T(8,128)}, f32[4,72,128]{2,1,0:T(8,128)S(1)}, u32[]{:S(2)}, u32[]{:S(2)}) collective-permute-start(f32[4,72,128]{2,1,0:T(8,128)} %get-tuple-element.22), channel_id=1, source_target_pairs={{0,4},{4,0},{1,5},{5,1},{2,6},{6,2},{3,7},{7,3},{8,12},{12,8},{9,1... | collective-permute-start | bytes 442376 | tf_op jit(solution)/shard_map/ppermute | solution.py:412
  16.5 3.3 %copy-start = (f32[16,72,128]{2,1,0:T(8,128)S(1)}, f32[16,72,128]{2,1,0:T(8,128)}, u32[]{:S(2)}) copy-start(f32[16,72,128]{2,1,0:T(8,128)} %get-tuple-element.18.after_ref.a_ref) | copy-start | bytes 1769476
  16.5 3.3 %copy-start.1 = (s32[1024,8]{0,1:T(8,128)S(1)}, s32[1024,8]{0,1:T(8,128)}, u32[]{:S(2)}) copy-start(s32[1024,8]{0,1:T(8,128)} %param.8) | copy-start | bytes 98308
  21.4 26.8 %collective-permute-start.8 = (bf16[1024,512]{1,0:T(8,128)(2,1)}, bf16[1024,512]{1,0:T(8,128)(2,1)S(1)}, u32[]{:S(2)}, u32[]{:S(2)}) collective-permute-start(bf16[1024,512]{1,0:T(8,128)(2,1)} %get-tuple-element.26), channel_id=1, source_target_pairs={{0,4},{4,0},{1,5},{5,1},{2,6},{6,2},{3,7},{7,3},{8,12},{12,8},{9,1... | collective-permute-start | bytes 3145736 | tf_op jit(solution)/shard_map/ppermute | solution.py:412
  21.8 26.3 %collective-permute-start.9 = (bf16[1024,512]{1,0:T(8,128)(2,1)}, bf16[1024,512]{1,0:T(8,128)(2,1)S(1)}, u32[]{:S(2)}, u32[]{:S(2)}) collective-permute-start(bf16[1024,512]{1,0:T(8,128)(2,1)} %get-tuple-element.27), channel_id=1, source_target_pairs={{0,4},{4,0},{1,5},{5,1},{2,6},{6,2},{3,7},{7,3},{8,12},{12,8},{9,1... | collective-permute-start | bytes 3145736 | tf_op jit(solution)/shard_map/ppermute | solution.py:412
  21.9 20.2 %all-to-all-start = ((f32[16,72,128]{2,1,0:T(8,128)}), f32[16,72,128]{2,1,0:T(8,128)S(1)}, u32[]{:S(2)}, u32[]{:S(2)}) async-start(f32[16,72,128]{2,1,0:T(8,128)} %get-tuple-element.24), calls=%async_computation | async-start | bytes 1179648 | tf_op jit(solution)/shard_map/all_to_all | solution.py:416
  31.2 3.0 %collective-permute-start.7 = (s32[8,1024]{1,0:T(8,128)S(1)}, s32[8,1024]{1,0:T(8,128)S(1)}, u32[]{:S(2)}, u32[]{:S(2)}) collective-permute-start(s32[8,1024]{1,0:T(8,128)S(1)} %get-tuple-element.25.rest_0_), channel_id=1, source_target_pairs={{0,3},{1,0},{2,1},{3,2},{4,7},{5,4},{6,5},{7,6},{8,11},{9,8},{10,9... | collective-permute-start | bytes 98312 | tf_op jit(solution)/shard_map/ppermute | solution.py:423
  33.0 4.3 %collective-permute-start.6 = (s32[8,1024]{1,0:T(8,128)S(1)}, s32[8,1024]{1,0:T(8,128)S(1)}, u32[]{:S(2)}, u32[]{:S(2)}) collective-permute-start(s32[8,1024]{1,0:T(8,128)S(1)} %get-tuple-element.25.rest_0_), channel_id=1, source_target_pairs={{0,2},{1,3},{2,0},{3,1},{4,6},{5,7},{6,4},{7,5},{8,10},{9,11},{10,... | collective-permute-start | bytes 98312 | tf_op jit(solution)/shard_map/ppermute | solution.py:423
  34.2 4.3 %collective-permute-start.5 = (s32[8,1024]{1,0:T(8,128)S(1)}, s32[8,1024]{1,0:T(8,128)S(1)}, u32[]{:S(2)}, u32[]{:S(2)}) collective-permute-start(s32[8,1024]{1,0:T(8,128)S(1)} %get-tuple-element.25.rest_0_), channel_id=1, source_target_pairs={{0,1},{1,2},{2,3},{3,0},{4,5},{5,6},{6,7},{7,4},{8,9},{9,10},{10,1... | collective-permute-start | bytes 98312 | tf_op jit(solution)/shard_map/ppermute | solution.py:423
  43.0 12.6 %all-to-all-start.1 = ((bf16[16,64,128]{2,1,0:T(8,128)(2,1)}), bf16[16,64,128]{2,1,0:T(8,128)(2,1)S(1)}, u32[]{:S(2)}, u32[]{:S(2)}) async-start(bf16[16,64,128]{2,1,0:T(8,128)(2,1)} %shard_map.58), calls=%async_computation.1 | async-start | bytes 524288 | tf_op jit(solution)/shard_map/all_to_all | solution.py:416
  48.2 7.4 %copy-start.2 = (bf16[1024,512]{1,0:T(8,128)(2,1)}, bf16[1024,512]{1,0:T(8,128)(2,1)S(1)}, u32[]{:S(2)}) copy-start(bf16[1024,512]{1,0:T(8,128)(2,1)S(1)} %collective-permute-done.9.rest_7_) | copy-start | bytes 3145732
  95.2 9.9 %collective-permute-start.10 = (bf16[16,256,128]{2,1,0:T(8,128)(2,1)S(1)}, bf16[16,256,128]{2,1,0:T(8,128)(2,1)S(1)}, u32[]{:S(2)}, u32[]{:S(2)}) collective-permute-start(bf16[16,256,128]{2,1,0:T(8,128)(2,1)S(1)} %bitcast.6), channel_id=1, source_target_pairs={{0,4},{4,0},{1,5},{5,1},{2,6},{6,2},{3,7},{7,3},{8,12},{12,8},{9,1... | collective-permute-start | bytes 3145736 | tf_op jit(solution)/shard_map/ppermute | solution.py:412
Sparse Core Ops, SparseCore 0:
  21.5 60.7 all-gather.2

commit v12 on v11

--- a/solution.py
+++ b/solution.py
@@ -209,15 +209,22 @@
     ones = jnp.ones((held.shape[1], HDIM), BF16)
     diagonal = eye(QUARTER, HDIM)
     line = lax.broadcasted_iota(jnp.int32, (TAIL, HDIM), 0)
+
+    def scores(i):
+        cols = slice(i * HDIM, (i + 1) * HDIM)
+        return (
+            lax.dot_general(centre_ref[i], held[0, :, cols], NT, preferred_element_type=F32),
+            lax.dot_general(centre_ref[i], others_ref[:, cols], NT, preferred_element_type=F32),
+        )
+
+    fetch(0).wait()
+    fetch(1).start()
+    fetch(2).start()
+    coming = scores(0)
     for i in range(HALF):
-        if i == 0:
-            fetch(0).wait()
-            fetch(1).start()
-            fetch(2).start()
         cols = slice(i * HDIM, (i + 1) * HDIM)
-        centre = centre_ref[i]
-        own = lax.dot_general(centre, held[0, :, cols], NT, preferred_element_type=F32)
-        other = lax.dot_general(centre, others_ref[:, cols], NT, preferred_element_type=F32)
+        own, other = coming
+        coming = scores(i + 1) if i + 1 < HALF else None
         peak = jnp.maximum(
             jnp.max(own, axis=1, keepdims=True), jnp.max(other, axis=1, keepdims=True)
         )

time: 127 us -> 127 us (level)
  no operation moved by 1% of the time
where the time goes in v12:
time: 127 us; the launch traced here: 126 us
  blocking collectives  33.9 us (27%)
  Pallas kernels  33.3 us (26%)
  starting transfers between devices  29.8 us (23%)
  waiting for transfers between devices  15.4 us (12%)
  between operations  13.5 us (11%)
    all_to_all x2, blocking collectives, exchanged(): return lax.all_to_all(value, axes, split_axis=0, concat_axis=0, tiled=True)  33.9 us
    pallas_call x1, Pallas kernels, project_of(): pl.pallas_call(project_kernel, out_shape=jax.ShapeDtypeStruct((tokens, bl...  14.4 us
    all_to_all x2, starting transfers between devices, exchanged(): return lax.all_to_all(value, axes, split_axis=0, concat_axis=0, tiled=True)  14.4 us
    all_to_all x2, waiting for transfers between devices, exchanged(): return lax.all_to_all(value, axes, split_axis=0, concat_axis=0, tiled=True)  11.1 us
    ppermute x7, starting transfers between devices, other_core(): return lax.ppermute(value, 'c', [(0, 1), (1, 0)])  8.87 us
    pallas_call x1, Pallas kernels, attention_of(): pl.pallas_call(functools.partial(attention_kernel, groups), out_shape=(ja...  4.88 us
    pallas_call x1, Pallas kernels, totals_of(): pl.pallas_call(totals_kernel, out_shape=[jax.ShapeDtypeStruct((4 * HALF /...  4.27 us
    ppermute x3, waiting for transfers between devices, from_all_groups(): lax.ppermute(value, 'z', [(i, (i + d) % size) for i in range(size)])  4.27 us
  transfers between devices with their start and end apart: 14, of which 4 were waited for; matrix products, arithmetic and copies ran while one was open for 0% of the time, Pallas kernels for 14%

profile of v12, /device:TPU:1, one launch (start us, length us, event | category | flops | bytes accessed | tf_op | source)
XLA Modules:
  0.0 126.0 jit_solution(3070357758065009720)
XLA Ops:
  6.5 0.0 all-gather.3.cloned.1.call-start
  6.5 3.6 %collective-permute-start.4 = (bf16[1024,128]{1,0:T(8,128)(2,1)}, bf16[1024,128]{1,0:T(8,128)(2,1)}, u32[]{:S(2)}, u32[]{:S(2)}) collective-permute-start(bf16[1024,128]{1,0:T(8,128)(2,1)} %param.9), channel_id=1, source_target_pairs={{0,0},{1,96},{2,64},{3,32},{32,65},{33,33},{34,1},{35,97},{64,2},{... | collective-permute-start | bytes 786440 | tf_op jit(solution)/shard_map/ppermute | solution.py:443
  10.1 4.3 %shard_map.55 = (f32[4,72,128]{2,1,0:T(8,128)}, f32[4,72,128]{2,1,0:T(8,128)}, f32[4,72,128]{2,1,0:T(8,128)}, f32[4,72,128]{2,1,0:T(8,128)}, f32[16,72,128]{2,1,0:T(8,128)}) custom-call(s32[1]{0:T(128)} %bitcast.side_ref, s32[8,1024]{1,0:T(8,128)} %bitcast.9, bf16[1024,1024]{1,0:T(8,128)(2,1)} %q_ref.1), custom_call_target="tpu_custom_call" | custom-call | tf_op jit(solution)/shard_map/pallas_call | solution.py:87
  14.4 1.5 %collective-permute-start = (f32[4,72,128]{2,1,0:T(8,128)}, f32[4,72,128]{2,1,0:T(8,128)S(1)}, u32[]{:S(2)}, u32[]{:S(2)}) collective-permute-start(f32[4,72,128]{2,1,0:T(8,128)} %get-tuple-element.19), channel_id=1, source_target_pairs={{0,4},{4,0},{1,5},{5,1},{2,6},{6,2},{3,7},{7,3},{8,12},{12,8},{9,1... | collective-permute-start | bytes 442376 | tf_op jit(solution)/shard_map/ppermute | solution.py:419
  15.9 0.1 collective-permute-start.1
  16.0 0.4 collective-permute-start.2
  16.4 0.1 collective-permute-start.3
  16.5 0.0 copy-start
  16.5 0.0 copy-start.1
  16.5 3.2 %shard_map.56 = (bf16[1024,512]{1,0:T(8,128)(2,1)}, bf16[1024,512]{1,0:T(8,128)(2,1)}, s32[1]{0:T(128)}) custom-call(s32[1]{0:T(128)} %bitcast.side_ref, f32[16,72,128]{2,1,0:T(8,128)} %get-tuple-element.18.after_ref.a_ref, bf16[1024,1024]{1,0:T(8,128)(2,1)} %rest_4_.1, bf16[1024,1024]{1,0:T(8,128)(2,1)} %rest_6_.1), custom_call_target="tpu_custom_call" | custom-call | tf_op jit(solution)/shard_map/pallas_call | solution.py:131
  19.7 0.0 collective-permute-done.rest_0_
  19.8 0.0 collective-permute-done.1.rest_1_
  19.8 0.0 collective-permute-done.2.rest_2_
  19.8 0.0 collective-permute-done.3.rest_3_
  19.8 0.0 collective-permute-done.4.rest_4_
  19.8 0.0 copy-done
  19.8 0.0 copy-done.1
  19.8 1.5 %shard_map.57 = (f32[16,72,128]{2,1,0:T(8,128)}, bf16[1024,128]{1,0:T(8,128)(2,1)}, s32[8,1024]{1,0:T(8,128)S(1)}) custom-call(f32[16,72,128]{2,1,0:T(8,128)S(1)} %copy-done, f32[4,72,128]{2,1,0:T(8,128)S(1)} %collective-permute-done.rest_0_, f32[4,72,128]{2,1,0:T(8,128)S(1)} %collective-permute-done.1.rest_1_, ...), custom_call_target="tpu_custom_call", output_to_operand_aliasing={{1}: (5, {})} | custom-call | tf_op jit(solution)/shard_map/pallas_call | solution.py:155
  21.3 0.0 all-gather.3.cloned.1.call-update
  21.4 0.5 collective-permute-start.8
  21.8 0.1 collective-permute-start.9
  21.9 9.2 %all-to-all-start = ((f32[16,72,128]{2,1,0:T(8,128)}), f32[16,72,128]{2,1,0:T(8,128)S(1)}, u32[]{:S(2)}, u32[]{:S(2)}) async-start(f32[16,72,128]{2,1,0:T(8,128)} %get-tuple-element.24), calls=%async_computation | async-start | bytes 1179648 | tf_op jit(solution)/shard_map/all_to_all | solution.py:423
  31.2 1.8 %collective-permute-start.7 = (s32[8,1024]{1,0:T(8,128)S(1)}, s32[8,1024]{1,0:T(8,128)S(1)}, u32[]{:S(2)}, u32[]{:S(2)}) collective-permute-start(s32[8,1024]{1,0:T(8,128)S(1)} %get-tuple-element.25.rest_0_), channel_id=1, source_target_pairs={{0,3},{1,0},{2,1},{3,2},{4,7},{5,4},{6,5},{7,6},{8,11},{9,8},{10,9... | collective-permute-start | bytes 98312 | tf_op jit(solution)/shard_map/ppermute | solution.py:430
  33.0 1.2 collective-permute-start.6
  34.2 0.0 collective-permute-start.5
  34.2 0.0 collective-permute-done.7.rest_2_.rest_3_
  34.2 3.1 %collective-permute-done.6.rest_1_.rest_2_ = s32[8,1024]{1,0:T(8,128)S(1)} collective-permute-done((s32[8,1024]{1,0:T(8,128)S(1)}, s32[8,1024]{1,0:T(8,128)S(1)}, u32[]{:S(2)}, u32[]{:S(2)}) %collective-permute-start.6) | collective-permute-done | bytes 32800 | tf_op jit(solution)/shard_map/ppermute | solution.py:430
  37.2 1.2 collective-permute-done.5.rest_0_.rest_1_
  38.4 3.7 %all-to-all-done.in_ref = f32[16,72,128]{2,1,0:T(8,128)S(1)} async-done(((f32[16,72,128]{2,1,0:T(8,128)}), f32[16,72,128]{2,1,0:T(8,128)S(1)}, u32[]{:S(2)}, u32[]{:S(2)}) %all-to-all-start) | async-done | bytes 589856 | tf_op jit(solution)/shard_map/all_to_all | solution.py:423
  42.1 0.8 shard_map.58
  43.0 5.2 %all-to-all-start.1 = ((bf16[16,64,128]{2,1,0:T(8,128)(2,1)}), bf16[16,64,128]{2,1,0:T(8,128)(2,1)S(1)}, u32[]{:S(2)}, u32[]{:S(2)}) async-start(bf16[16,64,128]{2,1,0:T(8,128)(2,1)} %shard_map.58), calls=%async_computation.1 | async-start | bytes 524288 | tf_op jit(solution)/shard_map/all_to_all | solution.py:423
  48.1 0.0 collective-permute-done.8.rest_5_
  48.2 0.0 collective-permute-done.9.rest_7_
  48.2 0.0 copy-start.2
  48.2 7.4 %all-to-all-done.1 = bf16[16,64,128]{2,1,0:T(8,128)(2,1)S(1)} async-done(((bf16[16,64,128]{2,1,0:T(8,128)(2,1)}), bf16[16,64,128]{2,1,0:T(8,128)(2,1)S(1)}, u32[]{:S(2)}, u32[]{:S(2)}) %all-to-all-start.1) | async-done | bytes 262176 | tf_op jit(solution)/shard_map/all_to_all | solution.py:423
  55.6 0.0 copy-done.2
  55.6 4.9 %shard_map.59 = (bf16[16,80,128]{2,1,0:T(8,128)(2,1)S(1)}, s32[4,8,1024]{2,1,0:T(8,128)S(1)}) custom-call(s32[1]{0:T(128)} %bitcast.side_ref, bf16[4,256,128]{2,1,0:T(8,128)(2,1)S(1)} %bitcast.8, s32[8,1024]{1,0:T(8,128)S(1)} %get-tuple-element.25.rest_0_, s32[8,1024]{1,0:T(8,128)S(1)} %collective-permute-done.5.rest_0_.rest_1_, ...), custom_call_target="tpu_custom_call" | custom-call | tf_op jit(solution)/shard_map/pallas_call | solution.py:262
  60.5 13.4 %all_to_all.20.in_ref = bf16[16,80,128]{2,1,0:T(8,128)(2,1)S(1)} all-to-all(bf16[16,80,128]{2,1,0:T(8,128)(2,1)S(1)} %get-tuple-element.29), channel_id=1, replica_groups=mesh['x'=4,'y'=4,'c'=2,'z'=4] {'x','y'}, dimensions={0} | all-to-all | bytes 655360 | tf_op jit(solution)/shard_map/all_to_all | solution.py:423
  73.9 0.4 shard_map.60
  74.3 20.4 %all_to_all.21 = bf16[64,64,128]{2,1,0:T(8,128)(2,1)S(1)} all-to-all(bf16[64,64,128]{2,1,0:T(8,128)(2,1)S(1)} %shard_map.60), channel_id=1, replica_groups=mesh['x'=4,'y'=4,'c'=2,'z'=4] {'z','x','y'}, dimensions={0} | all-to-all | bytes 2097152 | tf_op jit(solution)/shard_map/all_to_all | solution.py:423
  94.7 6.2 %collective-permute-start.10 = (bf16[16,256,128]{2,1,0:T(8,128)(2,1)S(1)}, bf16[16,256,128]{2,1,0:T(8,128)(2,1)S(1)}, u32[]{:S(2)}, u32[]{:S(2)}) collective-permute-start(bf16[16,256,128]{2,1,0:T(8,128)(2,1)S(1)} %bitcast.6), channel_id=1, source_target_pairs={{0,4},{4,0},{1,5},{5,1},{2,6},{6,2},{3,7},{7,3},{8,12},{12,8},{9,1... | collective-permute-start | bytes 3145736 | tf_op jit(solution)/shard_map/ppermute | solution.py:419
  100.9 0.0 all-gather.3.cloned.1.call-done
  100.9 3.8 %shard_map.61.near_ref = bf16[4,512,1024]{2,1,0:T(8,128)(2,1)} custom-call(s32[1]{0:T(128)} %bitcast.side_ref, s32[1]{0:T(128)} %bitcast.1.z_ref, s32[4,8,1024]{2,1,0:T(8,128)S(1)} %get-tuple-element.28.ids_ref, bf16[16,256,128]{2,1,0:T(8,128)(2,1)S(1)} %bitcast.7, bf16[4,8,1024,128]{3,2,1,0:T(8,128)(2,1)} %bitcast.11), custom_call_target="tpu_custom_call" | custom-call | tf_op jit(solution)/shard_map/pallas_call | solution.py:315
  104.7 0.0 collective-permute-done.10.table_ref
  104.7 14.4 %shard_map.62 = bf16[1024,1024]{1,0:T(8,128)(2,1)} custom-call(s32[1]{0:T(128)} %bitcast.side_ref, s32[1]{0:T(128)} %bitcast.1.z_ref, bf16[4,512,1024]{2,1,0:T(8,128)(2,1)} %shard_map.61.near_ref, s32[4,8,1024]{2,1,0:T(8,128)S(1)} %get-tuple-element.28.ids_ref, bf16[16,256,128]{2,1,0:T(8,128)(2,1)S(1)} %collective-permute-done.10.table_ref, ...), custom_call_target="tpu_custom_call" | custom-call | tf_op jit(solution)/shard_map/pallas_call | solution.py:401
Async XLA Ops:
  6.5 94.4 %all-gather.3.cloned.1.call-start = ((), (), s32[]{:S(2)}) async-start(), calls=%async_computation.4 | async-start | bytes 8650752 | tf_op jit(solution)/shard_map/all_gather | solution.py:450
  6.5 13.2 %collective-permute-start.4 = (bf16[1024,128]{1,0:T(8,128)(2,1)}, bf16[1024,128]{1,0:T(8,128)(2,1)}, u32[]{:S(2)}, u32[]{:S(2)}) collective-permute-start(bf16[1024,128]{1,0:T(8,128)(2,1)} %param.9), channel_id=1, source_target_pairs={{0,0},{1,96},{2,64},{3,32},{32,65},{33,33},{34,1},{35,97},{64,2},{... | collective-permute-start | bytes 786440 | tf_op jit(solution)/shard_map/ppermute | solution.py:443
  14.4 5.4 %collective-permute-start = (f32[4,72,128]{2,1,0:T(8,128)}, f32[4,72,128]{2,1,0:T(8,128)S(1)}, u32[]{:S(2)}, u32[]{:S(2)}) collective-permute-start(f32[4,72,128]{2,1,0:T(8,128)} %get-tuple-element.19), channel_id=1, source_target_pairs={{0,4},{4,0},{1,5},{5,1},{2,6},{6,2},{3,7},{7,3},{8,12},{12,8},{9,1... | collective-permute-start | bytes 442376 | tf_op jit(solution)/shard_map/ppermute | solution.py:419
  15.9 3.9 %collective-permute-start.1 = (f32[4,72,128]{2,1,0:T(8,128)}, f32[4,72,128]{2,1,0:T(8,128)S(1)}, u32[]{:S(2)}, u32[]{:S(2)}) collective-permute-start(f32[4,72,128]{2,1,0:T(8,128)} %get-tuple-element.20), channel_id=1, source_target_pairs={{0,4},{4,0},{1,5},{5,1},{2,6},{6,2},{3,7},{7,3},{8,12},{12,8},{9,1... | collective-permute-start | bytes 442376 | tf_op jit(solution)/shard_map/ppermute | solution.py:419
  16.0 3.8 %collective-permute-start.2 = (f32[4,72,128]{2,1,0:T(8,128)}, f32[4,72,128]{2,1,0:T(8,128)S(1)}, u32[]{:S(2)}, u32[]{:S(2)}) collective-permute-start(f32[4,72,128]{2,1,0:T(8,128)} %get-tuple-element.21), channel_id=1, source_target_pairs={{0,4},{4,0},{1,5},{5,1},{2,6},{6,2},{3,7},{7,3},{8,12},{12,8},{9,1... | collective-permute-start | bytes 442376 | tf_op jit(solution)/shard_map/ppermute | solution.py:419
  16.4 3.4 %collective-permute-start.3 = (f32[4,72,128]{2,1,0:T(8,128)}, f32[4,72,128]{2,1,0:T(8,128)S(1)}, u32[]{:S(2)}, u32[]{:S(2)}) collective-permute-start(f32[4,72,128]{2,1,0:T(8,128)} %get-tuple-element.22), channel_id=1, source_target_pairs={{0,4},{4,0},{1,5},{5,1},{2,6},{6,2},{3,7},{7,3},{8,12},{12,8},{9,1... | collective-permute-start | bytes 442376 | tf_op jit(solution)/shard_map/ppermute | solution.py:419
  16.5 3.3 %copy-start = (f32[16,72,128]{2,1,0:T(8,128)S(1)}, f32[16,72,128]{2,1,0:T(8,128)}, u32[]{:S(2)}) copy-start(f32[16,72,128]{2,1,0:T(8,128)} %get-tuple-element.18.after_ref.a_ref) | copy-start | bytes 1769476
  16.5 3.3 %copy-start.1 = (s32[1024,8]{0,1:T(8,128)S(1)}, s32[1024,8]{0,1:T(8,128)}, u32[]{:S(2)}) copy-start(s32[1024,8]{0,1:T(8,128)} %param.8) | copy-start | bytes 98308
  21.4 26.8 %collective-permute-start.8 = (bf16[1024,512]{1,0:T(8,128)(2,1)}, bf16[1024,512]{1,0:T(8,128)(2,1)S(1)}, u32[]{:S(2)}, u32[]{:S(2)}) collective-permute-start(bf16[1024,512]{1,0:T(8,128)(2,1)} %get-tuple-element.26), channel_id=1, source_target_pairs={{0,4},{4,0},{1,5},{5,1},{2,6},{6,2},{3,7},{7,3},{8,12},{12,8},{9,1... | collective-permute-start | bytes 3145736 | tf_op jit(solution)/shard_map/ppermute | solution.py:419
  21.8 26.3 %collective-permute-start.9 = (bf16[1024,512]{1,0:T(8,128)(2,1)}, bf16[1024,512]{1,0:T(8,128)(2,1)S(1)}, u32[]{:S(2)}, u32[]{:S(2)}) collective-permute-start(bf16[1024,512]{1,0:T(8,128)(2,1)} %get-tuple-element.27), channel_id=1, source_target_pairs={{0,4},{4,0},{1,5},{5,1},{2,6},{6,2},{3,7},{7,3},{8,12},{12,8},{9,1... | collective-permute-start | bytes 3145736 | tf_op jit(solution)/shard_map/ppermute | solution.py:419
  21.9 20.2 %all-to-all-start = ((f32[16,72,128]{2,1,0:T(8,128)}), f32[16,72,128]{2,1,0:T(8,128)S(1)}, u32[]{:S(2)}, u32[]{:S(2)}) async-start(f32[16,72,128]{2,1,0:T(8,128)} %get-tuple-element.24), calls=%async_computation | async-start | bytes 1179648 | tf_op jit(solution)/shard_map/all_to_all | solution.py:423
  31.2 3.0 %collective-permute-start.7 = (s32[8,1024]{1,0:T(8,128)S(1)}, s32[8,1024]{1,0:T(8,128)S(1)}, u32[]{:S(2)}, u32[]{:S(2)}) collective-permute-start(s32[8,1024]{1,0:T(8,128)S(1)} %get-tuple-element.25.rest_0_), channel_id=1, source_target_pairs={{0,3},{1,0},{2,1},{3,2},{4,7},{5,4},{6,5},{7,6},{8,11},{9,8},{10,9... | collective-permute-start | bytes 98312 | tf_op jit(solution)/shard_map/ppermute | solution.py:430
  33.0 4.3 %collective-permute-start.6 = (s32[8,1024]{1,0:T(8,128)S(1)}, s32[8,1024]{1,0:T(8,128)S(1)}, u32[]{:S(2)}, u32[]{:S(2)}) collective-permute-start(s32[8,1024]{1,0:T(8,128)S(1)} %get-tuple-element.25.rest_0_), channel_id=1, source_target_pairs={{0,2},{1,3},{2,0},{3,1},{4,6},{5,7},{6,4},{7,5},{8,10},{9,11},{10,... | collective-permute-start | bytes 98312 | tf_op jit(solution)/shard_map/ppermute | solution.py:430
  34.2 4.3 %collective-permute-start.5 = (s32[8,1024]{1,0:T(8,128)S(1)}, s32[8,1024]{1,0:T(8,128)S(1)}, u32[]{:S(2)}, u32[]{:S(2)}) collective-permute-start(s32[8,1024]{1,0:T(8,128)S(1)} %get-tuple-element.25.rest_0_), channel_id=1, source_target_pairs={{0,1},{1,2},{2,3},{3,0},{4,5},{5,6},{6,7},{7,4},{8,9},{9,10},{10,1... | collective-permute-start | bytes 98312 | tf_op jit(solution)/shard_map/ppermute | solution.py:430
  43.0 12.6 %all-to-all-start.1 = ((bf16[16,64,128]{2,1,0:T(8,128)(2,1)}), bf16[16,64,128]{2,1,0:T(8,128)(2,1)S(1)}, u32[]{:S(2)}, u32[]{:S(2)}) async-start(bf16[16,64,128]{2,1,0:T(8,128)(2,1)} %shard_map.58), calls=%async_computation.1 | async-start | bytes 524288 | tf_op jit(solution)/shard_map/all_to_all | solution.py:423
  48.2 7.4 %copy-start.2 = (bf16[1024,512]{1,0:T(8,128)(2,1)}, bf16[1024,512]{1,0:T(8,128)(2,1)S(1)}, u32[]{:S(2)}) copy-start(bf16[1024,512]{1,0:T(8,128)(2,1)S(1)} %collective-permute-done.9.rest_7_) | copy-start | bytes 3145732
  94.7 9.9 %collective-permute-start.10 = (bf16[16,256,128]{2,1,0:T(8,128)(2,1)S(1)}, bf16[16,256,128]{2,1,0:T(8,128)(2,1)S(1)}, u32[]{:S(2)}, u32[]{:S(2)}) collective-permute-start(bf16[16,256,128]{2,1,0:T(8,128)(2,1)S(1)} %bitcast.6), channel_id=1, source_target_pairs={{0,4},{4,0},{1,5},{5,1},{2,6},{6,2},{3,7},{7,3},{8,12},{12,8},{9,1... | collective-permute-start | bytes 3145736 | tf_op jit(solution)/shard_map/ppermute | solution.py:419
Sparse Core Ops, SparseCore 0:
  21.5 60.7 all-gather.2
